TPU v7x, 32 devices: a whole 2x2x4 slice. The times are simulated.
32 devices in a mesh: energy: 8 (over y, x, core), pair: 4 (over z).
Axes of the slice: x: 2, y: 2, z: 4, core: 2. Of those that a mesh axis runs over, the one named last changes fastest.
Arguments:
- green_less: bfloat16 [2, 8, 1024, 256], P(None, 'energy', 'pair'), may hold values from -6 to 6
- green_greater: bfloat16 [2, 8, 1024, 256], P(None, 'energy', 'pair'), may hold values from -6 to 6
- pair_blocks: int32 [4, 2], P('pair'), may hold values from 0 to 2, as said below
- onsite_scale: float32 [3], replicated, may hold values from 0.5 to 2
- coupling_scale: float32 [2], replicated, may hold values from 0.5 to 2
- coupling_mask: int32 [3, 3], replicated, may hold values 0 or 1
- onsite_block: bfloat16 [256, 256], replicated, may hold values from -0.375 to 0.375
- coupling_block: bfloat16 [256, 256], replicated, may hold values from -0.375 to 0.375
Outputs:
- screened: bfloat16 [2, 8, 1024, 256], P(None, 'energy', 'pair')
Inputs may be any that keep to these rules, and one draw needn't show every extreme that they name: `pair_blocks`: for each s below 2, slot s holds (i, i + 1) or (i + 1, i) for some i, and slot s + 2 holds the same two blocks in reverse order; every i from 0 to 1 occurs in exactly one slot below 2.
All inputs are finite; a program needn't handle non-finite values.
Results may differ from a plain program's by a relative error of at most 0.012.
Values may be sent and summed in bfloat16 or wider, within the bound.
No kernel may reach another device: no remote copies, remote signals or barrier semaphores. Data moves between devices by JAX's collectives and lax.ppermute only.
A program may use at most 64 MiB of HBM per device.

v0:
```python
import math

import jax
import jax.numpy as jnp
from jax import lax
from jax.sharding import PartitionSpec as P

PRECISE = lax.Precision.HIGHEST


def from_behind(value, axis, steps):
    count = lax.axis_size(axis)
    pairs = [(source, (source + steps) % count) for source in range(count)]
    return lax.ppermute(value, axis, pairs)


def fourier_tables(energies):
    length = 2 * energies
    frequency = jnp.arange(length, dtype=jnp.int32)
    energy_index = jnp.arange(energies, dtype=jnp.int32)
    phases = (frequency[:, None] * energy_index[None, :] % length).astype(jnp.float32) * (
        2.0 * math.pi / length
    )
    cosine = jnp.cos(phases)
    sine_table = jnp.sin(phases)
    forward = jnp.concatenate([cosine, sine_table], axis=0)
    top_rows = jnp.concatenate([cosine.T, -sine_table.T], axis=1)
    bottom_rows = jnp.concatenate([sine_table.T, cosine.T], axis=1)
    inverse = jnp.concatenate([top_rows, bottom_rows], axis=0) / length
    return (forward, inverse)


def transform(forward, real_part, imag_part, sign_flip):
    length = forward.shape[0] // 2
    real_spec = jnp.dot(forward, real_part, precision=PRECISE, preferred_element_type=jnp.float32)
    imag_spec = jnp.dot(forward, imag_part, precision=PRECISE, preferred_element_type=jnp.float32)
    out_real = real_spec[:length] + sign_flip * imag_spec[length:]
    out_imag = imag_spec[:length] - sign_flip * real_spec[length:]
    return (out_real, out_imag)


def spectrum(forward, element_block, sign_flip):
    flat = element_block.reshape(2, element_block.shape[1], -1).astype(jnp.float32)
    return transform(forward, flat[0], flat[1], sign_flip)


def multiply_spectra(less_spec, more_spec, inverse, energies):
    prod_real = less_spec[0] * more_spec[0] - less_spec[1] * more_spec[1]
    prod_imag = less_spec[0] * more_spec[1] + less_spec[1] * more_spec[0]
    lagged = jnp.dot(
        inverse,
        jnp.concatenate([prod_real, prod_imag], axis=0),
        precision=PRECISE,
        preferred_element_type=jnp.float32,
    )
    factor = energies ** (-0.5)
    return jnp.stack([factor * lagged[energies:], -factor * lagged[:energies]]).astype(jnp.bfloat16)


def lookup(source_table, wanted):
    positions = jnp.arange(source_table.shape[0], dtype=jnp.int32)
    return jnp.sum(jnp.where(positions == wanted, source_table, jnp.zeros_like(source_table)))


def sandwich(left_block, middle, right_block):
    inner_block = jnp.einsum(
        "ij,cejk->ceik", left_block, middle, preferred_element_type=jnp.float32
    ).astype(jnp.bfloat16)
    return jnp.einsum("ceij,jk->ceik", inner_block, right_block, preferred_element_type=jnp.float32)


def on_device(
    green_less,
    green_greater,
    pair_blocks,
    onsite_scale,
    coupling_scale,
    coupling_mask,
    onsite_block,
    coupling_block,
):
    pair_span = lax.axis_size("pair")
    energies = green_less.shape[1] * lax.axis_size("energy")
    block_width = green_less.shape[3]
    block_count = coupling_mask.shape[0]
    forward, inverse = fourier_tables(energies)
    mirrored = from_behind(green_greater, "pair", pair_span // 2)
    turned = jnp.swapaxes(mirrored, 2, 3)
    less_elem, greater_elem = (
        lax.all_to_all(green_less, "energy", split_axis=2, concat_axis=1, tiled=True),
        lax.all_to_all(turned, "energy", split_axis=2, concat_axis=1, tiled=True),
    )
    less_spec = spectrum(forward, less_elem, 1.0)
    more_spec = spectrum(forward, greater_elem, -1.0)
    polar_elem = multiply_spectra(less_spec, more_spec, inverse, energies)
    polar_rows = polar_elem.reshape(2, energies, -1, block_width)
    polar_local = lax.all_to_all(polar_rows, "energy", split_axis=1, concat_axis=2, tiled=True)
    row_block = pair_blocks[0, 0]
    col_block = pair_blocks[0, 1]
    lower_block = jnp.minimum(row_block, col_block)
    onsite_factor = lookup(onsite_scale, row_block) * lookup(onsite_scale, col_block)
    coupling_value = lookup(coupling_scale, lower_block)
    flat_mask = coupling_mask.reshape(-1).astype(jnp.float32)
    mask_value = lookup(flat_mask, lower_block * block_count + lower_block + 1)
    mirror_weight = mask_value * coupling_value * coupling_value
    own_term = onsite_factor * sandwich(onsite_block, polar_local, onsite_block)
    coupling = jnp.where(row_block < col_block, coupling_block, coupling_block.T)
    polar_other = from_behind(polar_local, "pair", pair_span // 2)
    other_term = (mirror_weight * sandwich(coupling, polar_other, coupling)).astype(jnp.bfloat16)
    return (own_term + other_term.astype(jnp.float32)).astype(jnp.bfloat16)


def solution(mesh):
    return jax.shard_map(
        on_device,
        mesh=mesh,
        in_specs=(
            P(None, "energy", "pair", None),
            P(None, "energy", "pair", None),
            P("pair", None),
            P(),
            P(),
            P(),
            P(),
            P(),
        ),
        out_specs=P(None, "energy", "pair", None),
        check_vma=False,
    )
```

profile of v0, /device:TPU:0, one launch (start us, length us, event | category | flops | bytes accessed | tf_op | source)
XLA Modules:
  0.0 59.8 jit_solution(3901138389117173066)
XLA Ops:
  0.0 1.2 %copy.50 = bf16[2,1,256,256]{2,0,1,3:T(2,128)(2,1)S(1)} copy(bf16[2,1,256,256]{3,2,1,0:T(8,128)(2,1)} %param.9) | data formatting | bytes 524288 | tf_op args[1]
  1.2 4.1 %collective-permute-start = (bf16[2,1,256,256]{2,0,1,3:T(2,128)(2,1)S(1)}, bf16[2,1,256,256]{2,0,1,3:T(2,128)(2,1)}, u32[]{:S(2)}, u32[]{:S(2)}) collective-permute-start(bf16[2,1,256,256]{2,0,1,3:T(2,128)(2,1)S(1)} %copy.50), channel_id=1, source_target_pairs={{0,2},{1,3},{2,0},{3,1},{4,6},{5,7},{6,4},{7,5},{8,10},{9,11},{10,... | collective-permute-start | bytes 786440 | tf_op jit(solution)/shard_map/ppermute | solution.py:14
  5.3 1.0 %copy.49 = bf16[2,1,256,256]{3,0,1,2:T(2,128)(2,1)} copy(bf16[2,1,256,256]{3,2,1,0:T(8,128)(2,1)S(1)} %copy-done.2) | data formatting | bytes 524288 | tf_op args[0]
  6.3 3.7 %all-to-all-start = ((bf16[2,1,256,256]{3,0,1,2:T(2,128)(2,1)}), bf16[2,1,256,256]{3,0,1,2:T(2,128)(2,1)S(1)}, u32[]{:S(2)}, u32[]{:S(2)}) async-start(bf16[2,1,256,256]{3,0,1,2:T(2,128)(2,1)} %copy.49), calls=%async_computation | async-start | bytes 524288 | tf_op jit(solution)/shard_map/all_to_all | solution.py:90
  10.2 6.7 %all-to-all-done = bf16[2,1,256,256]{3,0,1,2:T(2,128)(2,1)S(1)} async-done(((bf16[2,1,256,256]{3,0,1,2:T(2,128)(2,1)}), bf16[2,1,256,256]{3,0,1,2:T(2,128)(2,1)S(1)}, u32[]{:S(2)}, u32[]{:S(2)}) %all-to-all-start) | async-done | bytes 262176 | tf_op jit(solution)/shard_map/all_to_all | solution.py:90
  16.9 1.1 %slice_reduce_fusion.3 = (bf16[256,256]{1,0:T(8,128)(2,1)S(1)}, bf16[256,256]{1,0:T(8,128)(2,1)S(1)}) fusion(bf16[2,1,256,256]{3,0,1,2:T(2,128)(2,1)S(1)} %all-to-all-done), kind=kLoop, calls=%fused_computation.30 | loop fusion | bytes 524288 | tf_op jit(solution)/shard_map/slice | solution.py:44
  18.2 0.6 %fusion.53 = f32[32,8192]{1,0:T(8,128)S(1)} fusion(f32[32,8]{0,1:T(8,128)S(1)} %pad_maximum_fusion.1, bf16[8,8192]{1,0:T(8,128)(2,1)S(1)} %squeeze.20), kind=kOutput, calls=%fused_computation.80 | convolution fusion | flops 25165824 | bytes 1180672 | tf_op jit(solution)/shard_map/dot_general | solution.py:35
  18.8 3.4 %all-to-all-start.1 = ((bf16[2,1,256,256]{3,0,1,2:T(2,128)(2,1)}), bf16[2,1,256,256]{3,0,1,2:T(2,128)(2,1)S(1)}, u32[]{:S(2)}, u32[]{:S(2)}) async-start(bf16[2,1,256,256]{3,0,1,2:T(2,128)(2,1)} %bitcast.2), calls=%async_computation.1 | async-start | bytes 524288 | tf_op jit(solution)/shard_map/all_to_all | solution.py:91
  22.2 0.6 %fusion.54 = f32[32,8192]{1,0:T(8,128)S(1)} fusion(f32[32,8]{0,1:T(8,128)S(1)} %pad_maximum_fusion.1, bf16[8,8192]{1,0:T(8,128)(2,1)S(1)} %squeeze.21), kind=kOutput, calls=%fused_computation.81 | convolution fusion | flops 25165824 | bytes 1180672 | tf_op jit(solution)/shard_map/dot_general | solution.py:36
  22.9 6.3 %all-to-all-done.1 = bf16[2,1,256,256]{3,0,1,2:T(2,128)(2,1)S(1)} async-done(((bf16[2,1,256,256]{3,0,1,2:T(2,128)(2,1)}), bf16[2,1,256,256]{3,0,1,2:T(2,128)(2,1)S(1)}, u32[]{:S(2)}, u32[]{:S(2)}) %all-to-all-start.1) | async-done | bytes 262176 | tf_op jit(solution)/shard_map/all_to_all | solution.py:91
  29.1 1.1 %slice_reduce_fusion.1 = (bf16[256,256]{1,0:T(8,128)(2,1)S(1)}, bf16[256,256]{1,0:T(8,128)(2,1)S(1)}) fusion(bf16[2,1,256,256]{3,0,1,2:T(2,128)(2,1)S(1)} %all-to-all-done.1), kind=kLoop, calls=%fused_computation.28 | loop fusion | bytes 524288 | tf_op jit(solution)/shard_map/slice | solution.py:44
  30.3 0.6 %fusion.55 = f32[32,8192]{1,0:T(8,128)S(1)} fusion(f32[32,8]{0,1:T(8,128)S(1)} %pad_maximum_fusion.1, bf16[8,8192]{1,0:T(8,128)(2,1)S(1)} %squeeze.22), kind=kOutput, calls=%fused_computation.82 | convolution fusion | flops 25165824 | bytes 1180672 | tf_op jit(solution)/shard_map/dot_general | solution.py:35
  31.0 0.6 %fusion.56 = f32[32,8192]{1,0:T(8,128)S(1)} fusion(f32[32,8]{0,1:T(8,128)S(1)} %pad_maximum_fusion.1, bf16[8,8192]{1,0:T(8,128)(2,1)S(1)} %squeeze.23), kind=kOutput, calls=%fused_computation.83 | convolution fusion | flops 25165824 | bytes 1180672 | tf_op jit(solution)/shard_map/dot_general | solution.py:36
  31.9 0.6 %fusion.7 = f32[16,8192]{1,0:T(8,128)S(1)} fusion(f32[16,8192]{1,0:T(8,128)S(1)} %get-tuple-element.12, f32[16,8192]{1,0:T(8,128)S(1)} %get-tuple-element.11, f32[8,16]{1,0:T(8,128)S(1)} %get-tuple-element.20, f32[8,16]{1,0:T(8,128)S(1)} %get-tuple-element.19, f32[8,16]{1,0:T(8,128)S(1)} %fusion.46), kind=kOutput, calls=%fused_computation.11 | convolution fusion | flops 50595840 | bytes 1574400 | tf_op jit(solution)/shard_map/dot_general | solution.py:50
  32.6 0.7 %pad_maximum_fusion = bf16[2,8,32,256]{3,2,0,1:T(8,128)(2,1)} fusion(bf16[1,8,32,256]{3,2,0,1:T(8,128)(2,1)S(1)} %copy.52, bf16[1,8,32,256]{3,2,0,1:T(8,128)(2,1)S(1)} %copy.51), kind=kLoop, calls=%fused_computation.31 | loop fusion | flops 131072 | bytes 524288 | tf_op jit(solution)/shard_map/stack | solution.py:57
  33.4 3.5 %all-to-all-start.2 = ((bf16[2,8,32,256]{3,2,0,1:T(8,128)(2,1)}), bf16[2,8,32,256]{3,2,0,1:T(8,128)(2,1)S(1)}, u32[]{:S(2)}, u32[]{:S(2)}) async-start(bf16[2,8,32,256]{3,2,0,1:T(8,128)(2,1)} %pad_maximum_fusion), calls=%async_computation.2 | async-start | bytes 524288 | tf_op jit(solution)/shard_map/all_to_all | solution.py:97
  36.9 0.7 %fusion.52 = (s32[1,1]{1,0:T(1,128)}, s32[1,1]{1,0:T(1,128)}) fusion(s32[1,2]{1,0:T(1,128)S(1)} %copy-done.4), kind=kLoop, calls=%fused_computation.79 | loop fusion | bytes 16 | tf_op jit(solution)/shard_map/slice | solution.py:99
  38.9 4.9 %all-to-all-done.2 = bf16[2,8,32,256]{3,2,0,1:T(8,128)(2,1)S(1)} async-done(((bf16[2,8,32,256]{3,2,0,1:T(8,128)(2,1)}), bf16[2,8,32,256]{3,2,0,1:T(8,128)(2,1)S(1)}, u32[]{:S(2)}, u32[]{:S(2)}) %all-to-all-start.2) | async-done | bytes 262176 | tf_op jit(solution)/shard_map/all_to_all | solution.py:97
  44.5 0.6 %fusion.49 = f32[]{:T(128)} fusion(f32[2]{0:T(128)S(1)} %copy-done.6, s32[]{:T(128)S(6)} %min.3), kind=kLoop, calls=%fused_computation.76 | loop fusion | flops 5 | bytes 16 | tf_op jit(solution)/shard_map/reduce_sum | solution.py:62
  46.4 0.7 %copy-done.3 = s32[3,3]{1,0:T(4,128)S(1)} copy-done((s32[3,3]{1,0:T(4,128)S(1)}, s32[3,3]{1,0:T(4,128)}, u32[]{:S(2)}) %copy-start.3) | copy-done | bytes 60
  47.0 0.6 %select_reduce_fusion = f32[]{:T(128)} fusion(s32[3,3]{1,0:T(4,128)S(1)} %copy-done.3, s32[]{:T(128)S(6)} %add.44), kind=kLoop, calls=%fused_computation.64 | loop fusion | flops 53 | bytes 44 | tf_op jit(solution)/shard_map/reduce_sum | solution.py:62
  50.2 1.9 %fusion.48 = (f32[]{:T(128)}, f32[]{:T(128)}) fusion(f32[3]{0:T(128)S(1)} %copy-done.5, s32[]{:T(128)} %bitcast.1, s32[]{:T(128)} %bitcast), kind=kLoop, calls=%fused_computation.75 | loop fusion | flops 16 | bytes 28 | tf_op jit(solution)/shard_map/reduce_sum | solution.py:62
  53.4 4.6 %collective-permute-done.1 = bf16[2,1,256,256]{2,3,0,1:T(8,128)(2,1)S(1)} collective-permute-done((bf16[2,1,256,256]{2,3,0,1:T(8,128)(2,1)S(1)}, bf16[2,1,256,256]{2,3,0,1:T(8,128)(2,1)S(1)}, u32[]{:S(2)}, u32[]{:S(2)}) %collective-permute-start.1) | collective-permute-done | bytes 262176 | tf_op jit(solution)/shard_map/ppermute | solution.py:14
  58.5 1.3 %fusion.6 = bf16[2,1,256,256]{3,2,1,0:T(8,128)(2,1)} fusion(f32[2,256,256]{2,1,0:T(8,128)S(1)} %fusion.3, bf16[2,256,256]{2,1,0:T(8,128)(2,1)S(1)} %bitcast.59, f32[]{:T(128)S(6)} %mul.121, bf16[256,256]{1,0:T(8,128)(2,1)S(1)} %copy-done), kind=kOutput, calls=%fused_computation.10 | convolution fusion | flops 134742016 | bytes 1179652 | tf_op jit(solution)/shard_map/ceij,jk->ceik/dot_general | solution.py:69
  (31 shorter events, 2.7 us)
Async XLA Ops:
  0.0 58.5 %copy-start = (bf16[256,256]{1,0:T(8,128)(2,1)S(1)}, bf16[256,256]{1,0:T(8,128)(2,1)}, u32[]{:S(2)}) copy-start(bf16[256,256]{1,0:T(8,128)(2,1)} %param.14) | copy-start | bytes 393220
  0.0 5.3 %copy-start.2 = (bf16[2,1,256,256]{3,2,1,0:T(8,128)(2,1)S(1)}, bf16[2,1,256,256]{3,2,1,0:T(8,128)(2,1)}, u32[]{:S(2)}) copy-start(bf16[2,1,256,256]{3,2,1,0:T(8,128)(2,1)} %param.8) | copy-start | bytes 786436
  1.2 17.6 %collective-permute-start = (bf16[2,1,256,256]{2,0,1,3:T(2,128)(2,1)S(1)}, bf16[2,1,256,256]{2,0,1,3:T(2,128)(2,1)}, u32[]{:S(2)}, u32[]{:S(2)}) collective-permute-start(bf16[2,1,256,256]{2,0,1,3:T(2,128)(2,1)S(1)} %copy.50), channel_id=1, source_target_pairs={{0,2},{1,3},{2,0},{3,1},{4,6},{5,7},{6,4},{7,5},{8,10},{9,11},{10,... | collective-permute-start | bytes 786440 | tf_op jit(solution)/shard_map/ppermute | solution.py:14
  6.3 10.7 %all-to-all-start = ((bf16[2,1,256,256]{3,0,1,2:T(2,128)(2,1)}), bf16[2,1,256,256]{3,0,1,2:T(2,128)(2,1)S(1)}, u32[]{:S(2)}, u32[]{:S(2)}) async-start(bf16[2,1,256,256]{3,0,1,2:T(2,128)(2,1)} %copy.49), calls=%async_computation | async-start | bytes 524288 | tf_op jit(solution)/shard_map/all_to_all | solution.py:90
  18.8 10.3 %all-to-all-start.1 = ((bf16[2,1,256,256]{3,0,1,2:T(2,128)(2,1)}), bf16[2,1,256,256]{3,0,1,2:T(2,128)(2,1)S(1)}, u32[]{:S(2)}, u32[]{:S(2)}) async-start(bf16[2,1,256,256]{3,0,1,2:T(2,128)(2,1)} %bitcast.2), calls=%async_computation.1 | async-start | bytes 524288 | tf_op jit(solution)/shard_map/all_to_all | solution.py:91
  33.4 3.6 %copy-start.4 = (s32[1,2]{1,0:T(1,128)S(1)}, s32[1,2]{1,0:T(1,128)}, u32[]{:S(2)}) copy-start(s32[1,2]{1,0:T(1,128)} %param.10) | copy-start | bytes 28
  33.4 10.4 %all-to-all-start.2 = ((bf16[2,8,32,256]{3,2,0,1:T(8,128)(2,1)}), bf16[2,8,32,256]{3,2,0,1:T(8,128)(2,1)S(1)}, u32[]{:S(2)}, u32[]{:S(2)}) async-start(bf16[2,8,32,256]{3,2,0,1:T(8,128)(2,1)} %pad_maximum_fusion), calls=%async_computation.2 | async-start | bytes 524288 | tf_op jit(solution)/shard_map/all_to_all | solution.py:97
  43.8 0.7 %copy-start.6 = (f32[2]{0:T(128)S(1)}, f32[2]{0:T(128)}, u32[]{:S(2)}) copy-start(f32[2]{0:T(128)} %param.12) | copy-start | bytes 28
  43.8 5.7 %copy-start.1 = (bf16[256,256]{1,0:T(8,128)(2,1)S(1)}, bf16[256,256]{1,0:T(8,128)(2,1)}, u32[]{:S(2)}) copy-start(bf16[256,256]{1,0:T(8,128)(2,1)} %param.15) | copy-start | bytes 393220
  44.0 14.0 %collective-permute-start.1 = (bf16[2,1,256,256]{2,3,0,1:T(8,128)(2,1)S(1)}, bf16[2,1,256,256]{2,3,0,1:T(8,128)(2,1)S(1)}, u32[]{:S(2)}, u32[]{:S(2)}) collective-permute-start(bf16[2,1,256,256]{2,3,0,1:T(8,128)(2,1)S(1)} %copy.57), channel_id=1, source_target_pairs={{0,2},{1,3},{2,0},{3,1},{4,6},{5,7},{6,4},{7,5},{8,10},{9,11},{10,... | collective-permute-start | bytes 786440 | tf_op jit(solution)/shard_map/ppermute | solution.py:14
  46.4 0.7 %copy-start.3 = (s32[3,3]{1,0:T(4,128)S(1)}, s32[3,3]{1,0:T(4,128)}, u32[]{:S(2)}) copy-start(s32[3,3]{1,0:T(4,128)} %param.13) | copy-start | bytes 112
  49.6 0.7 %copy-start.5 = (f32[3]{0:T(128)S(1)}, f32[3]{0:T(128)}, u32[]{:S(2)}) copy-start(f32[3]{0:T(128)} %param.11) | copy-start | bytes 40
where the time goes:
time: 60.4 us; the launch traced here: 59.8 us
  waiting for transfers between devices  22.4 us (37%)
  starting transfers between devices  15.2 us (25%)
  local copies, waits for them, and re-layouts  6.94 us (11%)
  between operations  5.96 us (10%)
  matrix products  4.93 us (8%)
  other arithmetic  4.37 us (7%)
    all_to_all x1, waiting for transfers between devices, on_device(): lax.all_to_all(green_less, 'energy', split_axis=2, concat_axis=1, tiled=T...  6.7 us
    all_to_all x1, waiting for transfers between devices, on_device(): lax.all_to_all(turned, 'energy', split_axis=2, concat_axis=1, tiled=True)  6.25 us
    all_to_all x1, waiting for transfers between devices, on_device(): lax.all_to_all(polar_rows, 'energy', split_axis=1, concat_axis=2, tiled=T...  4.94 us
    ppermute x2, waiting for transfers between devices, from_behind(): return lax.ppermute(value, axis, pairs)  4.56 us
    ppermute x2, starting transfers between devices, from_behind(): return lax.ppermute(value, axis, pairs)  4.51 us
    all_to_all x1, starting transfers between devices, on_device(): lax.all_to_all(green_less, 'energy', split_axis=2, concat_axis=1, tiled=T...  3.72 us
    unnamed x17, local copies, waits for them, and re-layouts  3.58 us
    all_to_all x1, starting transfers between devices, on_device(): lax.all_to_all(polar_rows, 'energy', split_axis=1, concat_axis=2, tiled=T...  3.54 us
  transfers between devices with their start and end apart: 5, of which 4 were waited for; matrix products, arithmetic and copies ran while one was open for 13% of the time, Pallas kernels for 0%

commit v1 on v0

v1 whole, which is shorter than its diff:
```python
import functools

import jax
import jax.numpy as jnp
from jax import lax
from jax.experimental import pallas as pl
from jax.experimental.pallas import tpu as pltpu
from jax.sharding import Mesh
from jax.sharding import PartitionSpec as P

BF16 = jnp.bfloat16
F32 = jnp.float32
VMEM = pl.BlockSpec(memory_space=pltpu.VMEM)
SMEM = pl.BlockSpec(memory_space=pltpu.SMEM)


def run_kernel(body, outs, args, specs=None, scratch=(), flops=0):
    return pl.pallas_call(
        body,
        out_shape=[jax.ShapeDtypeStruct(shape, dtype) for shape, dtype in outs],
        in_specs=specs or [VMEM] * len(args),
        out_specs=[VMEM] * len(outs),
        scratch_shapes=list(scratch),
        compiler_params=pltpu.CompilerParams(vmem_limit_bytes=12 * 2**20),
        cost_estimate=pl.CostEstimate(flops=flops, bytes_accessed=2**19, transcendentals=0),
    )(*args)


def split_body(whole, away, keep):
    core = lax.axis_index("core")
    for part in range(2):
        away[:, part] = whole[part, :, 1 - core]
        keep[:, part] = whole[part, :, core]


def sort_body(keep, got, *routes):
    chip = lax.axis_index("chip")
    for step, route in enumerate(routes):
        route[0] = keep[chip ^ step]
        route[1] = got[chip ^ step]


def turn_body(less, turned):
    groups, _, rows, _ = turned.shape
    for part in range(2):
        flipped = less[part, 0].astype(F32).T.astype(BF16)
        for group in range(groups):
            turned[group, part] = flipped[group * rows : (group + 1) * rows]


def lag_body(*refs):
    less, routes = refs[0], refs[1:-4]
    own, away, keep, more = refs[-4:]
    energies, _, rows, width = less.shape
    chip, core = lax.axis_index("chip"), lax.axis_index("core")
    for step, route in enumerate(routes):
        first = 2 * (chip ^ step)
        more[first + core] = route[0]
        more[first + 1 - core] = route[1]
    factor = energies ** (-0.5)
    for top in range(0, rows, 16):
        for left in range(0, width, 128):
            at = (pl.ds(top, 16), pl.ds(left, 128))
            for lag in range(energies):
                real = jnp.zeros((16, 128), F32)
                imag = jnp.zeros((16, 128), F32)
                for late in range(lag, energies):
                    lr = less[(late, 0) + at].astype(F32)
                    li = less[(late, 1) + at].astype(F32)
                    mr = more[(late - lag, 0) + at].astype(F32)
                    mi = more[(late - lag, 1) + at].astype(F32)
                    real += lr * mr - li * mi
                    imag += lr * mi + li * mr
                own[(lag, 0) + at] = (factor * imag).astype(BF16)
                own[(lag, 1) + at] = (-factor * real).astype(BF16)
    for chip_at in range(energies // 2):
        away[chip_at] = own[2 * chip_at + 1 - core]
        keep[chip_at] = own[2 * chip_at + core]


def across(left, turned):
    return lax.dot_general(
        left, turned, (((1,), (1,)), ((), ())), preferred_element_type=F32
    ).astype(BF16)


def own_body(blocks, onsite_scale, coupling_scale, mask, own, onsite, link, term, coupling, weight):
    row, col = blocks[0, 0], blocks[0, 1]
    low = jnp.minimum(row, col)
    scale = onsite_scale[row] * onsite_scale[col]
    strength = coupling_scale[low]
    weight[...] = jnp.full(
        weight.shape, mask[low, low + 1].astype(F32) * strength * strength, F32
    )
    width = onsite.shape[0]
    for part in range(2):
        inner = across(onsite[...], own[:, part].reshape(width, width))
        term[part] = scale * jnp.dot(inner, onsite[...], preferred_element_type=F32)

    @pl.when(row < col)
    def _():
        coupling[...] = link[...]

    @pl.when(row >= col)
    def _():
        coupling[...] = link[...].astype(F32).T.astype(BF16)


def join_body(*refs):
    routes = refs[:-5]
    term, coupling, weight, out, other = refs[-5:]
    rows = routes[0].shape[2]
    chip, core = lax.axis_index("chip"), lax.axis_index("core")
    for step, route in enumerate(routes):
        first = 2 * (chip ^ step)
        for part in range(2):
            other[part, pl.ds(pl.multiple_of((first + core) * rows, rows), rows)] = route[0, part]
            other[part, pl.ds(pl.multiple_of((first + 1 - core) * rows, rows), rows)] = route[1, part]
    for part in range(2):
        inner = across(coupling[...], other[part])
        mirrored = jnp.dot(inner, coupling[...], preferred_element_type=F32)
        mirrored = (weight[0, 0] * mirrored).astype(BF16).astype(F32)
        out[part, 0] = (term[part] + mirrored).astype(BF16)


def on_device(
    green_less,
    green_greater,
    pair_blocks,
    onsite_scale,
    coupling_scale,
    coupling_mask,
    onsite_block,
    coupling_block,
):
    chips = lax.axis_size("chip")
    energies = 2 * chips
    width = green_less.shape[3]
    rows = width // energies
    half_shape = (chips, 2, rows, width)
    full_shape = (energies, 2, rows, width)

    def swap_cores(value):
        return lax.ppermute(value, "core", [(0, 1), (1, 0)])

    def to_partner(keep, got):
        routes = run_kernel(
            sort_body, [((2, 2, rows, width), BF16)] * chips, (keep, got)
        )
        sent = []
        for step, route in enumerate(routes):
            pairs = [
                (chip * 2 + side, (chip ^ step) * 2 + 1 - side)
                for chip in range(chips)
                for side in range(2)
            ]
            sent.append(lax.ppermute(route, ("chip", "half"), pairs))
        return sent

    def regroup(value):
        return lax.all_to_all(value, ("chip", "core"), split_axis=0, concat_axis=0, tiled=True)

    away, keep = run_kernel(
        split_body,
        [(half_shape, BF16)] * 2,
        (green_greater.reshape(2, chips, 2, rows, width),),
    )
    more = to_partner(keep, swap_cores(away))
    (turned,) = run_kernel(turn_body, [(full_shape, BF16)], (green_less,))
    less = regroup(turned)
    own, away, keep = run_kernel(
        lag_body,
        [(full_shape, BF16), (half_shape, BF16), (half_shape, BF16)],
        (less, *more),
        scratch=[pltpu.VMEM(full_shape, BF16)],
        flops=energies * (energies + 1) * 4 * rows * width,
    )
    other = to_partner(keep, swap_cores(away))
    term, coupling, weight = run_kernel(
        own_body,
        [((2, width, width), F32), ((width, width), BF16), ((8, 128), F32)],
        (
            pair_blocks,
            onsite_scale,
            coupling_scale,
            coupling_mask,
            regroup(own),
            onsite_block,
            coupling_block,
        ),
        specs=[SMEM] * 4 + [VMEM] * 3,
        flops=8 * width**3,
    )
    (screened,) = run_kernel(
        join_body,
        [((2, 1, width, width), BF16)],
        (*other, term, coupling, weight),
        scratch=[pltpu.VMEM((2, width, width), BF16)],
        flops=8 * width**3,
    )
    return screened


def solution(mesh):
    energies, pairs = mesh.shape["energy"], mesh.shape["pair"]
    fine = Mesh(
        mesh.devices.reshape(energies // 2, 2, 2, pairs // 2), ("chip", "core", "half", "low")
    )
    across_mesh = P(None, ("chip", "core"), ("half", "low"), None)
    return jax.shard_map(
        on_device,
        mesh=fine,
        in_specs=(across_mesh, across_mesh, P(("half", "low"), None), P(), P(), P(), P(), P()),
        out_specs=across_mesh,
        check_vma=False,
    )
```

time: 60.4 us -> 50.8 us (0.84)
  starting transfers between devices: 15.2 us -> 25.2 us
  local copies, waits for them, and re-layouts: 6.94 us -> 0.98 us
  between operations: 5.96 us -> 0.11 us
  matrix products: 4.93 us -> 0 us
  Pallas kernels: 0 us -> 4.47 us
  other arithmetic: 4.37 us -> 0 us
  waiting for transfers between devices: 22.4 us -> 19.7 us
    all_to_all x3 -> x2, waiting for transfers between devices: 17.9 us -> 0.01 us  [regroup(): lax.all_to_all(value, ('chip', 'core'), split_axis=0, concat_axis=0, tile...]
    ppermute x2 -> x10, waiting for transfers between devices: 4.56 us -> 19.7 us  [the longest x8 17.7 us: to_partner(): sent.append(lax.ppermute(route, ('chip', 'half'), pairs))]
    ppermute x2 -> x10, starting transfers between devices: 4.51 us -> 16.4 us  [the longest x8 15.5 us: to_partner(): sent.append(lax.ppermute(route, ('chip', 'half'), pairs))]
    dot_general x7 -> x0, matrix products: 4.93 us -> none  [the longest x2 1.86 us: sandwich(): jnp.einsum('ceij,jk->ceik', inner_block, right_block, preferred_element_t...]
    pallas_call x0 -> x7, Pallas kernels: none -> 4.47 us  [run_kernel(): pl.pallas_call(body, out_shape=[jax.ShapeDtypeStruct(shape, dtype) for sh...]
    reduce_sum x3 -> x0, other arithmetic: 3.1 us -> none  [lookup(): jnp.sum(jnp.where(positions == wanted, source_table, jnp.zeros_like(sourc...]
    slice x3 -> x0, local copies, waits for them, and re-layouts: 2.9 us -> none  [the longest x2 2.23 us: spectrum(): return transform(forward, flat[0], flat[1], sign_flip)]
    unnamed x17 -> x16, local copies, waits for them, and re-layouts: 3.58 us -> 0.98 us
  transfers between devices with their start and end apart: 5 -> 12, of which waited for: 4 -> 8; matrix products, arithmetic and copies ran while one was open for 13% -> 0% of each run, Pallas kernels for 0% -> 2%
where the time goes in v1:
time: 50.8 us; the launch traced here: 50.4 us
  starting transfers between devices  25.2 us (50%)
  waiting for transfers between devices  19.7 us (39%)
  Pallas kernels  4.47 us (9%)
  local copies, waits for them, and re-layouts  0.98 us (2%)
    ppermute x8, waiting for transfers between devices, to_partner(): sent.append(lax.ppermute(route, ('chip', 'half'), pairs))  17.7 us
    ppermute x8, starting transfers between devices, to_partner(): sent.append(lax.ppermute(route, ('chip', 'half'), pairs))  15.5 us
    all_to_all x2, starting transfers between devices, regroup(): lax.all_to_all(value, ('chip', 'core'), split_axis=0, concat_axis=0, tile...  8.71 us
    pallas_call x7, Pallas kernels, run_kernel(): pl.pallas_call(body, out_shape=[jax.ShapeDtypeStruct(shape, dtype) for sh...  4.47 us
    ppermute x2, waiting for transfers between devices, swap_cores(): return lax.ppermute(value, 'core', [(0, 1), (1, 0)])  2 us
  transfers between devices with their start and end apart: 12, of which 8 were waited for; matrix products, arithmetic and copies ran while one was open for 0% of the time, Pallas kernels for 2%

profile of v1, /device:TPU:0, one launch (start us, length us, event | category | flops | bytes accessed | tf_op | source)
XLA Modules:
  0.0 50.4 jit_solution(2522658722900622569)
XLA Ops:
  0.0 0.9 %copy-done = bf16[2,1,256,256]{3,2,1,0:T(8,128)(2,1)S(1)} copy-done((bf16[2,1,256,256]{3,2,1,0:T(8,128)(2,1)S(1)}, bf16[2,1,256,256]{3,2,1,0:T(8,128)(2,1)}, u32[]{:S(2)}) %copy-start) | copy-done | bytes 262168
  1.0 0.8 %shard_map.82 = bf16[8,2,32,256]{3,2,1,0:T(8,128)(2,1)} custom-call(bf16[2,1,256,256]{3,2,1,0:T(8,128)(2,1)S(1)} %copy-done), custom_call_target="tpu_custom_call" | custom-call | bytes 524288 | tf_op jit(solution)/shard_map/pallas_call | solution.py:18
  1.8 5.3 %all-to-all-start = ((bf16[8,2,32,256]{3,2,1,0:T(8,128)(2,1)}), bf16[8,2,32,256]{3,2,1,0:T(8,128)(2,1)S(1)}, u32[]{:S(2)}, u32[]{:S(2)}) async-start(bf16[8,2,32,256]{3,2,1,0:T(8,128)(2,1)} %shard_map.82), calls=%async_computation | async-start | bytes 524288 | tf_op jit(solution)/shard_map/all_to_all | solution.py:161
  7.1 0.6 %collective-permute-start = (bf16[4,2,32,256]{3,2,1,0:T(8,128)(2,1)S(1)}, bf16[4,2,32,256]{3,2,1,0:T(8,128)(2,1)S(1)}, u32[]{:S(2)}, u32[]{:S(2)}) collective-permute-start(bf16[4,2,32,256]{3,2,1,0:T(8,128)(2,1)S(1)} %get-tuple-element.22), channel_id=1, source_target_pairs={{0,4},{4,0},{1,5},{5,1},{2,6},{6,2},{3,7},{7,3},{8,12},{12,8},{9,1... | collective-permute-start | bytes 393224 | tf_op jit(solution)/shard_map/ppermute | solution.py:144
  7.7 1.0 %collective-permute-done.got = bf16[4,2,32,256]{3,2,1,0:T(8,128)(2,1)S(1)} collective-permute-done((bf16[4,2,32,256]{3,2,1,0:T(8,128)(2,1)S(1)}, bf16[4,2,32,256]{3,2,1,0:T(8,128)(2,1)S(1)}, u32[]{:S(2)}, u32[]{:S(2)}) %collective-permute-start) | collective-permute-done | bytes 131104 | tf_op jit(solution)/shard_map/ppermute | solution.py:144
  8.7 2.7 %collective-permute-start.1 = (bf16[2,2,32,256]{3,2,1,0:T(8,128)(2,1)S(1)}, bf16[2,2,32,256]{3,2,1,0:T(8,128)(2,1)S(1)}, u32[]{:S(2)}, u32[]{:S(2)}) collective-permute-start(bf16[2,2,32,256]{3,2,1,0:T(8,128)(2,1)S(1)} %get-tuple-element.23), channel_id=1, source_target_pairs={{0,2},{2,0},{8,10},{10,8},{16,18},{18,16},{24,26},{26,24},{1,3},{3... | collective-permute-start | bytes 196616 | tf_op jit(solution)/shard_map/ppermute | solution.py:157
  11.4 1.6 %collective-permute-start.2 = (bf16[2,2,32,256]{3,2,1,0:T(8,128)(2,1)S(1)}, bf16[2,2,32,256]{3,2,1,0:T(8,128)(2,1)S(1)}, u32[]{:S(2)}, u32[]{:S(2)}) collective-permute-start(bf16[2,2,32,256]{3,2,1,0:T(8,128)(2,1)S(1)} %get-tuple-element.24), channel_id=1, source_target_pairs={{0,10},{2,8},{8,2},{10,0},{16,26},{18,24},{24,18},{26,16},{1,11},{... | collective-permute-start | bytes 196616 | tf_op jit(solution)/shard_map/ppermute | solution.py:157
  13.0 3.5 %collective-permute-start.3 = (bf16[2,2,32,256]{3,2,1,0:T(8,128)(2,1)S(1)}, bf16[2,2,32,256]{3,2,1,0:T(8,128)(2,1)S(1)}, u32[]{:S(2)}, u32[]{:S(2)}) collective-permute-start(bf16[2,2,32,256]{3,2,1,0:T(8,128)(2,1)S(1)} %get-tuple-element.25), channel_id=1, source_target_pairs={{0,18},{2,16},{8,26},{10,24},{16,2},{18,0},{24,10},{26,8},{1,19},{... | collective-permute-start | bytes 196616 | tf_op jit(solution)/shard_map/ppermute | solution.py:157
  16.5 4.8 %collective-permute-done.2.refs_2_ = bf16[2,2,32,256]{3,2,1,0:T(8,128)(2,1)S(1)} collective-permute-done((bf16[2,2,32,256]{3,2,1,0:T(8,128)(2,1)S(1)}, bf16[2,2,32,256]{3,2,1,0:T(8,128)(2,1)S(1)}, u32[]{:S(2)}, u32[]{:S(2)}) %collective-permute-start.2) | collective-permute-done | bytes 65568 | tf_op jit(solution)/shard_map/ppermute | solution.py:157
  21.3 3.4 %collective-permute-done.3.refs_3_ = bf16[2,2,32,256]{3,2,1,0:T(8,128)(2,1)S(1)} collective-permute-done((bf16[2,2,32,256]{3,2,1,0:T(8,128)(2,1)S(1)}, bf16[2,2,32,256]{3,2,1,0:T(8,128)(2,1)S(1)}, u32[]{:S(2)}, u32[]{:S(2)}) %collective-permute-start.3) | collective-permute-done | bytes 65568 | tf_op jit(solution)/shard_map/ppermute | solution.py:157
  24.7 1.3 %collective-permute-done.4.refs_4_ = bf16[2,2,32,256]{3,2,1,0:T(8,128)(2,1)S(1)} collective-permute-done((bf16[2,2,32,256]{3,2,1,0:T(8,128)(2,1)S(1)}, bf16[2,2,32,256]{3,2,1,0:T(8,128)(2,1)S(1)}, u32[]{:S(2)}, u32[]{:S(2)}) %collective-permute-start.4) | collective-permute-done | bytes 65568 | tf_op jit(solution)/shard_map/ppermute | solution.py:157
  26.0 1.1 %shard_map.85 = (bf16[8,2,32,256]{3,2,1,0:T(8,128)(2,1)}, bf16[4,2,32,256]{3,2,1,0:T(8,128)(2,1)S(1)}, bf16[4,2,32,256]{3,2,1,0:T(8,128)(2,1)S(1)}) custom-call(bf16[8,2,32,256]{3,2,1,0:T(8,128)(2,1)S(1)} %all-to-all-done.refs_0_, bf16[2,2,32,256]{3,2,1,0:T(8,128)(2,1)S(1)} %collective-permute-done.1.refs_1_, ...), custom_call_target="tpu_custom_call" | custom-call | flops 2359296 | bytes 524288 | tf_op jit(solution)/shard_map/pallas_call | solution.py:18
  27.1 3.4 %all-to-all-start.1 = ((bf16[8,2,32,256]{3,2,1,0:T(8,128)(2,1)}), bf16[8,2,32,256]{3,2,1,0:T(8,128)(2,1)S(1)}, u32[]{:S(2)}, u32[]{:S(2)}) async-start(bf16[8,2,32,256]{3,2,1,0:T(8,128)(2,1)} %get-tuple-element.33), calls=%async_computation.1 | async-start | bytes 524288 | tf_op jit(solution)/shard_map/all_to_all | solution.py:161
  30.5 0.4 collective-permute-start.5
  30.9 1.0 %collective-permute-done.5.got = bf16[4,2,32,256]{3,2,1,0:T(8,128)(2,1)S(1)} collective-permute-done((bf16[4,2,32,256]{3,2,1,0:T(8,128)(2,1)S(1)}, bf16[4,2,32,256]{3,2,1,0:T(8,128)(2,1)S(1)}, u32[]{:S(2)}, u32[]{:S(2)}) %collective-permute-start.5) | collective-permute-done | bytes 131104 | tf_op jit(solution)/shard_map/ppermute | solution.py:144
  32.0 0.1 collective-permute-start.6
  32.1 4.2 %collective-permute-start.7 = (bf16[2,2,32,256]{3,2,1,0:T(8,128)(2,1)S(1)}, bf16[2,2,32,256]{3,2,1,0:T(8,128)(2,1)S(1)}, u32[]{:S(2)}, u32[]{:S(2)}) collective-permute-start(bf16[2,2,32,256]{3,2,1,0:T(8,128)(2,1)S(1)} %get-tuple-element.30), channel_id=1, source_target_pairs={{0,10},{2,8},{8,2},{10,0},{16,26},{18,24},{24,18},{26,16},{1,11},{... | collective-permute-start | bytes 196616 | tf_op jit(solution)/shard_map/ppermute | solution.py:157
  36.3 1.0 %collective-permute-start.8 = (bf16[2,2,32,256]{3,2,1,0:T(8,128)(2,1)S(1)}, bf16[2,2,32,256]{3,2,1,0:T(8,128)(2,1)S(1)}, u32[]{:S(2)}, u32[]{:S(2)}) collective-permute-start(bf16[2,2,32,256]{3,2,1,0:T(8,128)(2,1)S(1)} %get-tuple-element.31), channel_id=1, source_target_pairs={{0,18},{2,16},{8,26},{10,24},{16,2},{18,0},{24,10},{26,8},{1,19},{... | collective-permute-start | bytes 196616 | tf_op jit(solution)/shard_map/ppermute | solution.py:157
  37.3 2.4 %collective-permute-start.9 = (bf16[2,2,32,256]{3,2,1,0:T(8,128)(2,1)S(1)}, bf16[2,2,32,256]{3,2,1,0:T(8,128)(2,1)S(1)}, u32[]{:S(2)}, u32[]{:S(2)}) collective-permute-start(bf16[2,2,32,256]{3,2,1,0:T(8,128)(2,1)S(1)} %get-tuple-element.32), channel_id=1, source_target_pairs={{0,26},{2,24},{8,18},{10,16},{16,10},{18,8},{24,2},{26,0},{1,27},{... | collective-permute-start | bytes 196616 | tf_op jit(solution)/shard_map/ppermute | solution.py:157
  39.7 1.1 %shard_map.87 = (f32[2,256,256]{2,1,0:T(8,128)S(1)}, bf16[256,256]{1,0:T(8,128)(2,1)S(1)}, f32[8,128]{1,0:T(8,128)S(1)}) custom-call(s32[1,2]{1,0:T(1,128)S(1)} %copy-done.5, f32[3]{0:T(128)S(1)} %copy-done.6, f32[2]{0:T(128)S(1)} %copy-done.7, s32[3,3]{1,0:T(4,128)S(1)} %copy-done.4, bf16[8,2,32,256]{3,2,1,0:T(8,128)(2,1)S(1)} %all-to-all-done.1.own, ...), custom_call_target="tpu_custom_call" | custom-call | flops 134217728 | bytes 524288 | tf_op jit(solution)/shard_map/pallas_call | solution.py:18
  40.9 4.6 %collective-permute-done.7.refs_1_ = bf16[2,2,32,256]{3,2,1,0:T(8,128)(2,1)S(1)} collective-permute-done((bf16[2,2,32,256]{3,2,1,0:T(8,128)(2,1)S(1)}, bf16[2,2,32,256]{3,2,1,0:T(8,128)(2,1)S(1)}, u32[]{:S(2)}, u32[]{:S(2)}) %collective-permute-start.7) | collective-permute-done | bytes 65568 | tf_op jit(solution)/shard_map/ppermute | solution.py:157
  45.5 2.1 %collective-permute-done.8.refs_2_ = bf16[2,2,32,256]{3,2,1,0:T(8,128)(2,1)S(1)} collective-permute-done((bf16[2,2,32,256]{3,2,1,0:T(8,128)(2,1)S(1)}, bf16[2,2,32,256]{3,2,1,0:T(8,128)(2,1)S(1)}, u32[]{:S(2)}, u32[]{:S(2)}) %collective-permute-start.8) | collective-permute-done | bytes 65568 | tf_op jit(solution)/shard_map/ppermute | solution.py:157
  47.5 1.6 %collective-permute-done.9.refs_3_ = bf16[2,2,32,256]{3,2,1,0:T(8,128)(2,1)S(1)} collective-permute-done((bf16[2,2,32,256]{3,2,1,0:T(8,128)(2,1)S(1)}, bf16[2,2,32,256]{3,2,1,0:T(8,128)(2,1)S(1)}, u32[]{:S(2)}, u32[]{:S(2)}) %collective-permute-start.9) | collective-permute-done | bytes 65568 | tf_op jit(solution)/shard_map/ppermute | solution.py:157
  49.1 1.3 %shard_map.88 = bf16[2,1,256,256]{3,2,1,0:T(8,128)(2,1)} custom-call(bf16[2,2,32,256]{3,2,1,0:T(8,128)(2,1)S(1)} %collective-permute-done.6.refs_0_, bf16[2,2,32,256]{3,2,1,0:T(8,128)(2,1)S(1)} %collective-permute-done.7.refs_1_, bf16[2,2,32,256]{3,2,1,0:T(8,128)(2,1)S(1)} %collective-permute-done.8.refs_2_, ...), custom_call_target="tpu_custom_call" | custom-call | flops 134217728 | bytes 524288 | tf_op jit(solution)/shard_map/pallas_call | solution.py:18
  (23 shorter events, 0.1 us)
Async XLA Ops:
  0.0 0.9 %copy-start = (bf16[2,1,256,256]{3,2,1,0:T(8,128)(2,1)S(1)}, bf16[2,1,256,256]{3,2,1,0:T(8,128)(2,1)}, u32[]{:S(2)}) copy-start(bf16[2,1,256,256]{3,2,1,0:T(8,128)(2,1)} %less.1) | copy-start | bytes 786436
  1.8 5.3 %copy-start.1 = (bf16[2,1,256,256]{3,2,1,0:T(8,128)(2,1)S(1)}, bf16[2,1,256,256]{3,2,1,0:T(8,128)(2,1)}, u32[]{:S(2)}) copy-start(bf16[2,1,256,256]{3,2,1,0:T(8,128)(2,1)} %param.9) | copy-start | bytes 786436
  1.8 24.2 %all-to-all-start = ((bf16[8,2,32,256]{3,2,1,0:T(8,128)(2,1)}), bf16[8,2,32,256]{3,2,1,0:T(8,128)(2,1)S(1)}, u32[]{:S(2)}, u32[]{:S(2)}) async-start(bf16[8,2,32,256]{3,2,1,0:T(8,128)(2,1)} %shard_map.82), calls=%async_computation | async-start | bytes 524288 | tf_op jit(solution)/shard_map/all_to_all | solution.py:161
  7.1 1.5 %collective-permute-start = (bf16[4,2,32,256]{3,2,1,0:T(8,128)(2,1)S(1)}, bf16[4,2,32,256]{3,2,1,0:T(8,128)(2,1)S(1)}, u32[]{:S(2)}, u32[]{:S(2)}) collective-permute-start(bf16[4,2,32,256]{3,2,1,0:T(8,128)(2,1)S(1)} %get-tuple-element.22), channel_id=1, source_target_pairs={{0,4},{4,0},{1,5},{5,1},{2,6},{6,2},{3,7},{7,3},{8,12},{12,8},{9,1... | collective-permute-start | bytes 393224 | tf_op jit(solution)/shard_map/ppermute | solution.py:144
  8.7 7.8 %collective-permute-start.1 = (bf16[2,2,32,256]{3,2,1,0:T(8,128)(2,1)S(1)}, bf16[2,2,32,256]{3,2,1,0:T(8,128)(2,1)S(1)}, u32[]{:S(2)}, u32[]{:S(2)}) collective-permute-start(bf16[2,2,32,256]{3,2,1,0:T(8,128)(2,1)S(1)} %get-tuple-element.23), channel_id=1, source_target_pairs={{0,2},{2,0},{8,10},{10,8},{16,18},{18,16},{24,26},{26,24},{1,3},{3... | collective-permute-start | bytes 196616 | tf_op jit(solution)/shard_map/ppermute | solution.py:157
  11.4 9.9 %collective-permute-start.2 = (bf16[2,2,32,256]{3,2,1,0:T(8,128)(2,1)S(1)}, bf16[2,2,32,256]{3,2,1,0:T(8,128)(2,1)S(1)}, u32[]{:S(2)}, u32[]{:S(2)}) collective-permute-start(bf16[2,2,32,256]{3,2,1,0:T(8,128)(2,1)S(1)} %get-tuple-element.24), channel_id=1, source_target_pairs={{0,10},{2,8},{8,2},{10,0},{16,26},{18,24},{24,18},{26,16},{1,11},{... | collective-permute-start | bytes 196616 | tf_op jit(solution)/shard_map/ppermute | solution.py:157
  13.0 11.7 %collective-permute-start.3 = (bf16[2,2,32,256]{3,2,1,0:T(8,128)(2,1)S(1)}, bf16[2,2,32,256]{3,2,1,0:T(8,128)(2,1)S(1)}, u32[]{:S(2)}, u32[]{:S(2)}) collective-permute-start(bf16[2,2,32,256]{3,2,1,0:T(8,128)(2,1)S(1)} %get-tuple-element.25), channel_id=1, source_target_pairs={{0,18},{2,16},{8,26},{10,24},{16,2},{18,0},{24,10},{26,8},{1,19},{... | collective-permute-start | bytes 196616 | tf_op jit(solution)/shard_map/ppermute | solution.py:157
  16.5 9.5 %collective-permute-start.4 = (bf16[2,2,32,256]{3,2,1,0:T(8,128)(2,1)S(1)}, bf16[2,2,32,256]{3,2,1,0:T(8,128)(2,1)S(1)}, u32[]{:S(2)}, u32[]{:S(2)}) collective-permute-start(bf16[2,2,32,256]{3,2,1,0:T(8,128)(2,1)S(1)} %get-tuple-element.26), channel_id=1, source_target_pairs={{0,26},{2,24},{8,18},{10,16},{16,10},{18,8},{24,2},{26,0},{1,27},{... | collective-permute-start | bytes 196616 | tf_op jit(solution)/shard_map/ppermute | solution.py:157
  27.1 12.6 %all-to-all-start.1 = ((bf16[8,2,32,256]{3,2,1,0:T(8,128)(2,1)}), bf16[8,2,32,256]{3,2,1,0:T(8,128)(2,1)S(1)}, u32[]{:S(2)}, u32[]{:S(2)}) async-start(bf16[8,2,32,256]{3,2,1,0:T(8,128)(2,1)} %get-tuple-element.33), calls=%async_computation.1 | async-start | bytes 524288 | tf_op jit(solution)/shard_map/all_to_all | solution.py:161
  30.5 1.4 %collective-permute-start.5 = (bf16[4,2,32,256]{3,2,1,0:T(8,128)(2,1)S(1)}, bf16[4,2,32,256]{3,2,1,0:T(8,128)(2,1)S(1)}, u32[]{:S(2)}, u32[]{:S(2)}) collective-permute-start(bf16[4,2,32,256]{3,2,1,0:T(8,128)(2,1)S(1)} %get-tuple-element.28), channel_id=1, source_target_pairs={{0,4},{4,0},{1,5},{5,1},{2,6},{6,2},{3,7},{7,3},{8,12},{12,8},{9,1... | collective-permute-start | bytes 393224 | tf_op jit(solution)/shard_map/ppermute | solution.py:144
  31.9 7.8 %copy-start.2 = (bf16[256,256]{1,0:T(8,128)(2,1)S(1)}, bf16[256,256]{1,0:T(8,128)(2,1)}, u32[]{:S(2)}) copy-start(bf16[256,256]{1,0:T(8,128)(2,1)} %onsite.1) | copy-start | bytes 393220
  31.9 7.8 %copy-start.3 = (bf16[256,256]{1,0:T(8,128)(2,1)S(1)}, bf16[256,256]{1,0:T(8,128)(2,1)}, u32[]{:S(2)}) copy-start(bf16[256,256]{1,0:T(8,128)(2,1)} %link.1) | copy-start | bytes 393220
  32.0 8.9 %collective-permute-start.6 = (bf16[2,2,32,256]{3,2,1,0:T(8,128)(2,1)S(1)}, bf16[2,2,32,256]{3,2,1,0:T(8,128)(2,1)S(1)}, u32[]{:S(2)}, u32[]{:S(2)}) collective-permute-start(bf16[2,2,32,256]{3,2,1,0:T(8,128)(2,1)S(1)} %get-tuple-element.29), channel_id=1, source_target_pairs={{0,2},{2,0},{8,10},{10,8},{16,18},{18,16},{24,26},{26,24},{1,3},{3... | collective-permute-start | bytes 196616 | tf_op jit(solution)/shard_map/ppermute | solution.py:157
  32.0 7.7 %copy-start.4 = (s32[3,3]{1,0:T(4,128)S(1)}, s32[3,3]{1,0:T(4,128)}, u32[]{:S(2)}) copy-start(s32[3,3]{1,0:T(4,128)} %mask.1) | copy-start | bytes 112
  32.1 13.4 %collective-permute-start.7 = (bf16[2,2,32,256]{3,2,1,0:T(8,128)(2,1)S(1)}, bf16[2,2,32,256]{3,2,1,0:T(8,128)(2,1)S(1)}, u32[]{:S(2)}, u32[]{:S(2)}) collective-permute-start(bf16[2,2,32,256]{3,2,1,0:T(8,128)(2,1)S(1)} %get-tuple-element.30), channel_id=1, source_target_pairs={{0,10},{2,8},{8,2},{10,0},{16,26},{18,24},{24,18},{26,16},{1,11},{... | collective-permute-start | bytes 196616 | tf_op jit(solution)/shard_map/ppermute | solution.py:157
  36.3 3.5 %copy-start.5 = (s32[1,2]{1,0:T(1,128)S(1)}, s32[1,2]{1,0:T(1,128)}, u32[]{:S(2)}) copy-start(s32[1,2]{1,0:T(1,128)} %blocks.1) | copy-start | bytes 28
  36.3 3.5 %copy-start.6 = (f32[3]{0:T(128)S(1)}, f32[3]{0:T(128)}, u32[]{:S(2)}) copy-start(f32[3]{0:T(128)} %onsite_scale.1) | copy-start | bytes 40
  36.3 3.5 %copy-start.7 = (f32[2]{0:T(128)S(1)}, f32[2]{0:T(128)}, u32[]{:S(2)}) copy-start(f32[2]{0:T(128)} %coupling_scale.1) | copy-start | bytes 28
  36.3 11.3 %collective-permute-start.8 = (bf16[2,2,32,256]{3,2,1,0:T(8,128)(2,1)S(1)}, bf16[2,2,32,256]{3,2,1,0:T(8,128)(2,1)S(1)}, u32[]{:S(2)}, u32[]{:S(2)}) collective-permute-start(bf16[2,2,32,256]{3,2,1,0:T(8,128)(2,1)S(1)} %get-tuple-element.31), channel_id=1, source_target_pairs={{0,18},{2,16},{8,26},{10,24},{16,2},{18,0},{24,10},{26,8},{1,19},{... | collective-permute-start | bytes 196616 | tf_op jit(solution)/shard_map/ppermute | solution.py:157
  37.3 11.9 %collective-permute-start.9 = (bf16[2,2,32,256]{3,2,1,0:T(8,128)(2,1)S(1)}, bf16[2,2,32,256]{3,2,1,0:T(8,128)(2,1)S(1)}, u32[]{:S(2)}, u32[]{:S(2)}) collective-permute-start(bf16[2,2,32,256]{3,2,1,0:T(8,128)(2,1)S(1)} %get-tuple-element.32), channel_id=1, source_target_pairs={{0,26},{2,24},{8,18},{10,16},{16,10},{18,8},{24,2},{26,0},{1,27},{... | collective-permute-start | bytes 196616 | tf_op jit(solution)/shard_map/ppermute | solution.py:157

commit v2 on v1

v2 whole, which is shorter than its diff:
```python
import functools

import jax
import jax.numpy as jnp
from jax import lax
from jax.experimental import pallas as pl
from jax.experimental.pallas import tpu as pltpu
from jax.sharding import Mesh
from jax.sharding import PartitionSpec as P

BF16 = jnp.bfloat16
F32 = jnp.float32
VMEM = pl.BlockSpec(memory_space=pltpu.VMEM)
SMEM = pl.BlockSpec(memory_space=pltpu.SMEM)


def run_kernel(body, outs, args, specs=None, scratch=(), flops=0):
    return pl.pallas_call(
        body,
        out_shape=[jax.ShapeDtypeStruct(shape, dtype) for shape, dtype in outs],
        in_specs=specs or [VMEM] * len(args),
        out_specs=[VMEM] * len(outs),
        scratch_shapes=list(scratch),
        compiler_params=pltpu.CompilerParams(vmem_limit_bytes=12 * 2**20),
        cost_estimate=pl.CostEstimate(flops=flops, bytes_accessed=2**19, transcendentals=0),
    )(*args)


def pack_body(less, more, packed):
    half = lax.axis_index("half")
    groups, _, _, rows, _ = packed.shape
    for part in range(2):
        flipped = less[part, 0].astype(F32).T.astype(BF16)
        for group in range(groups):
            span = slice(group * rows, (group + 1) * rows)
            packed[group, half, part] = flipped[span]
            packed[group, 1 - half, part] = more[part, 0, span]


def lag_body(given, polar):
    half = lax.axis_index("half")
    energies, _, _, rows, width = given.shape
    factor = energies ** (-0.5)
    for top in range(0, rows, 16):
        for left in range(0, width, 128):
            at = (pl.ds(top, 16), pl.ds(left, 128))
            for lag in range(energies):
                real = jnp.zeros((16, 128), F32)
                imag = jnp.zeros((16, 128), F32)
                for late in range(lag, energies):
                    lr = given[(late, half, 0) + at].astype(F32)
                    li = given[(late, half, 1) + at].astype(F32)
                    mr = given[(late - lag, 1 - half, 0) + at].astype(F32)
                    mi = given[(late - lag, 1 - half, 1) + at].astype(F32)
                    real += lr * mr - li * mi
                    imag += lr * mi + li * mr
                for side in range(2):
                    polar[(lag, side, 0) + at] = (factor * imag).astype(BF16)
                    polar[(lag, side, 1) + at] = (-factor * real).astype(BF16)


def across(left, turned):
    return lax.dot_general(
        left, turned, (((1,), (1,)), ((), ())), preferred_element_type=F32
    ).astype(BF16)


def screen_body(blocks, onsite_scale, coupling_scale, mask, polar, onsite, link, out, coupling):
    half = lax.axis_index("half")
    width = onsite.shape[0]
    row, col = blocks[0, 0], blocks[0, 1]
    low = jnp.minimum(row, col)
    scale = onsite_scale[row] * onsite_scale[col]
    strength = coupling_scale[low]
    weight = mask[low, low + 1].astype(F32) * strength * strength

    @pl.when(row < col)
    def _():
        coupling[...] = link[...]

    @pl.when(row >= col)
    def _():
        coupling[...] = link[...].astype(F32).T.astype(BF16)

    for part in range(2):
        own = polar[:, half, part].reshape(width, width)
        other = polar[:, 1 - half, part].reshape(width, width)
        inner = across(onsite[...], own)
        term = scale * jnp.dot(inner, onsite[...], preferred_element_type=F32)
        inner = across(coupling[...], other)
        mirrored = weight * jnp.dot(inner, coupling[...], preferred_element_type=F32)
        out[part, 0] = (term + mirrored.astype(BF16).astype(F32)).astype(BF16)


def on_device(
    green_less,
    green_greater,
    pair_blocks,
    onsite_scale,
    coupling_scale,
    coupling_mask,
    onsite_block,
    coupling_block,
):
    energies = 2 * lax.axis_size("chip")
    width = green_less.shape[3]
    rows = width // energies
    shape = (energies, 2, 2, rows, width)

    def regroup(value):
        flat = value.reshape((2 * energies,) + shape[2:])
        axes = ("chip", "core", "half")
        return lax.all_to_all(flat, axes, split_axis=0, concat_axis=0, tiled=True).reshape(shape)

    (packed,) = run_kernel(pack_body, [(shape, BF16)], (green_less, green_greater))
    (polar,) = run_kernel(
        lag_body,
        [(shape, BF16)],
        (regroup(packed),),
        flops=energies * (energies + 1) * 4 * rows * width,
    )
    (screened,) = run_kernel(
        screen_body,
        [((2, 1, width, width), BF16)],
        (
            pair_blocks,
            onsite_scale,
            coupling_scale,
            coupling_mask,
            regroup(polar),
            onsite_block,
            coupling_block,
        ),
        specs=[SMEM] * 4 + [VMEM] * 3,
        scratch=[pltpu.VMEM((width, width), BF16)],
        flops=16 * width**3,
    )
    return screened


def solution(mesh):
    energies, pairs = mesh.shape["energy"], mesh.shape["pair"]
    fine = Mesh(
        mesh.devices.reshape(energies // 2, 2, 2, pairs // 2), ("chip", "core", "half", "low")
    )
    across_mesh = P(None, ("chip", "core"), ("half", "low"), None)
    return jax.shard_map(
        on_device,
        mesh=fine,
        in_specs=(across_mesh, across_mesh, P(("half", "low"), None), P(), P(), P(), P(), P()),
        out_specs=across_mesh,
        check_vma=False,
    )
```

time: 50.8 us -> 46.9 us (0.923)
  blocking collectives: 0 us -> 41.3 us
  starting transfers between devices: 25.2 us -> 0 us
  waiting for transfers between devices: 19.7 us -> 0 us
  Pallas kernels: 4.47 us -> 2.65 us
  local copies, waits for them, and re-layouts: 0.98 us -> 2.58 us
    all_to_all x0 -> x2, blocking collectives: none -> 41.3 us  [regroup(): lax.all_to_all(flat, axes, split_axis=0, concat_axis=0, tiled=True)]
    ppermute x10 -> x0, waiting for transfers between devices: 19.7 us -> none  [the longest x8 17.7 us: to_partner(): sent.append(lax.ppermute(route, ('chip', 'half'), pairs))]
    ppermute x10 -> x0, starting transfers between devices: 16.4 us -> none  [the longest x8 15.5 us: to_partner(): sent.append(lax.ppermute(route, ('chip', 'half'), pairs))]
    all_to_all x2 -> x0, starting transfers between devices: 8.71 us -> none  [regroup(): lax.all_to_all(value, ('chip', 'core'), split_axis=0, concat_axis=0, tile...]
    pallas_call x7 -> x3, Pallas kernels: 4.47 us -> 2.65 us  [run_kernel(): pl.pallas_call(body, out_shape=[jax.ShapeDtypeStruct(shape, dtype) for sh...]
    unnamed x16, local copies, waits for them, and re-layouts: 0.98 us -> 2.58 us
  transfers between devices with their start and end apart: 12 -> 0, of which waited for: 8 -> 0; matrix products, arithmetic and copies ran while one was open for 0% -> 0% of each run, Pallas kernels for 2% -> 0%
where the time goes in v2:
time: 46.9 us; the launch traced here: 46.6 us
  blocking collectives  41.3 us (88%)
  Pallas kernels  2.65 us (6%)
  local copies, waits for them, and re-layouts  2.58 us (6%)
    all_to_all x2, blocking collectives, regroup(): lax.all_to_all(flat, axes, split_axis=0, concat_axis=0, tiled=True)  41.3 us
    pallas_call x3, Pallas kernels, run_kernel(): pl.pallas_call(body, out_shape=[jax.ShapeDtypeStruct(shape, dtype) for sh...  2.65 us
    unnamed x16, local copies, waits for them, and re-layouts  2.58 us

profile of v2, /device:TPU:0, one launch (start us, length us, event | category | flops | bytes accessed | tf_op | source)
XLA Modules:
  0.0 46.6 jit_solution(5277315468529299933)
XLA Ops:
  0.0 0.0 copy-start
  0.0 0.9 %copy-done = bf16[2,1,256,256]{3,2,1,0:T(8,128)(2,1)S(1)} copy-done((bf16[2,1,256,256]{3,2,1,0:T(8,128)(2,1)S(1)}, bf16[2,1,256,256]{3,2,1,0:T(8,128)(2,1)}, u32[]{:S(2)}) %copy-start) | copy-done | bytes 262168
  1.0 0.0 copy-start.1
  1.0 0.9 %copy-done.1 = bf16[2,1,256,256]{3,2,1,0:T(8,128)(2,1)S(1)} copy-done((bf16[2,1,256,256]{3,2,1,0:T(8,128)(2,1)S(1)}, bf16[2,1,256,256]{3,2,1,0:T(8,128)(2,1)}, u32[]{:S(2)}) %copy-start.1) | copy-done | bytes 262168
  1.9 0.1 shard_map.82
  2.1 22.4 %all_to_all.10 = bf16[16,2,32,256]{3,2,1,0:T(8,128)(2,1)S(1)} all-to-all(bf16[16,2,32,256]{3,2,1,0:T(8,128)(2,1)S(1)} %bitcast.7), channel_id=1, replica_groups=mesh['chip'=4,'core'=2,'half'=2,'low'=2] {'chip','core','half'}, dimensions={0} | all-to-all | bytes 1048576 | tf_op jit(solution)/shard_map/all_to_all | solution.py:113
  24.4 0.4 shard_map.83
  24.8 0.0 copy-start.2
  24.8 0.0 copy-start.3
  24.8 0.0 copy-start.4
  24.9 18.9 %all_to_all.11 = bf16[16,2,32,256]{3,2,1,0:T(8,128)(2,1)S(1)} all-to-all(bf16[16,2,32,256]{3,2,1,0:T(8,128)(2,1)S(1)} %bitcast.5), channel_id=1, replica_groups=mesh['chip'=4,'core'=2,'half'=2,'low'=2] {'chip','core','half'}, dimensions={0} | all-to-all | bytes 1048576 | tf_op jit(solution)/shard_map/all_to_all | solution.py:113
  43.8 0.0 copy-start.5
  43.8 0.0 copy-start.6
  43.8 0.0 copy-start.7
  43.8 0.0 copy-done.2
  43.8 0.0 copy-done.3
  43.8 0.0 copy-done.4
  43.8 0.6 %copy-done.5 = s32[1,2]{1,0:T(1,128)S(1)} copy-done((s32[1,2]{1,0:T(1,128)S(1)}, s32[1,2]{1,0:T(1,128)}, u32[]{:S(2)}) %copy-start.5) | copy-done | bytes 32
  44.5 0.0 copy-done.6
  44.5 0.0 copy-done.7
  44.5 2.1 %shard_map.84 = bf16[2,1,256,256]{3,2,1,0:T(8,128)(2,1)} custom-call(s32[1,2]{1,0:T(1,128)S(1)} %copy-done.5, f32[3]{0:T(128)S(1)} %copy-done.6, f32[2]{0:T(128)S(1)} %copy-done.7, s32[3,3]{1,0:T(4,128)S(1)} %copy-done.4, bf16[8,2,2,32,256]{4,3,2,1,0:T(8,128)(2,1)S(1)} %bitcast.6, bf16[256,256]{1,0:T(8,128)(2,1)S(1)} %copy-done.2, bf16[256,256]{1,0:T(8,128)(2,1)S(1)} %copy-done.3), custom_call_target="tpu_custom_call" | custom-call | flops 268435456 | bytes 524288 | tf_op jit(solution)/shard_map/pallas_call | solution.py:18
Async XLA Ops:
  0.0 0.9 %copy-start = (bf16[2,1,256,256]{3,2,1,0:T(8,128)(2,1)S(1)}, bf16[2,1,256,256]{3,2,1,0:T(8,128)(2,1)}, u32[]{:S(2)}) copy-start(bf16[2,1,256,256]{3,2,1,0:T(8,128)(2,1)} %less.1) | copy-start | bytes 786436
  1.0 0.9 %copy-start.1 = (bf16[2,1,256,256]{3,2,1,0:T(8,128)(2,1)S(1)}, bf16[2,1,256,256]{3,2,1,0:T(8,128)(2,1)}, u32[]{:S(2)}) copy-start(bf16[2,1,256,256]{3,2,1,0:T(8,128)(2,1)} %more.1) | copy-start | bytes 786436
  24.8 19.0 %copy-start.2 = (bf16[256,256]{1,0:T(8,128)(2,1)S(1)}, bf16[256,256]{1,0:T(8,128)(2,1)}, u32[]{:S(2)}) copy-start(bf16[256,256]{1,0:T(8,128)(2,1)} %onsite.1) | copy-start | bytes 393220
  24.8 19.0 %copy-start.3 = (bf16[256,256]{1,0:T(8,128)(2,1)S(1)}, bf16[256,256]{1,0:T(8,128)(2,1)}, u32[]{:S(2)}) copy-start(bf16[256,256]{1,0:T(8,128)(2,1)} %link.1) | copy-start | bytes 393220
  24.8 19.0 %copy-start.4 = (s32[3,3]{1,0:T(4,128)S(1)}, s32[3,3]{1,0:T(4,128)}, u32[]{:S(2)}) copy-start(s32[3,3]{1,0:T(4,128)} %mask.1) | copy-start | bytes 112
  43.8 0.7 %copy-start.5 = (s32[1,2]{1,0:T(1,128)S(1)}, s32[1,2]{1,0:T(1,128)}, u32[]{:S(2)}) copy-start(s32[1,2]{1,0:T(1,128)} %blocks.1) | copy-start | bytes 28
  43.8 0.7 %copy-start.6 = (f32[3]{0:T(128)S(1)}, f32[3]{0:T(128)}, u32[]{:S(2)}) copy-start(f32[3]{0:T(128)} %onsite_scale.1) | copy-start | bytes 40
  43.8 0.7 %copy-start.7 = (f32[2]{0:T(128)S(1)}, f32[2]{0:T(128)}, u32[]{:S(2)}) copy-start(f32[2]{0:T(128)} %coupling_scale.1) | copy-start | bytes 28

commit v3 on v2

v3 whole, which is shorter than its diff:
```python
import functools

import jax
import jax.numpy as jnp
from jax import lax
from jax.experimental import pallas as pl
from jax.experimental.pallas import tpu as pltpu
from jax.sharding import Mesh
from jax.sharding import PartitionSpec as P

BF16 = jnp.bfloat16
F32 = jnp.float32
VMEM = pl.BlockSpec(memory_space=pltpu.VMEM)
SMEM = pl.BlockSpec(memory_space=pltpu.SMEM)
HBM = pl.BlockSpec(memory_space=pltpu.HBM)


def run_kernel(body, outs, args, specs=None, out_specs=None, scratch=(), flops=0):
    return pl.pallas_call(
        body,
        out_shape=[jax.ShapeDtypeStruct(shape, dtype) for shape, dtype in outs],
        in_specs=specs or [VMEM] * len(args),
        out_specs=out_specs or [VMEM] * len(outs),
        scratch_shapes=list(scratch),
        compiler_params=pltpu.CompilerParams(vmem_limit_bytes=12 * 2**20),
        cost_estimate=pl.CostEstimate(flops=flops, bytes_accessed=2**19, transcendentals=0),
    )(*args)


def rows_of(first, rows):
    return pl.ds(pl.multiple_of(first * rows, rows), rows)


def order_of(chips, second):
    plane = [(0, step) for step in range(1, chips)]
    cross = [(1, step) for step in range(chips)]
    return plane + cross if second else cross + plane


def in_second():
    return 2 * lax.axis_index("low") >= lax.axis_size("low")


def turn_of(chips, turn):
    second = in_second()
    return [
        jnp.where(second, late, soon)
        for soon, late in zip(order_of(chips, False)[turn], order_of(chips, True)[turn])
    ]


def pack_body(less, more, away, keep, held, turned, sems):
    chip, core = lax.axis_index("chip"), lax.axis_index("core")
    copies = [
        pltpu.make_async_copy(source, held.at[place], sems.at[place])
        for place, source in enumerate((less, more))
    ]
    for copy in copies:
        copy.start()
    rows = away.shape[3]
    for kind in range(2):
        copies[kind].wait()
        for part in range(2):
            whole = held[kind, part, 0]
            if kind == 0:
                whole = whole.astype(F32).T.astype(BF16)
            turned[part] = whole
        for place in range(away.shape[0]):
            first = 2 * (chip ^ place)
            away[place, kind] = turned[:, rows_of(first + 1 - core, rows)]
            keep[place, kind] = turned[:, rows_of(first + core, rows)]


def pair_body(keep, got, *blocks):
    chips, kinds = keep.shape[:2]
    for turn, block in enumerate(blocks):
        crosses, step = turn_of(chips, turn)
        kind = crosses if kinds == 2 else 0
        block[0] = keep[step, kind]
        block[1] = got[step, kind]


def lag_body(keep, got, *refs):
    blocks, (away, kept, joined, polar) = refs[:-4], refs[-4:]
    chip, core = lax.axis_index("chip"), lax.axis_index("core")
    energies, _, rows, width = polar.shape
    chips = energies // 2
    joined[2 * chip + core, 0] = keep[0, 0]
    joined[2 * chip + 1 - core, 0] = got[0, 0]
    for turn, block in enumerate(blocks):
        crosses, step = turn_of(chips, turn)
        joined[2 * (chip ^ step) + core, crosses] = block[0]
        joined[2 * (chip ^ step) + 1 - core, crosses] = block[1]
    factor = energies ** (-0.5)
    for top in range(0, rows, 16):
        for left in range(0, width, 128):
            at = (pl.ds(top, 16), pl.ds(left, 128))
            for lag in range(energies):
                real = imag = jnp.zeros((16, 128), F32)
                for late in range(lag, energies):
                    lr = joined[(late, 0, 0) + at].astype(F32)
                    li = joined[(late, 0, 1) + at].astype(F32)
                    mr = joined[(late - lag, 1, 0) + at].astype(F32)
                    mi = joined[(late - lag, 1, 1) + at].astype(F32)
                    real += lr * mr - li * mi
                    imag += lr * mi + li * mr
                polar[(lag, 0) + at] = (factor * imag).astype(BF16)
                polar[(lag, 1) + at] = (-factor * real).astype(BF16)
    for place in range(chips):
        first = 2 * (chip ^ place)
        away[place, 0] = polar[first + 1 - core]
        kept[place, 0] = polar[first + core]


def across(left, turned):
    return lax.dot_general(
        left, turned, (((1,), (1,)), ((), ())), preferred_element_type=F32
    ).astype(BF16)


def weigh_body(blocks, onsite_scale, coupling_scale, mask, link, _, coupling, weights):
    row, col = blocks[0, 0], blocks[0, 1]
    low = jnp.minimum(row, col)
    strength = coupling_scale[low]
    weights[0] = jnp.full(weights.shape[1:], onsite_scale[row] * onsite_scale[col], F32)
    weights[1] = jnp.full(
        weights.shape[1:], mask[low, low + 1].astype(F32) * strength * strength, F32
    )

    @pl.when(row < col)
    def _():
        coupling[...] = link[...]

    @pl.when(row >= col)
    def _():
        coupling[...] = link[...].astype(F32).T.astype(BF16)


def screen_body(onsite, coupling, weights, keep, got, *refs):
    blocks = refs[:-4]
    out, whole, ready, sems = refs[-4:]
    chip, core = lax.axis_index("chip"), lax.axis_index("core")
    chips, _, _, rows, _ = keep.shape

    def put(slot, step, mine, theirs):
        whole[slot, :, rows_of(2 * (chip ^ step) + core, rows)] = mine
        whole[slot, :, rows_of(2 * (chip ^ step) + 1 - core, rows)] = theirs

    put(0, 0, keep[0, 0], got[0, 0])
    for turn, block in enumerate(blocks):
        crosses, step = turn_of(chips, turn)
        put(crosses, step, block[0], block[1])
    copies = []
    for part in range(2):
        inner = across(onsite[...], whole[0, part])
        term = weights[0, 0, 0] * jnp.dot(inner, onsite[...], preferred_element_type=F32)
        inner = across(coupling[...], whole[1, part])
        mirrored = weights[1, 0, 0] * jnp.dot(inner, coupling[...], preferred_element_type=F32)
        ready[part, 0] = (term + mirrored.astype(BF16).astype(F32)).astype(BF16)
        copies.append(pltpu.make_async_copy(ready.at[part], out.at[part], sems.at[part]))
        copies[-1].start()
    for copy in copies:
        copy.wait()


def on_device(
    green_less,
    green_greater,
    pair_blocks,
    onsite_scale,
    coupling_scale,
    coupling_mask,
    onsite_block,
    coupling_block,
):
    chips, lows = lax.axis_size("chip"), lax.axis_size("low")
    energies = 2 * chips
    width = green_less.shape[3]
    rows = width // energies

    def piles(kinds):
        return ((chips, kinds, 2, rows, width), BF16)

    def spread(away, keep):
        got = lax.ppermute(away, "core", [(0, 1), (1, 0)])
        turns = 2 * chips - 1
        blocks = run_kernel(pair_body, [((2, 2, rows, width), BF16)] * turns, (keep, got))
        came = []
        for turn, block in enumerate(blocks):
            pairs = []
            for chip in range(chips):
                for half in range(2):
                    for low in range(lows):
                        crosses, step = order_of(chips, 2 * low >= lows)[turn]
                        source = (chip * 2 + half) * lows + low
                        target = ((chip ^ step) * 2 + (half ^ crosses)) * lows + low
                        pairs.append((source, target))
            came.append(lax.ppermute(block, ("chip", "half", "low"), pairs))
        return keep, got, *came

    away, keep = run_kernel(
        pack_body,
        [piles(2)] * 2,
        (green_less, green_greater),
        specs=[HBM] * 2,
        scratch=[
            pltpu.VMEM((2, 2, 1, width, width), BF16),
            pltpu.VMEM((2, width, width), BF16),
            pltpu.SemaphoreType.DMA((2,)),
        ],
    )
    away, keep = run_kernel(
        lag_body,
        [piles(1)] * 2,
        spread(away, keep),
        scratch=[
            pltpu.VMEM((energies, 2, 2, rows, width), BF16),
            pltpu.VMEM((energies, 2, rows, width), BF16),
        ],
        flops=energies * (energies + 1) * 4 * rows * width,
    )
    parts = spread(away, keep)
    coupling, weights = run_kernel(
        weigh_body,
        [((width, width), BF16), ((2, 8, 128), F32)],
        (pair_blocks, onsite_scale, coupling_scale, coupling_mask, coupling_block, away),
        specs=[SMEM] * 4 + [VMEM] * 2,
    )
    (screened,) = run_kernel(
        screen_body,
        [((2, 1, width, width), BF16)],
        (onsite_block, coupling, weights, *parts),
        out_specs=[HBM],
        scratch=[
            pltpu.VMEM((2, 2, width, width), BF16),
            pltpu.VMEM((2, 1, width, width), BF16),
            pltpu.SemaphoreType.DMA((2,)),
        ],
        flops=16 * width**3,
    )
    return screened


def solution(mesh):
    energies, pairs = mesh.shape["energy"], mesh.shape["pair"]
    fine = Mesh(
        mesh.devices.reshape(energies // 2, 2, 2, pairs // 2), ("chip", "core", "half", "low")
    )
    across_mesh = P(None, ("chip", "core"), ("half", "low"), None)
    return jax.shard_map(
        on_device,
        mesh=fine,
        in_specs=(across_mesh, across_mesh, P(("half", "low"), None), P(), P(), P(), P(), P()),
        out_specs=across_mesh,
        check_vma=False,
    )
```

time: 46.9 us -> 41.6 us (0.89)
  blocking collectives: 41.3 us -> 0 us
  starting transfers between devices: 0 us -> 25.9 us
  waiting for transfers between devices: 0 us -> 10.6 us
  local copies, waits for them, and re-layouts: 2.58 us -> 1.92 us
    all_to_all x2 -> x0, blocking collectives: 41.3 us -> none  [regroup(): lax.all_to_all(flat, axes, split_axis=0, concat_axis=0, tiled=True)]
    ppermute x0 -> x16, starting transfers between devices: none -> 25.9 us  [the longest x14 25.3 us: spread(): came.append(lax.ppermute(block, ('chip', 'half', 'low'), pairs))]
    ppermute x0 -> x16, waiting for transfers between devices: none -> 10.6 us  [the longest x14 8.1 us: spread(): came.append(lax.ppermute(block, ('chip', 'half', 'low'), pairs))]
    unnamed x16, local copies, waits for them, and re-layouts: 2.58 us -> 1.92 us
    pallas_call x3 -> x6, Pallas kernels: 2.65 us -> 2.91 us  [run_kernel(): pl.pallas_call(body, out_shape=[jax.ShapeDtypeStruct(shape, dtype) for sh...]
  transfers between devices with their start and end apart: 0 -> 16, of which waited for: 0 -> 6; matrix products, arithmetic and copies ran while one was open for 0% -> 0% of each run, Pallas kernels for 0% -> 2%
where the time goes in v3:
time: 41.6 us; the launch traced here: 41.4 us
  starting transfers between devices  25.9 us (62%)
  waiting for transfers between devices  10.6 us (25%)
  Pallas kernels  2.91 us (7%)
  local copies, waits for them, and re-layouts  1.92 us (5%)
    ppermute x14, starting transfers between devices, spread(): came.append(lax.ppermute(block, ('chip', 'half', 'low'), pairs))  25.3 us
    ppermute x14, waiting for transfers between devices, spread(): came.append(lax.ppermute(block, ('chip', 'half', 'low'), pairs))  8.1 us
    pallas_call x6, Pallas kernels, run_kernel(): pl.pallas_call(body, out_shape=[jax.ShapeDtypeStruct(shape, dtype) for sh...  2.91 us
    ppermute x2, waiting for transfers between devices, spread(): got = lax.ppermute(away, 'core', [(0, 1), (1, 0)])  2.5 us
    unnamed x16, local copies, waits for them, and re-layouts  1.92 us
  transfers between devices with their start and end apart: 16, of which 6 were waited for; matrix products, arithmetic and copies ran while one was open for 0% of the time, Pallas kernels for 2%

profile of v3, /device:TPU:0, one launch (start us, length us, event | category | flops | bytes accessed | tf_op | source)
XLA Modules:
  0.0 41.4 jit_solution(13574594710593195422)
XLA Ops:
  0.0 0.9 %copy-done = bf16[2,1,256,256]{3,2,1,0:T(8,128)(2,1)S(1)} copy-done((bf16[2,1,256,256]{3,2,1,0:T(8,128)(2,1)S(1)}, bf16[2,1,256,256]{3,2,1,0:T(8,128)(2,1)}, u32[]{:S(2)}) %copy-start) | copy-done | bytes 262168
  1.0 0.9 %copy-done.1 = bf16[2,1,256,256]{3,2,1,0:T(8,128)(2,1)S(1)} copy-done((bf16[2,1,256,256]{3,2,1,0:T(8,128)(2,1)S(1)}, bf16[2,1,256,256]{3,2,1,0:T(8,128)(2,1)}, u32[]{:S(2)}) %copy-start.1) | copy-done | bytes 262168
  2.2 0.5 %collective-permute-start = (bf16[4,2,2,32,256]{4,3,2,1,0:T(8,128)(2,1)S(1)}, bf16[4,2,2,32,256]{4,3,2,1,0:T(8,128)(2,1)S(1)}, u32[]{:S(2)}, u32[]{:S(2)}) collective-permute-start(bf16[4,2,2,32,256]{4,3,2,1,0:T(8,128)(2,1)S(1)} %get-tuple-element.26), channel_id=1, source_target_pairs={{0,4},{4,0},{1,5},{5,1},{2,6},{6,2},{3,7},{7,3},{8,12},{12,8},{9,1... | collective-permute-start | bytes 786440 | tf_op jit(solution)/shard_map/ppermute | solution.py:185
  2.7 1.2 %collective-permute-done.got = bf16[4,2,2,32,256]{4,3,2,1,0:T(8,128)(2,1)S(1)} collective-permute-done((bf16[4,2,2,32,256]{4,3,2,1,0:T(8,128)(2,1)S(1)}, bf16[4,2,2,32,256]{4,3,2,1,0:T(8,128)(2,1)S(1)}, u32[]{:S(2)}, u32[]{:S(2)}) %collective-permute-start) | collective-permute-done | bytes 262176 | tf_op jit(solution)/shard_map/ppermute | solution.py:185
  3.9 4.0 %collective-permute-start.1 = (bf16[2,2,32,256]{3,2,1,0:T(8,128)(2,1)S(1)}, bf16[2,2,32,256]{3,2,1,0:T(8,128)(2,1)S(1)}, u32[]{:S(2)}, u32[]{:S(2)}) collective-permute-start(bf16[2,2,32,256]{3,2,1,0:T(8,128)(2,1)S(1)} %get-tuple-element.27), channel_id=1, source_target_pairs={{0,2},{1,9},{2,0},{3,11},{8,10},{9,1},{10,8},{11,3},{16,18},{17,25... | collective-permute-start | bytes 196616 | tf_op jit(solution)/shard_map/ppermute | solution.py:198
  7.9 1.3 %collective-permute-start.2 = (bf16[2,2,32,256]{3,2,1,0:T(8,128)(2,1)S(1)}, bf16[2,2,32,256]{3,2,1,0:T(8,128)(2,1)S(1)}, u32[]{:S(2)}, u32[]{:S(2)}) collective-permute-start(bf16[2,2,32,256]{3,2,1,0:T(8,128)(2,1)S(1)} %get-tuple-element.28), channel_id=1, source_target_pairs={{0,10},{1,17},{2,8},{3,19},{8,2},{9,25},{10,0},{11,27},{16,26},{17... | collective-permute-start | bytes 196616 | tf_op jit(solution)/shard_map/ppermute | solution.py:198
  9.2 3.5 %collective-permute-start.3 = (bf16[2,2,32,256]{3,2,1,0:T(8,128)(2,1)S(1)}, bf16[2,2,32,256]{3,2,1,0:T(8,128)(2,1)S(1)}, u32[]{:S(2)}, u32[]{:S(2)}) collective-permute-start(bf16[2,2,32,256]{3,2,1,0:T(8,128)(2,1)S(1)} %get-tuple-element.29), channel_id=1, source_target_pairs={{0,18},{1,25},{2,16},{3,27},{8,26},{9,17},{10,24},{11,19},{16,2},{... | collective-permute-start | bytes 196616 | tf_op jit(solution)/shard_map/ppermute | solution.py:198
  12.7 1.7 %collective-permute-start.5 = (bf16[2,2,32,256]{3,2,1,0:T(8,128)(2,1)S(1)}, bf16[2,2,32,256]{3,2,1,0:T(8,128)(2,1)S(1)}, u32[]{:S(2)}, u32[]{:S(2)}) collective-permute-start(bf16[2,2,32,256]{3,2,1,0:T(8,128)(2,1)S(1)} %get-tuple-element.31), channel_id=1, source_target_pairs={{0,8},{1,11},{2,10},{3,9},{8,0},{9,3},{10,2},{11,1},{16,24},{17,27... | collective-permute-start | bytes 196616 | tf_op jit(solution)/shard_map/ppermute | solution.py:198
  14.5 1.5 %collective-permute-start.6 = (bf16[2,2,32,256]{3,2,1,0:T(8,128)(2,1)S(1)}, bf16[2,2,32,256]{3,2,1,0:T(8,128)(2,1)S(1)}, u32[]{:S(2)}, u32[]{:S(2)}) collective-permute-start(bf16[2,2,32,256]{3,2,1,0:T(8,128)(2,1)S(1)} %get-tuple-element.32), channel_id=1, source_target_pairs={{0,16},{1,19},{2,18},{3,17},{8,24},{9,27},{10,26},{11,25},{16,0},{... | collective-permute-start | bytes 196616 | tf_op jit(solution)/shard_map/ppermute | solution.py:198
  16.0 2.0 %collective-permute-start.7 = (bf16[2,2,32,256]{3,2,1,0:T(8,128)(2,1)S(1)}, bf16[2,2,32,256]{3,2,1,0:T(8,128)(2,1)S(1)}, u32[]{:S(2)}, u32[]{:S(2)}) collective-permute-start(bf16[2,2,32,256]{3,2,1,0:T(8,128)(2,1)S(1)} %get-tuple-element.33), channel_id=1, source_target_pairs={{0,24},{1,27},{2,26},{3,25},{8,16},{9,19},{10,18},{11,17},{16,8},{... | collective-permute-start | bytes 196616 | tf_op jit(solution)/shard_map/ppermute | solution.py:198
  17.9 3.7 %collective-permute-done.3.refs_2_ = bf16[2,2,32,256]{3,2,1,0:T(8,128)(2,1)S(1)} collective-permute-done((bf16[2,2,32,256]{3,2,1,0:T(8,128)(2,1)S(1)}, bf16[2,2,32,256]{3,2,1,0:T(8,128)(2,1)S(1)}, u32[]{:S(2)}, u32[]{:S(2)}) %collective-permute-start.3) | collective-permute-done | bytes 65568 | tf_op jit(solution)/shard_map/ppermute | solution.py:198
  21.6 0.8 %collective-permute-done.4.refs_3_ = bf16[2,2,32,256]{3,2,1,0:T(8,128)(2,1)S(1)} collective-permute-done((bf16[2,2,32,256]{3,2,1,0:T(8,128)(2,1)S(1)}, bf16[2,2,32,256]{3,2,1,0:T(8,128)(2,1)S(1)}, u32[]{:S(2)}, u32[]{:S(2)}) %collective-permute-start.4) | collective-permute-done | bytes 65568 | tf_op jit(solution)/shard_map/ppermute | solution.py:198
  23.0 1.3 %collective-permute-done.8.got = bf16[4,1,2,32,256]{4,3,2,1,0:T(8,128)(2,1)S(1)} collective-permute-done((bf16[4,1,2,32,256]{4,3,2,1,0:T(8,128)(2,1)S(1)}, bf16[4,1,2,32,256]{4,3,2,1,0:T(8,128)(2,1)S(1)}, u32[]{:S(2)}, u32[]{:S(2)}) %collective-permute-start.8) | collective-permute-done | bytes 131104 | tf_op jit(solution)/shard_map/ppermute | solution.py:185
  24.4 1.3 %collective-permute-start.9 = (bf16[2,2,32,256]{3,2,1,0:T(8,128)(2,1)S(1)}, bf16[2,2,32,256]{3,2,1,0:T(8,128)(2,1)S(1)}, u32[]{:S(2)}, u32[]{:S(2)}) collective-permute-start(bf16[2,2,32,256]{3,2,1,0:T(8,128)(2,1)S(1)} %get-tuple-element.38), channel_id=1, source_target_pairs={{0,2},{1,9},{2,0},{3,11},{8,10},{9,1},{10,8},{11,3},{16,18},{17,25... | collective-permute-start | bytes 196616 | tf_op jit(solution)/shard_map/ppermute | solution.py:198
  25.7 2.4 %collective-permute-start.10 = (bf16[2,2,32,256]{3,2,1,0:T(8,128)(2,1)S(1)}, bf16[2,2,32,256]{3,2,1,0:T(8,128)(2,1)S(1)}, u32[]{:S(2)}, u32[]{:S(2)}) collective-permute-start(bf16[2,2,32,256]{3,2,1,0:T(8,128)(2,1)S(1)} %get-tuple-element.39), channel_id=1, source_target_pairs={{0,10},{1,17},{2,8},{3,19},{8,2},{9,25},{10,0},{11,27},{16,26},{17... | collective-permute-start | bytes 196616 | tf_op jit(solution)/shard_map/ppermute | solution.py:198
  28.1 0.5 %collective-permute-start.11 = (bf16[2,2,32,256]{3,2,1,0:T(8,128)(2,1)S(1)}, bf16[2,2,32,256]{3,2,1,0:T(8,128)(2,1)S(1)}, u32[]{:S(2)}, u32[]{:S(2)}) collective-permute-start(bf16[2,2,32,256]{3,2,1,0:T(8,128)(2,1)S(1)} %get-tuple-element.40), channel_id=1, source_target_pairs={{0,18},{1,25},{2,16},{3,27},{8,26},{9,17},{10,24},{11,19},{16,2},{... | collective-permute-start | bytes 196616 | tf_op jit(solution)/shard_map/ppermute | solution.py:198
  28.5 3.5 %collective-permute-start.12 = (bf16[2,2,32,256]{3,2,1,0:T(8,128)(2,1)S(1)}, bf16[2,2,32,256]{3,2,1,0:T(8,128)(2,1)S(1)}, u32[]{:S(2)}, u32[]{:S(2)}) collective-permute-start(bf16[2,2,32,256]{3,2,1,0:T(8,128)(2,1)S(1)} %get-tuple-element.41), channel_id=1, source_target_pairs={{0,26},{1,3},{2,24},{3,1},{8,18},{9,11},{10,16},{11,9},{16,10},{17... | collective-permute-start | bytes 196616 | tf_op jit(solution)/shard_map/ppermute | solution.py:198
  32.1 1.3 %collective-permute-start.13 = (bf16[2,2,32,256]{3,2,1,0:T(8,128)(2,1)S(1)}, bf16[2,2,32,256]{3,2,1,0:T(8,128)(2,1)S(1)}, u32[]{:S(2)}, u32[]{:S(2)}) collective-permute-start(bf16[2,2,32,256]{3,2,1,0:T(8,128)(2,1)S(1)} %get-tuple-element.42), channel_id=1, source_target_pairs={{0,8},{1,11},{2,10},{3,9},{8,0},{9,3},{10,2},{11,1},{16,24},{17,27... | collective-permute-start | bytes 196616 | tf_op jit(solution)/shard_map/ppermute | solution.py:198
  33.4 0.7 %collective-permute-start.14 = (bf16[2,2,32,256]{3,2,1,0:T(8,128)(2,1)S(1)}, bf16[2,2,32,256]{3,2,1,0:T(8,128)(2,1)S(1)}, u32[]{:S(2)}, u32[]{:S(2)}) collective-permute-start(bf16[2,2,32,256]{3,2,1,0:T(8,128)(2,1)S(1)} %get-tuple-element.43), channel_id=1, source_target_pairs={{0,16},{1,19},{2,18},{3,17},{8,24},{9,27},{10,26},{11,25},{16,0},{... | collective-permute-start | bytes 196616 | tf_op jit(solution)/shard_map/ppermute | solution.py:198
  34.1 1.6 %collective-permute-start.15 = (bf16[2,2,32,256]{3,2,1,0:T(8,128)(2,1)S(1)}, bf16[2,2,32,256]{3,2,1,0:T(8,128)(2,1)S(1)}, u32[]{:S(2)}, u32[]{:S(2)}) collective-permute-start(bf16[2,2,32,256]{3,2,1,0:T(8,128)(2,1)S(1)} %get-tuple-element.44), channel_id=1, source_target_pairs={{0,24},{1,27},{2,26},{3,25},{8,16},{9,19},{10,18},{11,17},{16,8},{... | collective-permute-start | bytes 196616 | tf_op jit(solution)/shard_map/ppermute | solution.py:198
  35.7 0.7 %shard_map.85 = (bf16[256,256]{1,0:T(8,128)(2,1)S(1)}, f32[2,8,128]{2,1,0:T(8,128)S(1)}) custom-call(s32[1,2]{1,0:T(1,128)S(1)} %copy-done.5, f32[3]{0:T(128)S(1)} %copy-done.6, f32[2]{0:T(128)S(1)} %copy-done.7, s32[3,3]{1,0:T(4,128)S(1)} %copy-done.4, bf16[256,256]{1,0:T(8,128)(2,1)S(1)} %copy-done.3, bf16[4,1,2,32,256]{4,3,2,1,0:T(8,128)(2,1)S(1)} %get-tuple-element.34._), custom_call_target="tpu_custom_call" | custom-call | bytes 524288 | tf_op jit(solution)/shard_map/pallas_call | solution.py:19
  36.4 1.3 %collective-permute-done.11.refs_2_ = bf16[2,2,32,256]{3,2,1,0:T(8,128)(2,1)S(1)} collective-permute-done((bf16[2,2,32,256]{3,2,1,0:T(8,128)(2,1)S(1)}, bf16[2,2,32,256]{3,2,1,0:T(8,128)(2,1)S(1)}, u32[]{:S(2)}, u32[]{:S(2)}) %collective-permute-start.11) | collective-permute-done | bytes 65568 | tf_op jit(solution)/shard_map/ppermute | solution.py:198
  37.7 2.3 %collective-permute-done.12.refs_3_ = bf16[2,2,32,256]{3,2,1,0:T(8,128)(2,1)S(1)} collective-permute-done((bf16[2,2,32,256]{3,2,1,0:T(8,128)(2,1)S(1)}, bf16[2,2,32,256]{3,2,1,0:T(8,128)(2,1)S(1)}, u32[]{:S(2)}, u32[]{:S(2)}) %collective-permute-start.12) | collective-permute-done | bytes 65568 | tf_op jit(solution)/shard_map/ppermute | solution.py:198
  40.0 1.4 %shard_map.87 = bf16[2,1,256,256]{3,2,1,0:T(8,128)(2,1)} custom-call(bf16[256,256]{1,0:T(8,128)(2,1)S(1)} %copy-done.2, bf16[256,256]{1,0:T(8,128)(2,1)S(1)} %get-tuple-element.35.coupling, f32[2,8,128]{2,1,0:T(8,128)S(1)} %get-tuple-element.36.weights, bf16[4,1,2,32,256]{4,3,2,1,0:T(8,128)(2,1)S(1)} %get-tuple-element.37.keep, ...), custom_call_target="tpu_custom_call" | custom-call | flops 268435456 | bytes 524288 | tf_op jit(solution)/shard_map/pallas_call | solution.py:19
  (30 shorter events, 0.9 us)
Async XLA Ops:
  0.0 0.9 %copy-start = (bf16[2,1,256,256]{3,2,1,0:T(8,128)(2,1)S(1)}, bf16[2,1,256,256]{3,2,1,0:T(8,128)(2,1)}, u32[]{:S(2)}) copy-start(bf16[2,1,256,256]{3,2,1,0:T(8,128)(2,1)} %less.1) | copy-start | bytes 786436
  1.0 0.9 %copy-start.1 = (bf16[2,1,256,256]{3,2,1,0:T(8,128)(2,1)S(1)}, bf16[2,1,256,256]{3,2,1,0:T(8,128)(2,1)}, u32[]{:S(2)}) copy-start(bf16[2,1,256,256]{3,2,1,0:T(8,128)(2,1)} %more.1) | copy-start | bytes 786436
  2.2 1.7 %collective-permute-start = (bf16[4,2,2,32,256]{4,3,2,1,0:T(8,128)(2,1)S(1)}, bf16[4,2,2,32,256]{4,3,2,1,0:T(8,128)(2,1)S(1)}, u32[]{:S(2)}, u32[]{:S(2)}) collective-permute-start(bf16[4,2,2,32,256]{4,3,2,1,0:T(8,128)(2,1)S(1)} %get-tuple-element.26), channel_id=1, source_target_pairs={{0,4},{4,0},{1,5},{5,1},{2,6},{6,2},{3,7},{7,3},{8,12},{12,8},{9,1... | collective-permute-start | bytes 786440 | tf_op jit(solution)/shard_map/ppermute | solution.py:185
  3.9 10.6 %collective-permute-start.1 = (bf16[2,2,32,256]{3,2,1,0:T(8,128)(2,1)S(1)}, bf16[2,2,32,256]{3,2,1,0:T(8,128)(2,1)S(1)}, u32[]{:S(2)}, u32[]{:S(2)}) collective-permute-start(bf16[2,2,32,256]{3,2,1,0:T(8,128)(2,1)S(1)} %get-tuple-element.27), channel_id=1, source_target_pairs={{0,2},{1,9},{2,0},{3,11},{8,10},{9,1},{10,8},{11,3},{16,18},{17,25... | collective-permute-start | bytes 196616 | tf_op jit(solution)/shard_map/ppermute | solution.py:198
  7.9 8.1 %collective-permute-start.2 = (bf16[2,2,32,256]{3,2,1,0:T(8,128)(2,1)S(1)}, bf16[2,2,32,256]{3,2,1,0:T(8,128)(2,1)S(1)}, u32[]{:S(2)}, u32[]{:S(2)}) collective-permute-start(bf16[2,2,32,256]{3,2,1,0:T(8,128)(2,1)S(1)} %get-tuple-element.28), channel_id=1, source_target_pairs={{0,10},{1,17},{2,8},{3,19},{8,2},{9,25},{10,0},{11,27},{16,26},{17... | collective-permute-start | bytes 196616 | tf_op jit(solution)/shard_map/ppermute | solution.py:198
  9.2 12.4 %collective-permute-start.3 = (bf16[2,2,32,256]{3,2,1,0:T(8,128)(2,1)S(1)}, bf16[2,2,32,256]{3,2,1,0:T(8,128)(2,1)S(1)}, u32[]{:S(2)}, u32[]{:S(2)}) collective-permute-start(bf16[2,2,32,256]{3,2,1,0:T(8,128)(2,1)S(1)} %get-tuple-element.29), channel_id=1, source_target_pairs={{0,18},{1,25},{2,16},{3,27},{8,26},{9,17},{10,24},{11,19},{16,2},{... | collective-permute-start | bytes 196616 | tf_op jit(solution)/shard_map/ppermute | solution.py:198
  12.7 9.7 %collective-permute-start.4 = (bf16[2,2,32,256]{3,2,1,0:T(8,128)(2,1)S(1)}, bf16[2,2,32,256]{3,2,1,0:T(8,128)(2,1)S(1)}, u32[]{:S(2)}, u32[]{:S(2)}) collective-permute-start(bf16[2,2,32,256]{3,2,1,0:T(8,128)(2,1)S(1)} %get-tuple-element.30), channel_id=1, source_target_pairs={{0,26},{1,3},{2,24},{3,1},{8,18},{9,11},{10,16},{11,9},{16,10},{17... | collective-permute-start | bytes 196616 | tf_op jit(solution)/shard_map/ppermute | solution.py:198
  12.7 9.7 %collective-permute-start.5 = (bf16[2,2,32,256]{3,2,1,0:T(8,128)(2,1)S(1)}, bf16[2,2,32,256]{3,2,1,0:T(8,128)(2,1)S(1)}, u32[]{:S(2)}, u32[]{:S(2)}) collective-permute-start(bf16[2,2,32,256]{3,2,1,0:T(8,128)(2,1)S(1)} %get-tuple-element.31), channel_id=1, source_target_pairs={{0,8},{1,11},{2,10},{3,9},{8,0},{9,3},{10,2},{11,1},{16,24},{17,27... | collective-permute-start | bytes 196616 | tf_op jit(solution)/shard_map/ppermute | solution.py:198
  14.5 8.0 %collective-permute-start.6 = (bf16[2,2,32,256]{3,2,1,0:T(8,128)(2,1)S(1)}, bf16[2,2,32,256]{3,2,1,0:T(8,128)(2,1)S(1)}, u32[]{:S(2)}, u32[]{:S(2)}) collective-permute-start(bf16[2,2,32,256]{3,2,1,0:T(8,128)(2,1)S(1)} %get-tuple-element.32), channel_id=1, source_target_pairs={{0,16},{1,19},{2,18},{3,17},{8,24},{9,27},{10,26},{11,25},{16,0},{... | collective-permute-start | bytes 196616 | tf_op jit(solution)/shard_map/ppermute | solution.py:198
  16.0 6.5 %collective-permute-start.7 = (bf16[2,2,32,256]{3,2,1,0:T(8,128)(2,1)S(1)}, bf16[2,2,32,256]{3,2,1,0:T(8,128)(2,1)S(1)}, u32[]{:S(2)}, u32[]{:S(2)}) collective-permute-start(bf16[2,2,32,256]{3,2,1,0:T(8,128)(2,1)S(1)} %get-tuple-element.33), channel_id=1, source_target_pairs={{0,24},{1,27},{2,26},{3,25},{8,16},{9,19},{10,18},{11,17},{16,8},{... | collective-permute-start | bytes 196616 | tf_op jit(solution)/shard_map/ppermute | solution.py:198
  22.9 1.4 %collective-permute-start.8 = (bf16[4,1,2,32,256]{4,3,2,1,0:T(8,128)(2,1)S(1)}, bf16[4,1,2,32,256]{4,3,2,1,0:T(8,128)(2,1)S(1)}, u32[]{:S(2)}, u32[]{:S(2)}) collective-permute-start(bf16[4,1,2,32,256]{4,3,2,1,0:T(8,128)(2,1)S(1)} %get-tuple-element.34._), channel_id=1, source_target_pairs={{0,4},{4,0},{1,5},{5,1},{2,6},{6,2},{3,7},{7,3},{8,12},{12,8},{9,1... | collective-permute-start | bytes 393224 | tf_op jit(solution)/shard_map/ppermute | solution.py:185
  24.3 11.3 %copy-start.3 = (bf16[256,256]{1,0:T(8,128)(2,1)S(1)}, bf16[256,256]{1,0:T(8,128)(2,1)}, u32[]{:S(2)}) copy-start(bf16[256,256]{1,0:T(8,128)(2,1)} %link.1) | copy-start | bytes 393220
  24.4 9.0 %collective-permute-start.9 = (bf16[2,2,32,256]{3,2,1,0:T(8,128)(2,1)S(1)}, bf16[2,2,32,256]{3,2,1,0:T(8,128)(2,1)S(1)}, u32[]{:S(2)}, u32[]{:S(2)}) collective-permute-start(bf16[2,2,32,256]{3,2,1,0:T(8,128)(2,1)S(1)} %get-tuple-element.38), channel_id=1, source_target_pairs={{0,2},{1,9},{2,0},{3,11},{8,10},{9,1},{10,8},{11,3},{16,18},{17,25... | collective-permute-start | bytes 196616 | tf_op jit(solution)/shard_map/ppermute | solution.py:198
  25.7 8.4 %collective-permute-start.10 = (bf16[2,2,32,256]{3,2,1,0:T(8,128)(2,1)S(1)}, bf16[2,2,32,256]{3,2,1,0:T(8,128)(2,1)S(1)}, u32[]{:S(2)}, u32[]{:S(2)}) collective-permute-start(bf16[2,2,32,256]{3,2,1,0:T(8,128)(2,1)S(1)} %get-tuple-element.39), channel_id=1, source_target_pairs={{0,10},{1,17},{2,8},{3,19},{8,2},{9,25},{10,0},{11,27},{16,26},{17... | collective-permute-start | bytes 196616 | tf_op jit(solution)/shard_map/ppermute | solution.py:198
  28.1 9.6 %collective-permute-start.11 = (bf16[2,2,32,256]{3,2,1,0:T(8,128)(2,1)S(1)}, bf16[2,2,32,256]{3,2,1,0:T(8,128)(2,1)S(1)}, u32[]{:S(2)}, u32[]{:S(2)}) collective-permute-start(bf16[2,2,32,256]{3,2,1,0:T(8,128)(2,1)S(1)} %get-tuple-element.40), channel_id=1, source_target_pairs={{0,18},{1,25},{2,16},{3,27},{8,26},{9,17},{10,24},{11,19},{16,2},{... | collective-permute-start | bytes 196616 | tf_op jit(solution)/shard_map/ppermute | solution.py:198
  28.5 11.4 %collective-permute-start.12 = (bf16[2,2,32,256]{3,2,1,0:T(8,128)(2,1)S(1)}, bf16[2,2,32,256]{3,2,1,0:T(8,128)(2,1)S(1)}, u32[]{:S(2)}, u32[]{:S(2)}) collective-permute-start(bf16[2,2,32,256]{3,2,1,0:T(8,128)(2,1)S(1)} %get-tuple-element.41), channel_id=1, source_target_pairs={{0,26},{1,3},{2,24},{3,1},{8,18},{9,11},{10,16},{11,9},{16,10},{17... | collective-permute-start | bytes 196616 | tf_op jit(solution)/shard_map/ppermute | solution.py:198
  32.1 3.6 %copy-start.4 = (s32[3,3]{1,0:T(4,128)S(1)}, s32[3,3]{1,0:T(4,128)}, u32[]{:S(2)}) copy-start(s32[3,3]{1,0:T(4,128)} %mask.1) | copy-start | bytes 112
  32.1 7.9 %collective-permute-start.13 = (bf16[2,2,32,256]{3,2,1,0:T(8,128)(2,1)S(1)}, bf16[2,2,32,256]{3,2,1,0:T(8,128)(2,1)S(1)}, u32[]{:S(2)}, u32[]{:S(2)}) collective-permute-start(bf16[2,2,32,256]{3,2,1,0:T(8,128)(2,1)S(1)} %get-tuple-element.42), channel_id=1, source_target_pairs={{0,8},{1,11},{2,10},{3,9},{8,0},{9,3},{10,2},{11,1},{16,24},{17,27... | collective-permute-start | bytes 196616 | tf_op jit(solution)/shard_map/ppermute | solution.py:198
  33.4 2.3 %copy-start.5 = (s32[1,2]{1,0:T(1,128)S(1)}, s32[1,2]{1,0:T(1,128)}, u32[]{:S(2)}) copy-start(s32[1,2]{1,0:T(1,128)} %blocks.1) | copy-start | bytes 28
  33.4 2.3 %copy-start.6 = (f32[3]{0:T(128)S(1)}, f32[3]{0:T(128)}, u32[]{:S(2)}) copy-start(f32[3]{0:T(128)} %onsite_scale.1) | copy-start | bytes 40
  33.4 2.3 %copy-start.7 = (f32[2]{0:T(128)S(1)}, f32[2]{0:T(128)}, u32[]{:S(2)}) copy-start(f32[2]{0:T(128)} %coupling_scale.1) | copy-start | bytes 28
  33.4 6.6 %collective-permute-start.14 = (bf16[2,2,32,256]{3,2,1,0:T(8,128)(2,1)S(1)}, bf16[2,2,32,256]{3,2,1,0:T(8,128)(2,1)S(1)}, u32[]{:S(2)}, u32[]{:S(2)}) collective-permute-start(bf16[2,2,32,256]{3,2,1,0:T(8,128)(2,1)S(1)} %get-tuple-element.43), channel_id=1, source_target_pairs={{0,16},{1,19},{2,18},{3,17},{8,24},{9,27},{10,26},{11,25},{16,0},{... | collective-permute-start | bytes 196616 | tf_op jit(solution)/shard_map/ppermute | solution.py:198
  34.1 5.9 %copy-start.2 = (bf16[256,256]{1,0:T(8,128)(2,1)S(1)}, bf16[256,256]{1,0:T(8,128)(2,1)}, u32[]{:S(2)}) copy-start(bf16[256,256]{1,0:T(8,128)(2,1)} %onsite.1) | copy-start | bytes 393220
  34.1 5.9 %collective-permute-start.15 = (bf16[2,2,32,256]{3,2,1,0:T(8,128)(2,1)S(1)}, bf16[2,2,32,256]{3,2,1,0:T(8,128)(2,1)S(1)}, u32[]{:S(2)}, u32[]{:S(2)}) collective-permute-start(bf16[2,2,32,256]{3,2,1,0:T(8,128)(2,1)S(1)} %get-tuple-element.44), channel_id=1, source_target_pairs={{0,24},{1,27},{2,26},{3,25},{8,16},{9,19},{10,18},{11,17},{16,8},{... | collective-permute-start | bytes 196616 | tf_op jit(solution)/shard_map/ppermute | solution.py:198

commit v4 on v3

--- a/solution.py
+++ b/solution.py
@@ -32,7 +32,7 @@
 
 
 def order_of(chips, second):
-    plane = [(0, step) for step in range(1, chips)]
+    plane = [(0, step) for step in reversed(range(1, chips))]
     cross = [(1, step) for step in range(chips)]
     return plane + cross if second else cross + plane
 
@@ -49,7 +49,7 @@
     ]
 
 
-def pack_body(less, more, away, keep, held, turned, sems):
+def pack_body(less, more, first, away, keep, held, turned, sems):
     chip, core = lax.axis_index("chip"), lax.axis_index("core")
     copies = [
         pltpu.make_async_copy(source, held.at[place], sems.at[place])
@@ -57,40 +57,59 @@
     ]
     for copy in copies:
         copy.start()
-    rows = away.shape[3]
+    chips, _, _, rows, _ = away.shape
     for kind in range(2):
         copies[kind].wait()
         for part in range(2):
             whole = held[kind, part, 0]
             if kind == 0:
                 whole = whole.astype(F32).T.astype(BF16)
-            turned[part] = whole
-        for place in range(away.shape[0]):
-            first = 2 * (chip ^ place)
-            away[place, kind] = turned[:, rows_of(first + 1 - core, rows)]
-            keep[place, kind] = turned[:, rows_of(first + core, rows)]
+            turned[kind, part] = whole
+    crosses, step = turn_of(chips, 0)
+    for owner in range(2):
+        first[owner] = turned[crosses, :, rows_of(2 * (chip ^ step) + owner, rows)]
+    for kind in range(2):
+        for place in range(chips):
+            top = 2 * (chip ^ place)
+            away[place, kind] = turned[kind, :, rows_of(top + 1 - core, rows)]
+            keep[place, kind] = turned[kind, :, rows_of(top + core, rows)]
 
 
 def pair_body(keep, got, *blocks):
     chips, kinds = keep.shape[:2]
-    for turn, block in enumerate(blocks):
+    for turn, block in enumerate(blocks, 1):
         crosses, step = turn_of(chips, turn)
         kind = crosses if kinds == 2 else 0
         block[0] = keep[step, kind]
         block[1] = got[step, kind]
 
 
-def lag_body(keep, got, *refs):
-    blocks, (away, kept, joined, polar) = refs[:-4], refs[-4:]
+def late_body(came, _, away):
+    away[...] = came[1 - lax.axis_index("core")]
+
+
+def sort_blocks(chips, blocks, late, put):
+    core = lax.axis_index("core")
+    for turn, block in enumerate(blocks):
+        crosses, step = turn_of(chips, turn)
+        if turn == 0:
+            put(crosses, step, block[core], late[...])
+        else:
+            put(crosses, step, block[0], block[1])
+
+
+def lag_body(keep, got, late, *refs):
+    blocks, (first, away, kept, joined, polar) = refs[:-5], refs[-5:]
     chip, core = lax.axis_index("chip"), lax.axis_index("core")
     energies, _, rows, width = polar.shape
     chips = energies // 2
-    joined[2 * chip + core, 0] = keep[0, 0]
-    joined[2 * chip + 1 - core, 0] = got[0, 0]
-    for turn, block in enumerate(blocks):
-        crosses, step = turn_of(chips, turn)
-        joined[2 * (chip ^ step) + core, crosses] = block[0]
-        joined[2 * (chip ^ step) + 1 - core, crosses] = block[1]
+
+    def put(crosses, step, mine, theirs):
+        joined[2 * (chip ^ step) + core, crosses] = mine
+        joined[2 * (chip ^ step) + 1 - core, crosses] = theirs
+
+    put(0, 0, keep[0, 0], got[0, 0])
+    sort_blocks(chips, blocks, late, put)
     factor = energies ** (-0.5)
     for top in range(0, rows, 16):
         for left in range(0, width, 128):
@@ -106,10 +125,13 @@
                     imag += lr * mi + li * mr
                 polar[(lag, 0) + at] = (factor * imag).astype(BF16)
                 polar[(lag, 1) + at] = (-factor * real).astype(BF16)
+    _, step = turn_of(chips, 0)
+    for owner in range(2):
+        first[owner] = polar[2 * (chip ^ step) + owner]
     for place in range(chips):
-        first = 2 * (chip ^ place)
-        away[place, 0] = polar[first + 1 - core]
-        kept[place, 0] = polar[first + core]
+        top = 2 * (chip ^ place)
+        away[place, 0] = polar[top + 1 - core]
+        kept[place, 0] = polar[top + core]
 
 
 def across(left, turned):
@@ -136,7 +158,7 @@
         coupling[...] = link[...].astype(F32).T.astype(BF16)
 
 
-def screen_body(onsite, coupling, weights, keep, got, *refs):
+def screen_body(onsite, coupling, weights, keep, got, late, *refs):
     blocks = refs[:-4]
     out, whole, ready, sems = refs[-4:]
     chip, core = lax.axis_index("chip"), lax.axis_index("core")
@@ -147,9 +169,7 @@
         whole[slot, :, rows_of(2 * (chip ^ step) + 1 - core, rows)] = theirs
 
     put(0, 0, keep[0, 0], got[0, 0])
-    for turn, block in enumerate(blocks):
-        crosses, step = turn_of(chips, turn)
-        put(crosses, step, block[0], block[1])
+    sort_blocks(chips, blocks, late, put)
     copies = []
     for part in range(2):
         inner = across(onsite[...], whole[0, part])
@@ -181,12 +201,16 @@
     def piles(kinds):
         return ((chips, kinds, 2, rows, width), BF16)
 
-    def spread(away, keep):
-        got = lax.ppermute(away, "core", [(0, 1), (1, 0)])
-        turns = 2 * chips - 1
-        blocks = run_kernel(pair_body, [((2, 2, rows, width), BF16)] * turns, (keep, got))
+    block_shape = ((2, 2, rows, width), BF16)
+
+    def swap_cores(value):
+        return lax.ppermute(value, "core", [(0, 1), (1, 0)])
+
+    def spread(first, away, keep):
+        got = swap_cores(away)
+        later = run_kernel(pair_body, [block_shape] * (2 * chips - 2), (keep, got))
         came = []
-        for turn, block in enumerate(blocks):
+        for turn, block in enumerate((first, *later)):
             pairs = []
             for chip in range(chips):
                 for half in range(2):
@@ -196,30 +220,31 @@
                         target = ((chip ^ step) * 2 + (half ^ crosses)) * lows + low
                         pairs.append((source, target))
             came.append(lax.ppermute(block, ("chip", "half", "low"), pairs))
-        return keep, got, *came
-
-    away, keep = run_kernel(
+        (away,) = run_kernel(late_body, [((2, rows, width), BF16)], (came[0], came[1]))
+        return keep, got, swap_cores(away), *came
+
+    first, away, keep = run_kernel(
         pack_body,
-        [piles(2)] * 2,
-        (green_less, green_greater),
+        [block_shape] + [piles(2)] * 2,
+        [pltpu.with_memory_space_constraint(value, pltpu.HBM) for value in (green_less, green_greater)],
         specs=[HBM] * 2,
         scratch=[
             pltpu.VMEM((2, 2, 1, width, width), BF16),
-            pltpu.VMEM((2, width, width), BF16),
+            pltpu.VMEM((2, 2, width, width), BF16),
             pltpu.SemaphoreType.DMA((2,)),
         ],
     )
-    away, keep = run_kernel(
+    first, away, keep = run_kernel(
         lag_body,
-        [piles(1)] * 2,
-        spread(away, keep),
+        [block_shape] + [piles(1)] * 2,
+        spread(first, away, keep),
         scratch=[
             pltpu.VMEM((energies, 2, 2, rows, width), BF16),
             pltpu.VMEM((energies, 2, rows, width), BF16),
         ],
         flops=energies * (energies + 1) * 4 * rows * width,
     )
-    parts = spread(away, keep)
+    parts = spread(first, away, keep)
     coupling, weights = run_kernel(
         weigh_body,
         [((width, width), BF16), ((2, 8, 128), F32)],

time: 41.6 us -> 38.6 us (0.928)
  local copies, waits for them, and re-layouts: 1.92 us -> 0.03 us
  starting transfers between devices: 25.9 us -> 24.2 us
  Pallas kernels: 2.91 us -> 3.82 us
    unnamed x16 -> x12, local copies, waits for them, and re-layouts: 1.92 us -> 0.03 us
    ppermute x14, starting transfers between devices: 25.3 us -> 23.5 us  [spread(): came.append(lax.ppermute(block, ('chip', 'half', 'low'), pairs))]
    ppermute x2 -> x4, waiting for transfers between devices: 2.5 us -> 1.34 us  [swap_cores(): return lax.ppermute(value, 'core', [(0, 1), (1, 0)])]
    pallas_call x6 -> x8, Pallas kernels: 2.91 us -> 3.82 us  [run_kernel(): pl.pallas_call(body, out_shape=[jax.ShapeDtypeStruct(shape, dtype) for sh...]
    ppermute x14, waiting for transfers between devices: 8.1 us -> 8.93 us  [spread(): came.append(lax.ppermute(block, ('chip', 'half', 'low'), pairs))]
  transfers between devices with their start and end apart: 16 -> 18, of which waited for: 6 -> 6; matrix products, arithmetic and copies ran while one was open for 0% -> 0% of each run, Pallas kernels for 2% -> 2%
where the time goes in v4:
time: 38.6 us; the launch traced here: 38.5 us
  starting transfers between devices  24.2 us (63%)
  waiting for transfers between devices  10.3 us (27%)
  Pallas kernels  3.82 us (10%)
    ppermute x14, starting transfers between devices, spread(): came.append(lax.ppermute(block, ('chip', 'half', 'low'), pairs))  23.5 us
    ppermute x14, waiting for transfers between devices, spread(): came.append(lax.ppermute(block, ('chip', 'half', 'low'), pairs))  8.93 us
    pallas_call x8, Pallas kernels, run_kernel(): pl.pallas_call(body, out_shape=[jax.ShapeDtypeStruct(shape, dtype) for sh...  3.82 us
    ppermute x4, waiting for transfers between devices, swap_cores(): return lax.ppermute(value, 'core', [(0, 1), (1, 0)])  1.34 us
  transfers between devices with their start and end apart: 18, of which 6 were waited for; matrix products, arithmetic and copies ran while one was open for 0% of the time, Pallas kernels for 2%

profile of v4, /device:TPU:0, one launch (start us, length us, event | category | flops | bytes accessed | tf_op | source)
XLA Modules:
  0.0 38.5 jit_solution(13720531838629579212)
XLA Ops:
  0.0 1.2 %shard_map.82 = (bf16[2,2,32,256]{3,2,1,0:T(8,128)(2,1)S(1)}, bf16[4,2,2,32,256]{4,3,2,1,0:T(8,128)(2,1)S(1)}, bf16[4,2,2,32,256]{4,3,2,1,0:T(8,128)(2,1)S(1)}) custom-call(bf16[2,1,256,256]{3,2,1,0:T(8,128)(2,1)} %less.1, bf16[2,1,256,256]{3,2,1,0:T(8,128)(2,1)} %more.1), custom_call_target="tpu_custom_call" | custom-call | bytes 524288 | tf_op jit(solution)/shard_map/pallas_call | solution.py:19
  1.2 0.5 %collective-permute-start = (bf16[4,2,2,32,256]{4,3,2,1,0:T(8,128)(2,1)S(1)}, bf16[4,2,2,32,256]{4,3,2,1,0:T(8,128)(2,1)S(1)}, u32[]{:S(2)}, u32[]{:S(2)}) collective-permute-start(bf16[4,2,2,32,256]{4,3,2,1,0:T(8,128)(2,1)S(1)} %get-tuple-element.26), channel_id=1, source_target_pairs={{0,4},{4,0},{1,5},{5,1},{2,6},{6,2},{3,7},{7,3},{8,12},{12,8},{9,1... | collective-permute-start | bytes 786440 | tf_op jit(solution)/shard_map/ppermute | solution.py:207
  1.7 3.7 %collective-permute-start.1 = (bf16[2,2,32,256]{3,2,1,0:T(8,128)(2,1)S(1)}, bf16[2,2,32,256]{3,2,1,0:T(8,128)(2,1)S(1)}, u32[]{:S(2)}, u32[]{:S(2)}) collective-permute-start(bf16[2,2,32,256]{3,2,1,0:T(8,128)(2,1)S(1)} %get-tuple-element.27), channel_id=1, source_target_pairs={{0,2},{1,25},{2,0},{3,27},{8,10},{9,17},{10,8},{11,19},{16,18},{17... | collective-permute-start | bytes 196616 | tf_op jit(solution)/shard_map/ppermute | solution.py:222
  5.4 2.4 %collective-permute-start.2 = (bf16[2,2,32,256]{3,2,1,0:T(8,128)(2,1)S(1)}, bf16[2,2,32,256]{3,2,1,0:T(8,128)(2,1)S(1)}, u32[]{:S(2)}, u32[]{:S(2)}) collective-permute-start(bf16[2,2,32,256]{3,2,1,0:T(8,128)(2,1)S(1)} %get-tuple-element.28), channel_id=1, source_target_pairs={{0,10},{1,17},{2,8},{3,19},{8,2},{9,25},{10,0},{11,27},{16,26},{17... | collective-permute-start | bytes 196616 | tf_op jit(solution)/shard_map/ppermute | solution.py:222
  7.8 2.4 %collective-permute-start.4 = (bf16[2,2,32,256]{3,2,1,0:T(8,128)(2,1)S(1)}, bf16[2,2,32,256]{3,2,1,0:T(8,128)(2,1)S(1)}, u32[]{:S(2)}, u32[]{:S(2)}) collective-permute-start(bf16[2,2,32,256]{3,2,1,0:T(8,128)(2,1)S(1)} %get-tuple-element.29), channel_id=1, source_target_pairs={{0,18},{1,9},{2,16},{3,11},{8,26},{9,1},{10,24},{11,3},{16,2},{17,... | collective-permute-start | bytes 196616 | tf_op jit(solution)/shard_map/ppermute | solution.py:222
  10.3 1.4 %collective-permute-start.5 = (bf16[2,2,32,256]{3,2,1,0:T(8,128)(2,1)S(1)}, bf16[2,2,32,256]{3,2,1,0:T(8,128)(2,1)S(1)}, u32[]{:S(2)}, u32[]{:S(2)}) collective-permute-start(bf16[2,2,32,256]{3,2,1,0:T(8,128)(2,1)S(1)} %get-tuple-element.30), channel_id=1, source_target_pairs={{0,26},{1,3},{2,24},{3,1},{8,18},{9,11},{10,16},{11,9},{16,10},{17... | collective-permute-start | bytes 196616 | tf_op jit(solution)/shard_map/ppermute | solution.py:222
  11.6 2.4 %collective-permute-start.6 = (bf16[2,2,32,256]{3,2,1,0:T(8,128)(2,1)S(1)}, bf16[2,2,32,256]{3,2,1,0:T(8,128)(2,1)S(1)}, u32[]{:S(2)}, u32[]{:S(2)}) collective-permute-start(bf16[2,2,32,256]{3,2,1,0:T(8,128)(2,1)S(1)} %get-tuple-element.31), channel_id=1, source_target_pairs={{0,24},{1,11},{2,26},{3,9},{8,16},{9,3},{10,18},{11,1},{16,8},{17,... | collective-permute-start | bytes 196616 | tf_op jit(solution)/shard_map/ppermute | solution.py:222
  14.1 0.5 %collective-permute-start.7 = (bf16[2,2,32,256]{3,2,1,0:T(8,128)(2,1)S(1)}, bf16[2,2,32,256]{3,2,1,0:T(8,128)(2,1)S(1)}, u32[]{:S(2)}, u32[]{:S(2)}) collective-permute-start(bf16[2,2,32,256]{3,2,1,0:T(8,128)(2,1)S(1)} %get-tuple-element.32), channel_id=1, source_target_pairs={{0,16},{1,19},{2,18},{3,17},{8,24},{9,27},{10,26},{11,25},{16,0},{... | collective-permute-start | bytes 196616 | tf_op jit(solution)/shard_map/ppermute | solution.py:222
  14.6 0.5 %collective-permute-start.8 = (bf16[2,2,32,256]{3,2,1,0:T(8,128)(2,1)S(1)}, bf16[2,2,32,256]{3,2,1,0:T(8,128)(2,1)S(1)}, u32[]{:S(2)}, u32[]{:S(2)}) collective-permute-start(bf16[2,2,32,256]{3,2,1,0:T(8,128)(2,1)S(1)} %get-tuple-element.33), channel_id=1, source_target_pairs={{0,8},{1,27},{2,10},{3,25},{8,0},{9,19},{10,2},{11,17},{16,24},{17... | collective-permute-start | bytes 196616 | tf_op jit(solution)/shard_map/ppermute | solution.py:222
  15.1 4.1 %collective-permute-done.4.refs_2_ = bf16[2,2,32,256]{3,2,1,0:T(8,128)(2,1)S(1)} collective-permute-done((bf16[2,2,32,256]{3,2,1,0:T(8,128)(2,1)S(1)}, bf16[2,2,32,256]{3,2,1,0:T(8,128)(2,1)S(1)}, u32[]{:S(2)}, u32[]{:S(2)}) %collective-permute-start.4) | collective-permute-done | bytes 65568 | tf_op jit(solution)/shard_map/ppermute | solution.py:222
  19.3 1.0 %collective-permute-done.5.refs_3_ = bf16[2,2,32,256]{3,2,1,0:T(8,128)(2,1)S(1)} collective-permute-done((bf16[2,2,32,256]{3,2,1,0:T(8,128)(2,1)S(1)}, bf16[2,2,32,256]{3,2,1,0:T(8,128)(2,1)S(1)}, u32[]{:S(2)}, u32[]{:S(2)}) %collective-permute-start.5) | collective-permute-done | bytes 65568 | tf_op jit(solution)/shard_map/ppermute | solution.py:222
  20.5 0.5 %shard_map.85 = (bf16[2,2,32,256]{3,2,1,0:T(8,128)(2,1)S(1)}, bf16[4,1,2,32,256]{4,3,2,1,0:T(8,128)(2,1)S(1)}, bf16[4,1,2,32,256]{4,3,2,1,0:T(8,128)(2,1)S(1)}) custom-call(bf16[4,2,2,32,256]{4,3,2,1,0:T(8,128)(2,1)S(1)} %get-tuple-element.25.keep, bf16[4,2,2,32,256]{4,3,2,1,0:T(8,128)(2,1)S(1)} %collective-permute-done.got, ...), custom_call_target="tpu_custom_call" | custom-call | flops 2359296 | bytes 524288 | tf_op jit(solution)/shard_map/pallas_call | solution.py:19
  20.9 0.2 collective-permute-start.9
  21.2 1.2 %collective-permute-done.9.got = bf16[4,1,2,32,256]{4,3,2,1,0:T(8,128)(2,1)S(1)} collective-permute-done((bf16[4,1,2,32,256]{4,3,2,1,0:T(8,128)(2,1)S(1)}, bf16[4,1,2,32,256]{4,3,2,1,0:T(8,128)(2,1)S(1)}, u32[]{:S(2)}, u32[]{:S(2)}) %collective-permute-start.9) | collective-permute-done | bytes 131104 | tf_op jit(solution)/shard_map/ppermute | solution.py:207
  22.4 2.3 %collective-permute-start.11 = (bf16[2,2,32,256]{3,2,1,0:T(8,128)(2,1)S(1)}, bf16[2,2,32,256]{3,2,1,0:T(8,128)(2,1)S(1)}, u32[]{:S(2)}, u32[]{:S(2)}) collective-permute-start(bf16[2,2,32,256]{3,2,1,0:T(8,128)(2,1)S(1)} %get-tuple-element.39), channel_id=1, source_target_pairs={{0,10},{1,17},{2,8},{3,19},{8,2},{9,25},{10,0},{11,27},{16,26},{17... | collective-permute-start | bytes 196616 | tf_op jit(solution)/shard_map/ppermute | solution.py:222
  24.7 1.3 %collective-permute-start.13 = (bf16[2,2,32,256]{3,2,1,0:T(8,128)(2,1)S(1)}, bf16[2,2,32,256]{3,2,1,0:T(8,128)(2,1)S(1)}, u32[]{:S(2)}, u32[]{:S(2)}) collective-permute-start(bf16[2,2,32,256]{3,2,1,0:T(8,128)(2,1)S(1)} %get-tuple-element.40), channel_id=1, source_target_pairs={{0,18},{1,9},{2,16},{3,11},{8,26},{9,1},{10,24},{11,3},{16,2},{17,... | collective-permute-start | bytes 196616 | tf_op jit(solution)/shard_map/ppermute | solution.py:222
  26.0 2.9 %collective-permute-start.14 = (bf16[2,2,32,256]{3,2,1,0:T(8,128)(2,1)S(1)}, bf16[2,2,32,256]{3,2,1,0:T(8,128)(2,1)S(1)}, u32[]{:S(2)}, u32[]{:S(2)}) collective-permute-start(bf16[2,2,32,256]{3,2,1,0:T(8,128)(2,1)S(1)} %get-tuple-element.41), channel_id=1, source_target_pairs={{0,26},{1,3},{2,24},{3,1},{8,18},{9,11},{10,16},{11,9},{16,10},{17... | collective-permute-start | bytes 196616 | tf_op jit(solution)/shard_map/ppermute | solution.py:222
  28.9 1.1 %collective-permute-start.15 = (bf16[2,2,32,256]{3,2,1,0:T(8,128)(2,1)S(1)}, bf16[2,2,32,256]{3,2,1,0:T(8,128)(2,1)S(1)}, u32[]{:S(2)}, u32[]{:S(2)}) collective-permute-start(bf16[2,2,32,256]{3,2,1,0:T(8,128)(2,1)S(1)} %get-tuple-element.42), channel_id=1, source_target_pairs={{0,24},{1,11},{2,26},{3,9},{8,16},{9,3},{10,18},{11,1},{16,8},{17,... | collective-permute-start | bytes 196616 | tf_op jit(solution)/shard_map/ppermute | solution.py:222
  30.0 1.4 %collective-permute-start.16 = (bf16[2,2,32,256]{3,2,1,0:T(8,128)(2,1)S(1)}, bf16[2,2,32,256]{3,2,1,0:T(8,128)(2,1)S(1)}, u32[]{:S(2)}, u32[]{:S(2)}) collective-permute-start(bf16[2,2,32,256]{3,2,1,0:T(8,128)(2,1)S(1)} %get-tuple-element.43), channel_id=1, source_target_pairs={{0,16},{1,19},{2,18},{3,17},{8,24},{9,27},{10,26},{11,25},{16,0},{... | collective-permute-start | bytes 196616 | tf_op jit(solution)/shard_map/ppermute | solution.py:222
  31.5 1.0 %collective-permute-start.17 = (bf16[2,2,32,256]{3,2,1,0:T(8,128)(2,1)S(1)}, bf16[2,2,32,256]{3,2,1,0:T(8,128)(2,1)S(1)}, u32[]{:S(2)}, u32[]{:S(2)}) collective-permute-start(bf16[2,2,32,256]{3,2,1,0:T(8,128)(2,1)S(1)} %get-tuple-element.44), channel_id=1, source_target_pairs={{0,8},{1,27},{2,10},{3,25},{8,0},{9,19},{10,2},{11,17},{16,24},{17... | collective-permute-start | bytes 196616 | tf_op jit(solution)/shard_map/ppermute | solution.py:222
  32.5 1.9 %collective-permute-done.13.refs_2_ = bf16[2,2,32,256]{3,2,1,0:T(8,128)(2,1)S(1)} collective-permute-done((bf16[2,2,32,256]{3,2,1,0:T(8,128)(2,1)S(1)}, bf16[2,2,32,256]{3,2,1,0:T(8,128)(2,1)S(1)}, u32[]{:S(2)}, u32[]{:S(2)}) %collective-permute-start.13) | collective-permute-done | bytes 65568 | tf_op jit(solution)/shard_map/ppermute | solution.py:222
  34.5 0.7 %shard_map.86 = (bf16[256,256]{1,0:T(8,128)(2,1)S(1)}, f32[2,8,128]{2,1,0:T(8,128)S(1)}) custom-call(s32[1,2]{1,0:T(1,128)S(1)} %copy-done.3, f32[3]{0:T(128)S(1)} %copy-done.4, f32[2]{0:T(128)S(1)} %copy-done.5, s32[3,3]{1,0:T(4,128)S(1)} %copy-done.2, bf16[256,256]{1,0:T(8,128)(2,1)S(1)} %copy-done.1, bf16[4,1,2,32,256]{4,3,2,1,0:T(8,128)(2,1)S(1)} %get-tuple-element.34._), custom_call_target="tpu_custom_call" | custom-call | bytes 524288 | tf_op jit(solution)/shard_map/pallas_call | solution.py:19
  35.2 1.8 %collective-permute-done.14.refs_3_ = bf16[2,2,32,256]{3,2,1,0:T(8,128)(2,1)S(1)} collective-permute-done((bf16[2,2,32,256]{3,2,1,0:T(8,128)(2,1)S(1)}, bf16[2,2,32,256]{3,2,1,0:T(8,128)(2,1)S(1)}, u32[]{:S(2)}, u32[]{:S(2)}) %collective-permute-start.14) | collective-permute-done | bytes 65568 | tf_op jit(solution)/shard_map/ppermute | solution.py:222
  37.0 1.4 %shard_map.89 = bf16[2,1,256,256]{3,2,1,0:T(8,128)(2,1)} custom-call(bf16[256,256]{1,0:T(8,128)(2,1)S(1)} %copy-done, bf16[256,256]{1,0:T(8,128)(2,1)S(1)} %get-tuple-element.35.coupling, f32[2,8,128]{2,1,0:T(8,128)S(1)} %get-tuple-element.36.weights, bf16[4,1,2,32,256]{4,3,2,1,0:T(8,128)(2,1)S(1)} %get-tuple-element.37.keep, ...), custom_call_target="tpu_custom_call" | custom-call | flops 268435456 | bytes 524288 | tf_op jit(solution)/shard_map/pallas_call | solution.py:19
  (32 shorter events, 0.3 us)
Async XLA Ops:
  1.2 4.2 %collective-permute-start = (bf16[4,2,2,32,256]{4,3,2,1,0:T(8,128)(2,1)S(1)}, bf16[4,2,2,32,256]{4,3,2,1,0:T(8,128)(2,1)S(1)}, u32[]{:S(2)}, u32[]{:S(2)}) collective-permute-start(bf16[4,2,2,32,256]{4,3,2,1,0:T(8,128)(2,1)S(1)} %get-tuple-element.26), channel_id=1, source_target_pairs={{0,4},{4,0},{1,5},{5,1},{2,6},{6,2},{3,7},{7,3},{8,12},{12,8},{9,1... | collective-permute-start | bytes 786440 | tf_op jit(solution)/shard_map/ppermute | solution.py:207
  1.7 12.4 %collective-permute-start.1 = (bf16[2,2,32,256]{3,2,1,0:T(8,128)(2,1)S(1)}, bf16[2,2,32,256]{3,2,1,0:T(8,128)(2,1)S(1)}, u32[]{:S(2)}, u32[]{:S(2)}) collective-permute-start(bf16[2,2,32,256]{3,2,1,0:T(8,128)(2,1)S(1)} %get-tuple-element.27), channel_id=1, source_target_pairs={{0,2},{1,25},{2,0},{3,27},{8,10},{9,17},{10,8},{11,19},{16,18},{17... | collective-permute-start | bytes 196616 | tf_op jit(solution)/shard_map/ppermute | solution.py:222
  5.4 9.2 %collective-permute-start.2 = (bf16[2,2,32,256]{3,2,1,0:T(8,128)(2,1)S(1)}, bf16[2,2,32,256]{3,2,1,0:T(8,128)(2,1)S(1)}, u32[]{:S(2)}, u32[]{:S(2)}) collective-permute-start(bf16[2,2,32,256]{3,2,1,0:T(8,128)(2,1)S(1)} %get-tuple-element.28), channel_id=1, source_target_pairs={{0,10},{1,17},{2,8},{3,19},{8,2},{9,25},{10,0},{11,27},{16,26},{17... | collective-permute-start | bytes 196616 | tf_op jit(solution)/shard_map/ppermute | solution.py:222
  7.8 11.4 %collective-permute-start.4 = (bf16[2,2,32,256]{3,2,1,0:T(8,128)(2,1)S(1)}, bf16[2,2,32,256]{3,2,1,0:T(8,128)(2,1)S(1)}, u32[]{:S(2)}, u32[]{:S(2)}) collective-permute-start(bf16[2,2,32,256]{3,2,1,0:T(8,128)(2,1)S(1)} %get-tuple-element.29), channel_id=1, source_target_pairs={{0,18},{1,9},{2,16},{3,11},{8,26},{9,1},{10,24},{11,3},{16,2},{17,... | collective-permute-start | bytes 196616 | tf_op jit(solution)/shard_map/ppermute | solution.py:222
  10.3 10.0 %collective-permute-start.5 = (bf16[2,2,32,256]{3,2,1,0:T(8,128)(2,1)S(1)}, bf16[2,2,32,256]{3,2,1,0:T(8,128)(2,1)S(1)}, u32[]{:S(2)}, u32[]{:S(2)}) collective-permute-start(bf16[2,2,32,256]{3,2,1,0:T(8,128)(2,1)S(1)} %get-tuple-element.30), channel_id=1, source_target_pairs={{0,26},{1,3},{2,24},{3,1},{8,18},{9,11},{10,16},{11,9},{16,10},{17... | collective-permute-start | bytes 196616 | tf_op jit(solution)/shard_map/ppermute | solution.py:222
  11.6 8.7 %collective-permute-start.6 = (bf16[2,2,32,256]{3,2,1,0:T(8,128)(2,1)S(1)}, bf16[2,2,32,256]{3,2,1,0:T(8,128)(2,1)S(1)}, u32[]{:S(2)}, u32[]{:S(2)}) collective-permute-start(bf16[2,2,32,256]{3,2,1,0:T(8,128)(2,1)S(1)} %get-tuple-element.31), channel_id=1, source_target_pairs={{0,24},{1,11},{2,26},{3,9},{8,16},{9,3},{10,18},{11,1},{16,8},{17,... | collective-permute-start | bytes 196616 | tf_op jit(solution)/shard_map/ppermute | solution.py:222
  14.1 6.2 %collective-permute-start.7 = (bf16[2,2,32,256]{3,2,1,0:T(8,128)(2,1)S(1)}, bf16[2,2,32,256]{3,2,1,0:T(8,128)(2,1)S(1)}, u32[]{:S(2)}, u32[]{:S(2)}) collective-permute-start(bf16[2,2,32,256]{3,2,1,0:T(8,128)(2,1)S(1)} %get-tuple-element.32), channel_id=1, source_target_pairs={{0,16},{1,19},{2,18},{3,17},{8,24},{9,27},{10,26},{11,25},{16,0},{... | collective-permute-start | bytes 196616 | tf_op jit(solution)/shard_map/ppermute | solution.py:222
  14.6 5.7 %collective-permute-start.8 = (bf16[2,2,32,256]{3,2,1,0:T(8,128)(2,1)S(1)}, bf16[2,2,32,256]{3,2,1,0:T(8,128)(2,1)S(1)}, u32[]{:S(2)}, u32[]{:S(2)}) collective-permute-start(bf16[2,2,32,256]{3,2,1,0:T(8,128)(2,1)S(1)} %get-tuple-element.33), channel_id=1, source_target_pairs={{0,8},{1,27},{2,10},{3,25},{8,0},{9,19},{10,2},{11,17},{16,24},{17... | collective-permute-start | bytes 196616 | tf_op jit(solution)/shard_map/ppermute | solution.py:222
  19.3 1.2 %collective-permute-start.3 = (bf16[2,32,256]{2,1,0:T(8,128)(2,1)S(1)}, bf16[2,32,256]{2,1,0:T(8,128)(2,1)S(1)}, u32[]{:S(2)}, u32[]{:S(2)}) collective-permute-start(bf16[2,32,256]{2,1,0:T(8,128)(2,1)S(1)} %shard_map.84), channel_id=1, source_target_pairs={{0,4},{4,0},{1,5},{5,1},{2,6},{6,2},{3,7},{7,3},{8,12},{12,8},{9,1... | collective-permute-start | bytes 98312 | tf_op jit(solution)/shard_map/ppermute | solution.py:207
  20.9 1.4 %collective-permute-start.9 = (bf16[4,1,2,32,256]{4,3,2,1,0:T(8,128)(2,1)S(1)}, bf16[4,1,2,32,256]{4,3,2,1,0:T(8,128)(2,1)S(1)}, u32[]{:S(2)}, u32[]{:S(2)}) collective-permute-start(bf16[4,1,2,32,256]{4,3,2,1,0:T(8,128)(2,1)S(1)} %get-tuple-element.34._), channel_id=1, source_target_pairs={{0,4},{4,0},{1,5},{5,1},{2,6},{6,2},{3,7},{7,3},{8,12},{12,8},{9,1... | collective-permute-start | bytes 393224 | tf_op jit(solution)/shard_map/ppermute | solution.py:207
  21.2 8.9 %collective-permute-start.10 = (bf16[2,2,32,256]{3,2,1,0:T(8,128)(2,1)S(1)}, bf16[2,2,32,256]{3,2,1,0:T(8,128)(2,1)S(1)}, u32[]{:S(2)}, u32[]{:S(2)}) collective-permute-start(bf16[2,2,32,256]{3,2,1,0:T(8,128)(2,1)S(1)} %get-tuple-element.38), channel_id=1, source_target_pairs={{0,2},{1,25},{2,0},{3,27},{8,10},{9,17},{10,8},{11,19},{16,18},{17... | collective-permute-start | bytes 196616 | tf_op jit(solution)/shard_map/ppermute | solution.py:222
  22.4 12.0 %copy-start.1 = (bf16[256,256]{1,0:T(8,128)(2,1)S(1)}, bf16[256,256]{1,0:T(8,128)(2,1)}, u32[]{:S(2)}) copy-start(bf16[256,256]{1,0:T(8,128)(2,1)} %link.1) | copy-start | bytes 393220
  22.4 9.1 %collective-permute-start.11 = (bf16[2,2,32,256]{3,2,1,0:T(8,128)(2,1)S(1)}, bf16[2,2,32,256]{3,2,1,0:T(8,128)(2,1)S(1)}, u32[]{:S(2)}, u32[]{:S(2)}) collective-permute-start(bf16[2,2,32,256]{3,2,1,0:T(8,128)(2,1)S(1)} %get-tuple-element.39), channel_id=1, source_target_pairs={{0,10},{1,17},{2,8},{3,19},{8,2},{9,25},{10,0},{11,27},{16,26},{17... | collective-permute-start | bytes 196616 | tf_op jit(solution)/shard_map/ppermute | solution.py:222
  24.7 9.7 %collective-permute-start.13 = (bf16[2,2,32,256]{3,2,1,0:T(8,128)(2,1)S(1)}, bf16[2,2,32,256]{3,2,1,0:T(8,128)(2,1)S(1)}, u32[]{:S(2)}, u32[]{:S(2)}) collective-permute-start(bf16[2,2,32,256]{3,2,1,0:T(8,128)(2,1)S(1)} %get-tuple-element.40), channel_id=1, source_target_pairs={{0,18},{1,9},{2,16},{3,11},{8,26},{9,1},{10,24},{11,3},{16,2},{17,... | collective-permute-start | bytes 196616 | tf_op jit(solution)/shard_map/ppermute | solution.py:222
  26.0 11.0 %collective-permute-start.14 = (bf16[2,2,32,256]{3,2,1,0:T(8,128)(2,1)S(1)}, bf16[2,2,32,256]{3,2,1,0:T(8,128)(2,1)S(1)}, u32[]{:S(2)}, u32[]{:S(2)}) collective-permute-start(bf16[2,2,32,256]{3,2,1,0:T(8,128)(2,1)S(1)} %get-tuple-element.41), channel_id=1, source_target_pairs={{0,26},{1,3},{2,24},{3,1},{8,18},{9,11},{10,16},{11,9},{16,10},{17... | collective-permute-start | bytes 196616 | tf_op jit(solution)/shard_map/ppermute | solution.py:222
  28.9 8.1 %collective-permute-start.15 = (bf16[2,2,32,256]{3,2,1,0:T(8,128)(2,1)S(1)}, bf16[2,2,32,256]{3,2,1,0:T(8,128)(2,1)S(1)}, u32[]{:S(2)}, u32[]{:S(2)}) collective-permute-start(bf16[2,2,32,256]{3,2,1,0:T(8,128)(2,1)S(1)} %get-tuple-element.42), channel_id=1, source_target_pairs={{0,24},{1,11},{2,26},{3,9},{8,16},{9,3},{10,18},{11,1},{16,8},{17,... | collective-permute-start | bytes 196616 | tf_op jit(solution)/shard_map/ppermute | solution.py:222
  30.0 7.0 %collective-permute-start.16 = (bf16[2,2,32,256]{3,2,1,0:T(8,128)(2,1)S(1)}, bf16[2,2,32,256]{3,2,1,0:T(8,128)(2,1)S(1)}, u32[]{:S(2)}, u32[]{:S(2)}) collective-permute-start(bf16[2,2,32,256]{3,2,1,0:T(8,128)(2,1)S(1)} %get-tuple-element.43), channel_id=1, source_target_pairs={{0,16},{1,19},{2,18},{3,17},{8,24},{9,27},{10,26},{11,25},{16,0},{... | collective-permute-start | bytes 196616 | tf_op jit(solution)/shard_map/ppermute | solution.py:222
  31.5 3.0 %copy-start.2 = (s32[3,3]{1,0:T(4,128)S(1)}, s32[3,3]{1,0:T(4,128)}, u32[]{:S(2)}) copy-start(s32[3,3]{1,0:T(4,128)} %mask.1) | copy-start | bytes 112
  31.5 3.0 %copy-start.3 = (s32[1,2]{1,0:T(1,128)S(1)}, s32[1,2]{1,0:T(1,128)}, u32[]{:S(2)}) copy-start(s32[1,2]{1,0:T(1,128)} %blocks.1) | copy-start | bytes 28
  31.5 3.0 %copy-start.4 = (f32[3]{0:T(128)S(1)}, f32[3]{0:T(128)}, u32[]{:S(2)}) copy-start(f32[3]{0:T(128)} %onsite_scale.1) | copy-start | bytes 40
  31.5 3.0 %copy-start.5 = (f32[2]{0:T(128)S(1)}, f32[2]{0:T(128)}, u32[]{:S(2)}) copy-start(f32[2]{0:T(128)} %coupling_scale.1) | copy-start | bytes 28
  31.5 5.5 %collective-permute-start.17 = (bf16[2,2,32,256]{3,2,1,0:T(8,128)(2,1)S(1)}, bf16[2,2,32,256]{3,2,1,0:T(8,128)(2,1)S(1)}, u32[]{:S(2)}, u32[]{:S(2)}) collective-permute-start(bf16[2,2,32,256]{3,2,1,0:T(8,128)(2,1)S(1)} %get-tuple-element.44), channel_id=1, source_target_pairs={{0,8},{1,27},{2,10},{3,25},{8,0},{9,19},{10,2},{11,17},{16,24},{17... | collective-permute-start | bytes 196616 | tf_op jit(solution)/shard_map/ppermute | solution.py:222
  32.5 4.5 %copy-start = (bf16[256,256]{1,0:T(8,128)(2,1)S(1)}, bf16[256,256]{1,0:T(8,128)(2,1)}, u32[]{:S(2)}) copy-start(bf16[256,256]{1,0:T(8,128)(2,1)} %onsite.1) | copy-start | bytes 393220
  34.4 2.6 %collective-permute-start.12 = (bf16[2,32,256]{2,1,0:T(8,128)(2,1)S(1)}, bf16[2,32,256]{2,1,0:T(8,128)(2,1)S(1)}, u32[]{:S(2)}, u32[]{:S(2)}) collective-permute-start(bf16[2,32,256]{2,1,0:T(8,128)(2,1)S(1)} %shard_map.88), channel_id=1, source_target_pairs={{0,4},{4,0},{1,5},{5,1},{2,6},{6,2},{3,7},{7,3},{8,12},{12,8},{9,1... | collective-permute-start | bytes 98312 | tf_op jit(solution)/shard_map/ppermute | solution.py:207

commit v5 on v4

--- a/solution.py
+++ b/solution.py
@@ -31,21 +31,23 @@
     return pl.ds(pl.multiple_of(first * rows, rows), rows)
 
 
-def order_of(chips, second):
+def order_of(chips, second, phase):
     plane = [(0, step) for step in reversed(range(1, chips))]
     cross = [(1, step) for step in range(chips)]
-    return plane + cross if second else cross + plane
+    if second:
+        return plane[:-1] + cross[:1] + plane[-1:] + cross[1:]
+    return cross + plane
 
 
 def in_second():
     return 2 * lax.axis_index("low") >= lax.axis_size("low")
 
 
-def turn_of(chips, turn):
+def turn_of(chips, turn, phase):
     second = in_second()
     return [
         jnp.where(second, late, soon)
-        for soon, late in zip(order_of(chips, False)[turn], order_of(chips, True)[turn])
+        for soon, late in zip(order_of(chips, False, phase)[turn], order_of(chips, True, phase)[turn])
     ]
 
 
@@ -65,7 +67,7 @@
             if kind == 0:
                 whole = whole.astype(F32).T.astype(BF16)
             turned[kind, part] = whole
-    crosses, step = turn_of(chips, 0)
+    crosses, step = turn_of(chips, 0, 0)
     for owner in range(2):
         first[owner] = turned[crosses, :, rows_of(2 * (chip ^ step) + owner, rows)]
     for kind in range(2):
@@ -75,10 +77,10 @@
             keep[place, kind] = turned[kind, :, rows_of(top + core, rows)]
 
 
-def pair_body(keep, got, *blocks):
+def pair_body(phase, keep, got, *blocks):
     chips, kinds = keep.shape[:2]
     for turn, block in enumerate(blocks, 1):
-        crosses, step = turn_of(chips, turn)
+        crosses, step = turn_of(chips, turn, phase)
         kind = crosses if kinds == 2 else 0
         block[0] = keep[step, kind]
         block[1] = got[step, kind]
@@ -88,10 +90,10 @@
     away[...] = came[1 - lax.axis_index("core")]
 
 
-def sort_blocks(chips, blocks, late, put):
+def sort_blocks(chips, phase, blocks, late, put):
     core = lax.axis_index("core")
     for turn, block in enumerate(blocks):
-        crosses, step = turn_of(chips, turn)
+        crosses, step = turn_of(chips, turn, phase)
         if turn == 0:
             put(crosses, step, block[core], late[...])
         else:
@@ -109,7 +111,7 @@
         joined[2 * (chip ^ step) + 1 - core, crosses] = theirs
 
     put(0, 0, keep[0, 0], got[0, 0])
-    sort_blocks(chips, blocks, late, put)
+    sort_blocks(chips, 0, blocks, late, put)
     factor = energies ** (-0.5)
     for top in range(0, rows, 16):
         for left in range(0, width, 128):
@@ -125,7 +127,7 @@
                     imag += lr * mi + li * mr
                 polar[(lag, 0) + at] = (factor * imag).astype(BF16)
                 polar[(lag, 1) + at] = (-factor * real).astype(BF16)
-    _, step = turn_of(chips, 0)
+    _, step = turn_of(chips, 0, 1)
     for owner in range(2):
         first[owner] = polar[2 * (chip ^ step) + owner]
     for place in range(chips):
@@ -162,20 +164,25 @@
     blocks = refs[:-4]
     out, whole, ready, sems = refs[-4:]
     chip, core = lax.axis_index("chip"), lax.axis_index("core")
-    chips, _, _, rows, _ = keep.shape
+    chips, _, _, rows, width = keep.shape
 
     def put(slot, step, mine, theirs):
         whole[slot, :, rows_of(2 * (chip ^ step) + core, rows)] = mine
         whole[slot, :, rows_of(2 * (chip ^ step) + 1 - core, rows)] = theirs
 
     put(0, 0, keep[0, 0], got[0, 0])
-    sort_blocks(chips, blocks, late, put)
+    sort_blocks(chips, 1, blocks, late, put)
     copies = []
+    inner_own = across(onsite[...], whole[0].reshape(2 * width, width))
+    inner_other = across(coupling[...], whole[1].reshape(2 * width, width))
     for part in range(2):
-        inner = across(onsite[...], whole[0, part])
-        term = weights[0, 0, 0] * jnp.dot(inner, onsite[...], preferred_element_type=F32)
-        inner = across(coupling[...], whole[1, part])
-        mirrored = weights[1, 0, 0] * jnp.dot(inner, coupling[...], preferred_element_type=F32)
+        at = slice(part * width, (part + 1) * width)
+        term = weights[0, 0, 0] * jnp.dot(
+            inner_own[:, at], onsite[...], preferred_element_type=F32
+        )
+        mirrored = weights[1, 0, 0] * jnp.dot(
+            inner_other[:, at], coupling[...], preferred_element_type=F32
+        )
         ready[part, 0] = (term + mirrored.astype(BF16).astype(F32)).astype(BF16)
         copies.append(pltpu.make_async_copy(ready.at[part], out.at[part], sems.at[part]))
         copies[-1].start()
@@ -206,16 +213,18 @@
     def swap_cores(value):
         return lax.ppermute(value, "core", [(0, 1), (1, 0)])
 
-    def spread(first, away, keep):
+    def spread(first, away, keep, phase):
         got = swap_cores(away)
-        later = run_kernel(pair_body, [block_shape] * (2 * chips - 2), (keep, got))
+        later = run_kernel(
+            functools.partial(pair_body, phase), [block_shape] * (2 * chips - 2), (keep, got)
+        )
         came = []
         for turn, block in enumerate((first, *later)):
             pairs = []
             for chip in range(chips):
                 for half in range(2):
                     for low in range(lows):
-                        crosses, step = order_of(chips, 2 * low >= lows)[turn]
+                        crosses, step = order_of(chips, 2 * low >= lows, phase)[turn]
                         source = (chip * 2 + half) * lows + low
                         target = ((chip ^ step) * 2 + (half ^ crosses)) * lows + low
                         pairs.append((source, target))
@@ -237,14 +246,14 @@
     first, away, keep = run_kernel(
         lag_body,
         [block_shape] + [piles(1)] * 2,
-        spread(first, away, keep),
+        spread(first, away, keep, 0),
         scratch=[
             pltpu.VMEM((energies, 2, 2, rows, width), BF16),
             pltpu.VMEM((energies, 2, rows, width), BF16),
         ],
         flops=energies * (energies + 1) * 4 * rows * width,
     )
-    parts = spread(first, away, keep)
+    parts = spread(first, away, keep, 1)
     coupling, weights = run_kernel(
         weigh_body,
         [((width, width), BF16), ((2, 8, 128), F32)],

time: 38.6 us -> 37.4 us (0.969)
  waiting for transfers between devices: 10.3 us -> 9.4 us
    ppermute x14, waiting for transfers between devices: 8.93 us -> 8.06 us  [spread(): came.append(lax.ppermute(block, ('chip', 'half', 'low'), pairs))]
  transfers between devices with their start and end apart: 18 -> 18, of which waited for: 6 -> 8; matrix products, arithmetic and copies ran while one was open for 0% -> 0% of each run, Pallas kernels for 2% -> 2%
where the time goes in v5:
time: 37.4 us; the launch traced here: 37.3 us
  starting transfers between devices  24.2 us (65%)
  waiting for transfers between devices  9.4 us (25%)
  Pallas kernels  3.53 us (9%)
    ppermute x14, starting transfers between devices, spread(): came.append(lax.ppermute(block, ('chip', 'half', 'low'), pairs))  23.5 us
    ppermute x14, waiting for transfers between devices, spread(): came.append(lax.ppermute(block, ('chip', 'half', 'low'), pairs))  8.06 us
    pallas_call x8, Pallas kernels, run_kernel(): pl.pallas_call(body, out_shape=[jax.ShapeDtypeStruct(shape, dtype) for sh...  3.53 us
    ppermute x4, waiting for transfers between devices, swap_cores(): return lax.ppermute(value, 'core', [(0, 1), (1, 0)])  1.34 us
    ppermute x4, starting transfers between devices, swap_cores(): return lax.ppermute(value, 'core', [(0, 1), (1, 0)])  0.75 us
  transfers between devices with their start and end apart: 18, of which 8 were waited for; matrix products, arithmetic and copies ran while one was open for 0% of the time, Pallas kernels for 2%

profile of v5, /device:TPU:0, one launch (start us, length us, event | category | flops | bytes accessed | tf_op | source)
XLA Modules:
  0.0 37.3 jit_solution(15056798830112430834)
XLA Ops:
  0.0 1.2 %shard_map.82 = (bf16[2,2,32,256]{3,2,1,0:T(8,128)(2,1)S(1)}, bf16[4,2,2,32,256]{4,3,2,1,0:T(8,128)(2,1)S(1)}, bf16[4,2,2,32,256]{4,3,2,1,0:T(8,128)(2,1)S(1)}) custom-call(bf16[2,1,256,256]{3,2,1,0:T(8,128)(2,1)} %less.1, bf16[2,1,256,256]{3,2,1,0:T(8,128)(2,1)} %more.1), custom_call_target="tpu_custom_call" | custom-call | bytes 524288 | tf_op jit(solution)/shard_map/pallas_call | solution.py:19
  1.2 0.5 %collective-permute-start = (bf16[4,2,2,32,256]{4,3,2,1,0:T(8,128)(2,1)S(1)}, bf16[4,2,2,32,256]{4,3,2,1,0:T(8,128)(2,1)S(1)}, u32[]{:S(2)}, u32[]{:S(2)}) collective-permute-start(bf16[4,2,2,32,256]{4,3,2,1,0:T(8,128)(2,1)S(1)} %get-tuple-element.26), channel_id=1, source_target_pairs={{0,4},{4,0},{1,5},{5,1},{2,6},{6,2},{3,7},{7,3},{8,12},{12,8},{9,1... | collective-permute-start | bytes 786440 | tf_op jit(solution)/shard_map/ppermute | solution.py:214
  1.7 3.7 %collective-permute-start.1 = (bf16[2,2,32,256]{3,2,1,0:T(8,128)(2,1)S(1)}, bf16[2,2,32,256]{3,2,1,0:T(8,128)(2,1)S(1)}, u32[]{:S(2)}, u32[]{:S(2)}) collective-permute-start(bf16[2,2,32,256]{3,2,1,0:T(8,128)(2,1)S(1)} %get-tuple-element.27), channel_id=1, source_target_pairs={{0,2},{1,25},{2,0},{3,27},{8,10},{9,17},{10,8},{11,19},{16,18},{17... | collective-permute-start | bytes 196616 | tf_op jit(solution)/shard_map/ppermute | solution.py:231
  5.4 2.4 %collective-permute-start.2 = (bf16[2,2,32,256]{3,2,1,0:T(8,128)(2,1)S(1)}, bf16[2,2,32,256]{3,2,1,0:T(8,128)(2,1)S(1)}, u32[]{:S(2)}, u32[]{:S(2)}) collective-permute-start(bf16[2,2,32,256]{3,2,1,0:T(8,128)(2,1)S(1)} %get-tuple-element.28), channel_id=1, source_target_pairs={{0,10},{1,17},{2,8},{3,19},{8,2},{9,25},{10,0},{11,27},{16,26},{17... | collective-permute-start | bytes 196616 | tf_op jit(solution)/shard_map/ppermute | solution.py:231
  7.8 2.4 %collective-permute-start.4 = (bf16[2,2,32,256]{3,2,1,0:T(8,128)(2,1)S(1)}, bf16[2,2,32,256]{3,2,1,0:T(8,128)(2,1)S(1)}, u32[]{:S(2)}, u32[]{:S(2)}) collective-permute-start(bf16[2,2,32,256]{3,2,1,0:T(8,128)(2,1)S(1)} %get-tuple-element.29), channel_id=1, source_target_pairs={{0,18},{1,3},{2,16},{3,1},{8,26},{9,11},{10,24},{11,9},{16,2},{17,... | collective-permute-start | bytes 196616 | tf_op jit(solution)/shard_map/ppermute | solution.py:231
  10.3 1.4 %collective-permute-start.5 = (bf16[2,2,32,256]{3,2,1,0:T(8,128)(2,1)S(1)}, bf16[2,2,32,256]{3,2,1,0:T(8,128)(2,1)S(1)}, u32[]{:S(2)}, u32[]{:S(2)}) collective-permute-start(bf16[2,2,32,256]{3,2,1,0:T(8,128)(2,1)S(1)} %get-tuple-element.30), channel_id=1, source_target_pairs={{0,26},{1,9},{2,24},{3,11},{8,18},{9,1},{10,16},{11,3},{16,10},{17... | collective-permute-start | bytes 196616 | tf_op jit(solution)/shard_map/ppermute | solution.py:231
  11.6 2.4 %collective-permute-start.6 = (bf16[2,2,32,256]{3,2,1,0:T(8,128)(2,1)S(1)}, bf16[2,2,32,256]{3,2,1,0:T(8,128)(2,1)S(1)}, u32[]{:S(2)}, u32[]{:S(2)}) collective-permute-start(bf16[2,2,32,256]{3,2,1,0:T(8,128)(2,1)S(1)} %get-tuple-element.31), channel_id=1, source_target_pairs={{0,24},{1,11},{2,26},{3,9},{8,16},{9,3},{10,18},{11,1},{16,8},{17,... | collective-permute-start | bytes 196616 | tf_op jit(solution)/shard_map/ppermute | solution.py:231
  14.1 0.5 %collective-permute-start.7 = (bf16[2,2,32,256]{3,2,1,0:T(8,128)(2,1)S(1)}, bf16[2,2,32,256]{3,2,1,0:T(8,128)(2,1)S(1)}, u32[]{:S(2)}, u32[]{:S(2)}) collective-permute-start(bf16[2,2,32,256]{3,2,1,0:T(8,128)(2,1)S(1)} %get-tuple-element.32), channel_id=1, source_target_pairs={{0,16},{1,19},{2,18},{3,17},{8,24},{9,27},{10,26},{11,25},{16,0},{... | collective-permute-start | bytes 196616 | tf_op jit(solution)/shard_map/ppermute | solution.py:231
  14.6 0.5 %collective-permute-start.8 = (bf16[2,2,32,256]{3,2,1,0:T(8,128)(2,1)S(1)}, bf16[2,2,32,256]{3,2,1,0:T(8,128)(2,1)S(1)}, u32[]{:S(2)}, u32[]{:S(2)}) collective-permute-start(bf16[2,2,32,256]{3,2,1,0:T(8,128)(2,1)S(1)} %get-tuple-element.33), channel_id=1, source_target_pairs={{0,8},{1,27},{2,10},{3,25},{8,0},{9,19},{10,2},{11,17},{16,24},{17... | collective-permute-start | bytes 196616 | tf_op jit(solution)/shard_map/ppermute | solution.py:231
  15.1 4.0 %collective-permute-done.4.refs_2_ = bf16[2,2,32,256]{3,2,1,0:T(8,128)(2,1)S(1)} collective-permute-done((bf16[2,2,32,256]{3,2,1,0:T(8,128)(2,1)S(1)}, bf16[2,2,32,256]{3,2,1,0:T(8,128)(2,1)S(1)}, u32[]{:S(2)}, u32[]{:S(2)}) %collective-permute-start.4) | collective-permute-done | bytes 65568 | tf_op jit(solution)/shard_map/ppermute | solution.py:231
  19.2 1.0 %collective-permute-done.5.refs_3_ = bf16[2,2,32,256]{3,2,1,0:T(8,128)(2,1)S(1)} collective-permute-done((bf16[2,2,32,256]{3,2,1,0:T(8,128)(2,1)S(1)}, bf16[2,2,32,256]{3,2,1,0:T(8,128)(2,1)S(1)}, u32[]{:S(2)}, u32[]{:S(2)}) %collective-permute-start.5) | collective-permute-done | bytes 65568 | tf_op jit(solution)/shard_map/ppermute | solution.py:231
  20.4 0.5 %shard_map.85 = (bf16[2,2,32,256]{3,2,1,0:T(8,128)(2,1)S(1)}, bf16[4,1,2,32,256]{4,3,2,1,0:T(8,128)(2,1)S(1)}, bf16[4,1,2,32,256]{4,3,2,1,0:T(8,128)(2,1)S(1)}) custom-call(bf16[4,2,2,32,256]{4,3,2,1,0:T(8,128)(2,1)S(1)} %get-tuple-element.25.keep, bf16[4,2,2,32,256]{4,3,2,1,0:T(8,128)(2,1)S(1)} %collective-permute-done.got, ...), custom_call_target="tpu_custom_call" | custom-call | flops 2359296 | bytes 524288 | tf_op jit(solution)/shard_map/pallas_call | solution.py:19
  21.1 1.2 %collective-permute-done.9.got = bf16[4,1,2,32,256]{4,3,2,1,0:T(8,128)(2,1)S(1)} collective-permute-done((bf16[4,1,2,32,256]{4,3,2,1,0:T(8,128)(2,1)S(1)}, bf16[4,1,2,32,256]{4,3,2,1,0:T(8,128)(2,1)S(1)}, u32[]{:S(2)}, u32[]{:S(2)}) %collective-permute-start.9) | collective-permute-done | bytes 131104 | tf_op jit(solution)/shard_map/ppermute | solution.py:214
  22.3 2.5 %collective-permute-start.11 = (bf16[2,2,32,256]{3,2,1,0:T(8,128)(2,1)S(1)}, bf16[2,2,32,256]{3,2,1,0:T(8,128)(2,1)S(1)}, u32[]{:S(2)}, u32[]{:S(2)}) collective-permute-start(bf16[2,2,32,256]{3,2,1,0:T(8,128)(2,1)S(1)} %get-tuple-element.39), channel_id=1, source_target_pairs={{0,10},{1,17},{2,8},{3,19},{8,2},{9,25},{10,0},{11,27},{16,26},{17... | collective-permute-start | bytes 196616 | tf_op jit(solution)/shard_map/ppermute | solution.py:231
  24.8 1.1 %collective-permute-start.13 = (bf16[2,2,32,256]{3,2,1,0:T(8,128)(2,1)S(1)}, bf16[2,2,32,256]{3,2,1,0:T(8,128)(2,1)S(1)}, u32[]{:S(2)}, u32[]{:S(2)}) collective-permute-start(bf16[2,2,32,256]{3,2,1,0:T(8,128)(2,1)S(1)} %get-tuple-element.40), channel_id=1, source_target_pairs={{0,18},{1,3},{2,16},{3,1},{8,26},{9,11},{10,24},{11,9},{16,2},{17,... | collective-permute-start | bytes 196616 | tf_op jit(solution)/shard_map/ppermute | solution.py:231
  25.9 2.9 %collective-permute-start.14 = (bf16[2,2,32,256]{3,2,1,0:T(8,128)(2,1)S(1)}, bf16[2,2,32,256]{3,2,1,0:T(8,128)(2,1)S(1)}, u32[]{:S(2)}, u32[]{:S(2)}) collective-permute-start(bf16[2,2,32,256]{3,2,1,0:T(8,128)(2,1)S(1)} %get-tuple-element.41), channel_id=1, source_target_pairs={{0,26},{1,9},{2,24},{3,11},{8,18},{9,1},{10,16},{11,3},{16,10},{17... | collective-permute-start | bytes 196616 | tf_op jit(solution)/shard_map/ppermute | solution.py:231
  28.8 1.1 %collective-permute-start.15 = (bf16[2,2,32,256]{3,2,1,0:T(8,128)(2,1)S(1)}, bf16[2,2,32,256]{3,2,1,0:T(8,128)(2,1)S(1)}, u32[]{:S(2)}, u32[]{:S(2)}) collective-permute-start(bf16[2,2,32,256]{3,2,1,0:T(8,128)(2,1)S(1)} %get-tuple-element.42), channel_id=1, source_target_pairs={{0,24},{1,11},{2,26},{3,9},{8,16},{9,3},{10,18},{11,1},{16,8},{17,... | collective-permute-start | bytes 196616 | tf_op jit(solution)/shard_map/ppermute | solution.py:231
  29.9 1.6 %collective-permute-start.16 = (bf16[2,2,32,256]{3,2,1,0:T(8,128)(2,1)S(1)}, bf16[2,2,32,256]{3,2,1,0:T(8,128)(2,1)S(1)}, u32[]{:S(2)}, u32[]{:S(2)}) collective-permute-start(bf16[2,2,32,256]{3,2,1,0:T(8,128)(2,1)S(1)} %get-tuple-element.43), channel_id=1, source_target_pairs={{0,16},{1,19},{2,18},{3,17},{8,24},{9,27},{10,26},{11,25},{16,0},{... | collective-permute-start | bytes 196616 | tf_op jit(solution)/shard_map/ppermute | solution.py:231
  31.6 0.8 %collective-permute-start.17 = (bf16[2,2,32,256]{3,2,1,0:T(8,128)(2,1)S(1)}, bf16[2,2,32,256]{3,2,1,0:T(8,128)(2,1)S(1)}, u32[]{:S(2)}, u32[]{:S(2)}) collective-permute-start(bf16[2,2,32,256]{3,2,1,0:T(8,128)(2,1)S(1)} %get-tuple-element.44), channel_id=1, source_target_pairs={{0,8},{1,27},{2,10},{3,25},{8,0},{9,19},{10,2},{11,17},{16,24},{17... | collective-permute-start | bytes 196616 | tf_op jit(solution)/shard_map/ppermute | solution.py:231
  32.4 1.7 %collective-permute-done.13.refs_2_ = bf16[2,2,32,256]{3,2,1,0:T(8,128)(2,1)S(1)} collective-permute-done((bf16[2,2,32,256]{3,2,1,0:T(8,128)(2,1)S(1)}, bf16[2,2,32,256]{3,2,1,0:T(8,128)(2,1)S(1)}, u32[]{:S(2)}, u32[]{:S(2)}) %collective-permute-start.13) | collective-permute-done | bytes 65568 | tf_op jit(solution)/shard_map/ppermute | solution.py:231
  34.1 0.6 %shard_map.86 = (bf16[256,256]{1,0:T(8,128)(2,1)S(1)}, f32[2,8,128]{2,1,0:T(8,128)S(1)}) custom-call(s32[1,2]{1,0:T(1,128)S(1)} %copy-done.3, f32[3]{0:T(128)S(1)} %copy-done.4, f32[2]{0:T(128)S(1)} %copy-done.5, s32[3,3]{1,0:T(4,128)S(1)} %copy-done.2, bf16[256,256]{1,0:T(8,128)(2,1)S(1)} %copy-done.1, bf16[4,1,2,32,256]{4,3,2,1,0:T(8,128)(2,1)S(1)} %get-tuple-element.34._), custom_call_target="tpu_custom_call" | custom-call | bytes 524288 | tf_op jit(solution)/shard_map/pallas_call | solution.py:19
  34.7 0.3 collective-permute-done.14.refs_3_
  35.1 0.9 %collective-permute-done.16.refs_5_ = bf16[2,2,32,256]{3,2,1,0:T(8,128)(2,1)S(1)} collective-permute-done((bf16[2,2,32,256]{3,2,1,0:T(8,128)(2,1)S(1)}, bf16[2,2,32,256]{3,2,1,0:T(8,128)(2,1)S(1)}, u32[]{:S(2)}, u32[]{:S(2)}) %collective-permute-start.16) | collective-permute-done | bytes 65568 | tf_op jit(solution)/shard_map/ppermute | solution.py:231
  36.0 1.3 %shard_map.89 = bf16[2,1,256,256]{3,2,1,0:T(8,128)(2,1)} custom-call(bf16[256,256]{1,0:T(8,128)(2,1)S(1)} %copy-done, bf16[256,256]{1,0:T(8,128)(2,1)S(1)} %get-tuple-element.35.coupling, f32[2,8,128]{2,1,0:T(8,128)S(1)} %get-tuple-element.36.weights, bf16[4,1,2,32,256]{4,3,2,1,0:T(8,128)(2,1)S(1)} %get-tuple-element.37.keep, ...), custom_call_target="tpu_custom_call" | custom-call | flops 268435456 | bytes 524288 | tf_op jit(solution)/shard_map/pallas_call | solution.py:19
  (32 shorter events, 0.6 us)
Async XLA Ops:
  1.2 4.2 %collective-permute-start = (bf16[4,2,2,32,256]{4,3,2,1,0:T(8,128)(2,1)S(1)}, bf16[4,2,2,32,256]{4,3,2,1,0:T(8,128)(2,1)S(1)}, u32[]{:S(2)}, u32[]{:S(2)}) collective-permute-start(bf16[4,2,2,32,256]{4,3,2,1,0:T(8,128)(2,1)S(1)} %get-tuple-element.26), channel_id=1, source_target_pairs={{0,4},{4,0},{1,5},{5,1},{2,6},{6,2},{3,7},{7,3},{8,12},{12,8},{9,1... | collective-permute-start | bytes 786440 | tf_op jit(solution)/shard_map/ppermute | solution.py:214
  1.7 12.4 %collective-permute-start.1 = (bf16[2,2,32,256]{3,2,1,0:T(8,128)(2,1)S(1)}, bf16[2,2,32,256]{3,2,1,0:T(8,128)(2,1)S(1)}, u32[]{:S(2)}, u32[]{:S(2)}) collective-permute-start(bf16[2,2,32,256]{3,2,1,0:T(8,128)(2,1)S(1)} %get-tuple-element.27), channel_id=1, source_target_pairs={{0,2},{1,25},{2,0},{3,27},{8,10},{9,17},{10,8},{11,19},{16,18},{17... | collective-permute-start | bytes 196616 | tf_op jit(solution)/shard_map/ppermute | solution.py:231
  5.4 9.2 %collective-permute-start.2 = (bf16[2,2,32,256]{3,2,1,0:T(8,128)(2,1)S(1)}, bf16[2,2,32,256]{3,2,1,0:T(8,128)(2,1)S(1)}, u32[]{:S(2)}, u32[]{:S(2)}) collective-permute-start(bf16[2,2,32,256]{3,2,1,0:T(8,128)(2,1)S(1)} %get-tuple-element.28), channel_id=1, source_target_pairs={{0,10},{1,17},{2,8},{3,19},{8,2},{9,25},{10,0},{11,27},{16,26},{17... | collective-permute-start | bytes 196616 | tf_op jit(solution)/shard_map/ppermute | solution.py:231
  7.8 11.3 %collective-permute-start.4 = (bf16[2,2,32,256]{3,2,1,0:T(8,128)(2,1)S(1)}, bf16[2,2,32,256]{3,2,1,0:T(8,128)(2,1)S(1)}, u32[]{:S(2)}, u32[]{:S(2)}) collective-permute-start(bf16[2,2,32,256]{3,2,1,0:T(8,128)(2,1)S(1)} %get-tuple-element.29), channel_id=1, source_target_pairs={{0,18},{1,3},{2,16},{3,1},{8,26},{9,11},{10,24},{11,9},{16,2},{17,... | collective-permute-start | bytes 196616 | tf_op jit(solution)/shard_map/ppermute | solution.py:231
  10.3 9.9 %collective-permute-start.5 = (bf16[2,2,32,256]{3,2,1,0:T(8,128)(2,1)S(1)}, bf16[2,2,32,256]{3,2,1,0:T(8,128)(2,1)S(1)}, u32[]{:S(2)}, u32[]{:S(2)}) collective-permute-start(bf16[2,2,32,256]{3,2,1,0:T(8,128)(2,1)S(1)} %get-tuple-element.30), channel_id=1, source_target_pairs={{0,26},{1,9},{2,24},{3,11},{8,18},{9,1},{10,16},{11,3},{16,10},{17... | collective-permute-start | bytes 196616 | tf_op jit(solution)/shard_map/ppermute | solution.py:231
  11.6 8.6 %collective-permute-start.6 = (bf16[2,2,32,256]{3,2,1,0:T(8,128)(2,1)S(1)}, bf16[2,2,32,256]{3,2,1,0:T(8,128)(2,1)S(1)}, u32[]{:S(2)}, u32[]{:S(2)}) collective-permute-start(bf16[2,2,32,256]{3,2,1,0:T(8,128)(2,1)S(1)} %get-tuple-element.31), channel_id=1, source_target_pairs={{0,24},{1,11},{2,26},{3,9},{8,16},{9,3},{10,18},{11,1},{16,8},{17,... | collective-permute-start | bytes 196616 | tf_op jit(solution)/shard_map/ppermute | solution.py:231
  14.1 6.1 %collective-permute-start.7 = (bf16[2,2,32,256]{3,2,1,0:T(8,128)(2,1)S(1)}, bf16[2,2,32,256]{3,2,1,0:T(8,128)(2,1)S(1)}, u32[]{:S(2)}, u32[]{:S(2)}) collective-permute-start(bf16[2,2,32,256]{3,2,1,0:T(8,128)(2,1)S(1)} %get-tuple-element.32), channel_id=1, source_target_pairs={{0,16},{1,19},{2,18},{3,17},{8,24},{9,27},{10,26},{11,25},{16,0},{... | collective-permute-start | bytes 196616 | tf_op jit(solution)/shard_map/ppermute | solution.py:231
  14.6 5.6 %collective-permute-start.8 = (bf16[2,2,32,256]{3,2,1,0:T(8,128)(2,1)S(1)}, bf16[2,2,32,256]{3,2,1,0:T(8,128)(2,1)S(1)}, u32[]{:S(2)}, u32[]{:S(2)}) collective-permute-start(bf16[2,2,32,256]{3,2,1,0:T(8,128)(2,1)S(1)} %get-tuple-element.33), channel_id=1, source_target_pairs={{0,8},{1,27},{2,10},{3,25},{8,0},{9,19},{10,2},{11,17},{16,24},{17... | collective-permute-start | bytes 196616 | tf_op jit(solution)/shard_map/ppermute | solution.py:231
  19.2 1.2 %collective-permute-start.3 = (bf16[2,32,256]{2,1,0:T(8,128)(2,1)S(1)}, bf16[2,32,256]{2,1,0:T(8,128)(2,1)S(1)}, u32[]{:S(2)}, u32[]{:S(2)}) collective-permute-start(bf16[2,32,256]{2,1,0:T(8,128)(2,1)S(1)} %shard_map.84), channel_id=1, source_target_pairs={{0,4},{4,0},{1,5},{5,1},{2,6},{6,2},{3,7},{7,3},{8,12},{12,8},{9,1... | collective-permute-start | bytes 98312 | tf_op jit(solution)/shard_map/ppermute | solution.py:214
  20.8 1.4 %collective-permute-start.9 = (bf16[4,1,2,32,256]{4,3,2,1,0:T(8,128)(2,1)S(1)}, bf16[4,1,2,32,256]{4,3,2,1,0:T(8,128)(2,1)S(1)}, u32[]{:S(2)}, u32[]{:S(2)}) collective-permute-start(bf16[4,1,2,32,256]{4,3,2,1,0:T(8,128)(2,1)S(1)} %get-tuple-element.34._), channel_id=1, source_target_pairs={{0,4},{4,0},{1,5},{5,1},{2,6},{6,2},{3,7},{7,3},{8,12},{12,8},{9,1... | collective-permute-start | bytes 393224 | tf_op jit(solution)/shard_map/ppermute | solution.py:214
  21.0 8.9 %collective-permute-start.10 = (bf16[2,2,32,256]{3,2,1,0:T(8,128)(2,1)S(1)}, bf16[2,2,32,256]{3,2,1,0:T(8,128)(2,1)S(1)}, u32[]{:S(2)}, u32[]{:S(2)}) collective-permute-start(bf16[2,2,32,256]{3,2,1,0:T(8,128)(2,1)S(1)} %get-tuple-element.38), channel_id=1, source_target_pairs={{0,2},{1,25},{2,0},{3,27},{8,10},{9,17},{10,8},{11,19},{16,18},{17... | collective-permute-start | bytes 196616 | tf_op jit(solution)/shard_map/ppermute | solution.py:231
  22.3 11.8 %copy-start.1 = (bf16[256,256]{1,0:T(8,128)(2,1)S(1)}, bf16[256,256]{1,0:T(8,128)(2,1)}, u32[]{:S(2)}) copy-start(bf16[256,256]{1,0:T(8,128)(2,1)} %link.1) | copy-start | bytes 393220
  22.3 9.3 %collective-permute-start.11 = (bf16[2,2,32,256]{3,2,1,0:T(8,128)(2,1)S(1)}, bf16[2,2,32,256]{3,2,1,0:T(8,128)(2,1)S(1)}, u32[]{:S(2)}, u32[]{:S(2)}) collective-permute-start(bf16[2,2,32,256]{3,2,1,0:T(8,128)(2,1)S(1)} %get-tuple-element.39), channel_id=1, source_target_pairs={{0,10},{1,17},{2,8},{3,19},{8,2},{9,25},{10,0},{11,27},{16,26},{17... | collective-permute-start | bytes 196616 | tf_op jit(solution)/shard_map/ppermute | solution.py:231
  24.8 9.3 %collective-permute-start.13 = (bf16[2,2,32,256]{3,2,1,0:T(8,128)(2,1)S(1)}, bf16[2,2,32,256]{3,2,1,0:T(8,128)(2,1)S(1)}, u32[]{:S(2)}, u32[]{:S(2)}) collective-permute-start(bf16[2,2,32,256]{3,2,1,0:T(8,128)(2,1)S(1)} %get-tuple-element.40), channel_id=1, source_target_pairs={{0,18},{1,3},{2,16},{3,1},{8,26},{9,11},{10,24},{11,9},{16,2},{17,... | collective-permute-start | bytes 196616 | tf_op jit(solution)/shard_map/ppermute | solution.py:231
  25.9 9.2 %collective-permute-start.14 = (bf16[2,2,32,256]{3,2,1,0:T(8,128)(2,1)S(1)}, bf16[2,2,32,256]{3,2,1,0:T(8,128)(2,1)S(1)}, u32[]{:S(2)}, u32[]{:S(2)}) collective-permute-start(bf16[2,2,32,256]{3,2,1,0:T(8,128)(2,1)S(1)} %get-tuple-element.41), channel_id=1, source_target_pairs={{0,26},{1,9},{2,24},{3,11},{8,18},{9,1},{10,16},{11,3},{16,10},{17... | collective-permute-start | bytes 196616 | tf_op jit(solution)/shard_map/ppermute | solution.py:231
  28.8 6.3 %collective-permute-start.15 = (bf16[2,2,32,256]{3,2,1,0:T(8,128)(2,1)S(1)}, bf16[2,2,32,256]{3,2,1,0:T(8,128)(2,1)S(1)}, u32[]{:S(2)}, u32[]{:S(2)}) collective-permute-start(bf16[2,2,32,256]{3,2,1,0:T(8,128)(2,1)S(1)} %get-tuple-element.42), channel_id=1, source_target_pairs={{0,24},{1,11},{2,26},{3,9},{8,16},{9,3},{10,18},{11,1},{16,8},{17,... | collective-permute-start | bytes 196616 | tf_op jit(solution)/shard_map/ppermute | solution.py:231
  29.9 6.1 %collective-permute-start.16 = (bf16[2,2,32,256]{3,2,1,0:T(8,128)(2,1)S(1)}, bf16[2,2,32,256]{3,2,1,0:T(8,128)(2,1)S(1)}, u32[]{:S(2)}, u32[]{:S(2)}) collective-permute-start(bf16[2,2,32,256]{3,2,1,0:T(8,128)(2,1)S(1)} %get-tuple-element.43), channel_id=1, source_target_pairs={{0,16},{1,19},{2,18},{3,17},{8,24},{9,27},{10,26},{11,25},{16,0},{... | collective-permute-start | bytes 196616 | tf_op jit(solution)/shard_map/ppermute | solution.py:231
  31.5 2.5 %copy-start.2 = (s32[3,3]{1,0:T(4,128)S(1)}, s32[3,3]{1,0:T(4,128)}, u32[]{:S(2)}) copy-start(s32[3,3]{1,0:T(4,128)} %mask.1) | copy-start | bytes 112
  31.5 2.6 %copy-start.3 = (s32[1,2]{1,0:T(1,128)S(1)}, s32[1,2]{1,0:T(1,128)}, u32[]{:S(2)}) copy-start(s32[1,2]{1,0:T(1,128)} %blocks.1) | copy-start | bytes 28
  31.5 2.6 %copy-start.4 = (f32[3]{0:T(128)S(1)}, f32[3]{0:T(128)}, u32[]{:S(2)}) copy-start(f32[3]{0:T(128)} %onsite_scale.1) | copy-start | bytes 40
  31.6 2.6 %copy-start.5 = (f32[2]{0:T(128)S(1)}, f32[2]{0:T(128)}, u32[]{:S(2)}) copy-start(f32[2]{0:T(128)} %coupling_scale.1) | copy-start | bytes 28
  31.6 4.5 %collective-permute-start.17 = (bf16[2,2,32,256]{3,2,1,0:T(8,128)(2,1)S(1)}, bf16[2,2,32,256]{3,2,1,0:T(8,128)(2,1)S(1)}, u32[]{:S(2)}, u32[]{:S(2)}) collective-permute-start(bf16[2,2,32,256]{3,2,1,0:T(8,128)(2,1)S(1)} %get-tuple-element.44), channel_id=1, source_target_pairs={{0,8},{1,27},{2,10},{3,25},{8,0},{9,19},{10,2},{11,17},{16,24},{17... | collective-permute-start | bytes 196616 | tf_op jit(solution)/shard_map/ppermute | solution.py:231
  32.4 3.6 %copy-start = (bf16[256,256]{1,0:T(8,128)(2,1)S(1)}, bf16[256,256]{1,0:T(8,128)(2,1)}, u32[]{:S(2)}) copy-start(bf16[256,256]{1,0:T(8,128)(2,1)} %onsite.1) | copy-start | bytes 393220
  34.1 2.0 %collective-permute-start.12 = (bf16[2,32,256]{2,1,0:T(8,128)(2,1)S(1)}, bf16[2,32,256]{2,1,0:T(8,128)(2,1)S(1)}, u32[]{:S(2)}, u32[]{:S(2)}) collective-permute-start(bf16[2,32,256]{2,1,0:T(8,128)(2,1)S(1)} %shard_map.88), channel_id=1, source_target_pairs={{0,4},{4,0},{1,5},{5,1},{2,6},{6,2},{3,7},{7,3},{8,12},{12,8},{9,1... | collective-permute-start | bytes 98312 | tf_op jit(solution)/shard_map/ppermute | solution.py:214

commit v6 on v5

--- a/solution.py
+++ b/solution.py
@@ -13,6 +13,11 @@
 VMEM = pl.BlockSpec(memory_space=pltpu.VMEM)
 SMEM = pl.BlockSpec(memory_space=pltpu.SMEM)
 HBM = pl.BlockSpec(memory_space=pltpu.HBM)
+SOON = 2
+TURNS = (
+    ((0, 2, -3, 1, 3, -1, -2), (-3, -2, 3, 0, -1, 2, 1)),
+    ((0, 1, -1, 3, -2, 2, -3), (-2, 0, 2, -3, -1, 1, 3)),
+)
 
 
 def run_kernel(body, outs, args, specs=None, out_specs=None, scratch=(), flops=0):
@@ -32,11 +37,12 @@
 
 
 def order_of(chips, second, phase):
-    plane = [(0, step) for step in reversed(range(1, chips))]
-    cross = [(1, step) for step in range(chips)]
-    if second:
-        return plane[:-1] + cross[:1] + plane[-1:] + cross[1:]
-    return cross + plane
+    if 2 * chips - 1 == len(TURNS[0][0]):
+        turns = TURNS[phase][int(second)]
+    else:
+        cross, plane = list(range(chips)), [-step for step in reversed(range(1, chips))]
+        turns = plane + cross if second else cross + plane
+    return [(int(turn >= 0), abs(turn)) for turn in turns]
 
 
 def in_second():
@@ -51,7 +57,8 @@
     ]
 
 
-def pack_body(less, more, first, away, keep, held, turned, sems):
+def pack_body(less, more, *refs):
+    soon, (away, keep, held, turned, sems) = refs[:SOON], refs[SOON:]
     chip, core = lax.axis_index("chip"), lax.axis_index("core")
     copies = [
         pltpu.make_async_copy(source, held.at[place], sems.at[place])
@@ -67,9 +74,10 @@
             if kind == 0:
                 whole = whole.astype(F32).T.astype(BF16)
             turned[kind, part] = whole
-    crosses, step = turn_of(chips, 0, 0)
-    for owner in range(2):
-        first[owner] = turned[crosses, :, rows_of(2 * (chip ^ step) + owner, rows)]
+    for turn, block in enumerate(soon):
+        crosses, step = turn_of(chips, turn, 0)
+        for owner in range(2):
+            block[owner] = turned[crosses, :, rows_of(2 * (chip ^ step) + owner, rows)]
     for kind in range(2):
         for place in range(chips):
             top = 2 * (chip ^ place)
@@ -79,29 +87,32 @@
 
 def pair_body(phase, keep, got, *blocks):
     chips, kinds = keep.shape[:2]
-    for turn, block in enumerate(blocks, 1):
+    for turn, block in enumerate(blocks, SOON):
         crosses, step = turn_of(chips, turn, phase)
         kind = crosses if kinds == 2 else 0
         block[0] = keep[step, kind]
         block[1] = got[step, kind]
 
 
-def late_body(came, _, away):
-    away[...] = came[1 - lax.axis_index("core")]
+def late_body(*refs):
+    away = refs[-1]
+    for turn in range(SOON):
+        away[turn] = refs[turn][1 - lax.axis_index("core")]
 
 
 def sort_blocks(chips, phase, blocks, late, put):
     core = lax.axis_index("core")
     for turn, block in enumerate(blocks):
         crosses, step = turn_of(chips, turn, phase)
-        if turn == 0:
-            put(crosses, step, block[core], late[...])
+        if turn < SOON:
+            put(crosses, step, block[core], late[turn])
         else:
             put(crosses, step, block[0], block[1])
 
 
 def lag_body(keep, got, late, *refs):
-    blocks, (first, away, kept, joined, polar) = refs[:-5], refs[-5:]
+    blocks, soon = refs[: -4 - SOON], refs[-4 - SOON : -4]
+    away, kept, joined, polar = refs[-4:]
     chip, core = lax.axis_index("chip"), lax.axis_index("core")
     energies, _, rows, width = polar.shape
     chips = energies // 2
@@ -127,9 +138,10 @@
                     imag += lr * mi + li * mr
                 polar[(lag, 0) + at] = (factor * imag).astype(BF16)
                 polar[(lag, 1) + at] = (-factor * real).astype(BF16)
-    _, step = turn_of(chips, 0, 1)
-    for owner in range(2):
-        first[owner] = polar[2 * (chip ^ step) + owner]
+    for turn, block in enumerate(soon):
+        _, step = turn_of(chips, turn, 1)
+        for owner in range(2):
+            block[owner] = polar[2 * (chip ^ step) + owner]
     for place in range(chips):
         top = 2 * (chip ^ place)
         away[place, 0] = polar[top + 1 - core]
@@ -213,13 +225,13 @@
     def swap_cores(value):
         return lax.ppermute(value, "core", [(0, 1), (1, 0)])
 
-    def spread(first, away, keep, phase):
+    def spread(soon, away, keep, phase):
         got = swap_cores(away)
         later = run_kernel(
-            functools.partial(pair_body, phase), [block_shape] * (2 * chips - 2), (keep, got)
+            functools.partial(pair_body, phase), [block_shape] * (2 * chips - 1 - SOON), (keep, got)
         )
         came = []
-        for turn, block in enumerate((first, *later)):
+        for turn, block in enumerate((*soon, *later)):
             pairs = []
             for chip in range(chips):
                 for half in range(2):
@@ -229,12 +241,12 @@
                         target = ((chip ^ step) * 2 + (half ^ crosses)) * lows + low
                         pairs.append((source, target))
             came.append(lax.ppermute(block, ("chip", "half", "low"), pairs))
-        (away,) = run_kernel(late_body, [((2, rows, width), BF16)], (came[0], came[1]))
+        (away,) = run_kernel(late_body, [((SOON, 2, rows, width), BF16)], (*came[:SOON], later[0], came[3]))
         return keep, got, swap_cores(away), *came
 
-    first, away, keep = run_kernel(
+    *soon, away, keep = run_kernel(
         pack_body,
-        [block_shape] + [piles(2)] * 2,
+        [block_shape] * SOON + [piles(2)] * 2,
         [pltpu.with_memory_space_constraint(value, pltpu.HBM) for value in (green_less, green_greater)],
         specs=[HBM] * 2,
         scratch=[
@@ -243,17 +255,17 @@
             pltpu.SemaphoreType.DMA((2,)),
         ],
     )
-    first, away, keep = run_kernel(
+    *soon, away, keep = run_kernel(
         lag_body,
-        [block_shape] + [piles(1)] * 2,
-        spread(first, away, keep, 0),
+        [block_shape] * SOON + [piles(1)] * 2,
+        spread(soon, away, keep, 0),
         scratch=[
             pltpu.VMEM((energies, 2, 2, rows, width), BF16),
             pltpu.VMEM((energies, 2, rows, width), BF16),
         ],
         flops=energies * (energies + 1) * 4 * rows * width,
     )
-    parts = spread(first, away, keep, 1)
+    parts = spread(soon, away, keep, 1)
     coupling, weights = run_kernel(
         weigh_body,
         [((width, width), BF16), ((2, 8, 128), F32)],

time: 37.4 us -> 36.4 us (0.973)
  waiting for transfers between devices: 9.4 us -> 7.02 us
  starting transfers between devices: 24.2 us -> 25.2 us
    ppermute x4, waiting for transfers between devices: 1.34 us -> 0.01 us  [swap_cores(): return lax.ppermute(value, 'core', [(0, 1), (1, 0)])]
    ppermute x14, waiting for transfers between devices: 8.06 us -> 7.01 us  [spread(): came.append(lax.ppermute(block, ('chip', 'half', 'low'), pairs))]
    ppermute x14, starting transfers between devices: 23.5 us -> 24.5 us  [spread(): came.append(lax.ppermute(block, ('chip', 'half', 'low'), pairs))]
  transfers between devices with their start and end apart: 18 -> 18, of which waited for: 8 -> 5; matrix products, arithmetic and copies ran while one was open for 0% -> 0% of each run, Pallas kernels for 2% -> 2%
where the time goes in v6:
time: 36.4 us; the launch traced here: 36.1 us
  starting transfers between devices  25.2 us (69%)
  waiting for transfers between devices  7.02 us (19%)
  Pallas kernels  3.63 us (10%)
    ppermute x14, starting transfers between devices, spread(): came.append(lax.ppermute(block, ('chip', 'half', 'low'), pairs))  24.5 us
    ppermute x14, waiting for transfers between devices, spread(): came.append(lax.ppermute(block, ('chip', 'half', 'low'), pairs))  7.01 us
    pallas_call x8, Pallas kernels, run_kernel(): pl.pallas_call(body, out_shape=[jax.ShapeDtypeStruct(shape, dtype) for sh...  3.63 us
    ppermute x4, starting transfers between devices, swap_cores(): return lax.ppermute(value, 'core', [(0, 1), (1, 0)])  0.73 us
  transfers between devices with their start and end apart: 18, of which 5 were waited for; matrix products, arithmetic and copies ran while one was open for 0% of the time, Pallas kernels for 2%

profile of v6, /device:TPU:0, one launch (start us, length us, event | category | flops | bytes accessed | tf_op | source)
XLA Modules:
  0.0 36.1 jit_solution(5980857374892210285)
XLA Ops:
  0.0 1.2 %shard_map.82 = (bf16[2,2,32,256]{3,2,1,0:T(8,128)(2,1)S(1)}, bf16[2,2,32,256]{3,2,1,0:T(8,128)(2,1)S(1)}, bf16[4,2,2,32,256]{4,3,2,1,0:T(8,128)(2,1)S(1)}, bf16[4,2,2,32,256]{4,3,2,1,0:T(8,128)(2,1)S(1)}) custom-call(bf16[2,1,256,256]{3,2,1,0:T(8,128)(2,1)} %less.1, bf16[2,1,256,256]{3,2,1,0:T(8,128)(2,1)} %more.1), custom_call_target="tpu_custom_call" | custom-call | bytes 524288 | tf_op jit(solution)/shard_map/pallas_call | solution.py:24
  1.2 0.5 %collective-permute-start = (bf16[4,2,2,32,256]{4,3,2,1,0:T(8,128)(2,1)S(1)}, bf16[4,2,2,32,256]{4,3,2,1,0:T(8,128)(2,1)S(1)}, u32[]{:S(2)}, u32[]{:S(2)}) collective-permute-start(bf16[4,2,2,32,256]{4,3,2,1,0:T(8,128)(2,1)S(1)} %get-tuple-element.26), channel_id=1, source_target_pairs={{0,4},{4,0},{1,5},{5,1},{2,6},{6,2},{3,7},{7,3},{8,12},{12,8},{9,1... | collective-permute-start | bytes 786440 | tf_op jit(solution)/shard_map/ppermute | solution.py:226
  1.7 3.7 %collective-permute-start.1 = (bf16[2,2,32,256]{3,2,1,0:T(8,128)(2,1)S(1)}, bf16[2,2,32,256]{3,2,1,0:T(8,128)(2,1)S(1)}, u32[]{:S(2)}, u32[]{:S(2)}) collective-permute-start(bf16[2,2,32,256]{3,2,1,0:T(8,128)(2,1)S(1)} %get-tuple-element.27), channel_id=1, source_target_pairs={{0,2},{1,25},{2,0},{3,27},{8,10},{9,17},{10,8},{11,19},{16,18},{17... | collective-permute-start | bytes 196616 | tf_op jit(solution)/shard_map/ppermute | solution.py:243
  5.4 1.3 %collective-permute-start.2 = (bf16[2,2,32,256]{3,2,1,0:T(8,128)(2,1)S(1)}, bf16[2,2,32,256]{3,2,1,0:T(8,128)(2,1)S(1)}, u32[]{:S(2)}, u32[]{:S(2)}) collective-permute-start(bf16[2,2,32,256]{3,2,1,0:T(8,128)(2,1)S(1)} %get-tuple-element.28), channel_id=1, source_target_pairs={{0,18},{1,17},{2,16},{3,19},{8,26},{9,25},{10,24},{11,27},{16,2},{... | collective-permute-start | bytes 196616 | tf_op jit(solution)/shard_map/ppermute | solution.py:243
  6.7 3.6 %collective-permute-start.3 = (bf16[2,2,32,256]{3,2,1,0:T(8,128)(2,1)S(1)}, bf16[2,2,32,256]{3,2,1,0:T(8,128)(2,1)S(1)}, u32[]{:S(2)}, u32[]{:S(2)}) collective-permute-start(bf16[2,2,32,256]{3,2,1,0:T(8,128)(2,1)S(1)} %get-tuple-element.30), channel_id=1, source_target_pairs={{0,10},{1,3},{2,8},{3,1},{8,2},{9,11},{10,0},{11,9},{16,26},{17,19... | collective-permute-start | bytes 196616 | tf_op jit(solution)/shard_map/ppermute | solution.py:243
  10.3 1.7 %collective-permute-start.7 = (bf16[2,2,32,256]{3,2,1,0:T(8,128)(2,1)S(1)}, bf16[2,2,32,256]{3,2,1,0:T(8,128)(2,1)S(1)}, u32[]{:S(2)}, u32[]{:S(2)}) collective-permute-start(bf16[2,2,32,256]{3,2,1,0:T(8,128)(2,1)S(1)} %get-tuple-element.32), channel_id=1, source_target_pairs={{0,8},{1,19},{2,10},{3,17},{8,0},{9,27},{10,2},{11,25},{16,24},{17... | collective-permute-start | bytes 196616 | tf_op jit(solution)/shard_map/ppermute | solution.py:243
  12.0 1.5 %collective-permute-start.8 = (bf16[2,2,32,256]{3,2,1,0:T(8,128)(2,1)S(1)}, bf16[2,2,32,256]{3,2,1,0:T(8,128)(2,1)S(1)}, u32[]{:S(2)}, u32[]{:S(2)}) collective-permute-start(bf16[2,2,32,256]{3,2,1,0:T(8,128)(2,1)S(1)} %get-tuple-element.33), channel_id=1, source_target_pairs={{0,16},{1,11},{2,18},{3,9},{8,24},{9,3},{10,26},{11,1},{16,0},{17,... | collective-permute-start | bytes 196616 | tf_op jit(solution)/shard_map/ppermute | solution.py:243
  13.5 1.4 %collective-permute-start.5 = (bf16[2,2,32,256]{3,2,1,0:T(8,128)(2,1)S(1)}, bf16[2,2,32,256]{3,2,1,0:T(8,128)(2,1)S(1)}, u32[]{:S(2)}, u32[]{:S(2)}) collective-permute-start(bf16[2,2,32,256]{3,2,1,0:T(8,128)(2,1)S(1)} %get-tuple-element.29.refs_2_), channel_id=1, source_target_pairs={{0,24},{1,27},{2,26},{3,25},{8,16},{9,19},{10,18},{11,17},{16,8},{... | collective-permute-start | bytes 196616 | tf_op jit(solution)/shard_map/ppermute | solution.py:243
  15.0 5.0 %collective-permute-done.6.refs_4_ = bf16[2,2,32,256]{3,2,1,0:T(8,128)(2,1)S(1)} collective-permute-done((bf16[2,2,32,256]{3,2,1,0:T(8,128)(2,1)S(1)}, bf16[2,2,32,256]{3,2,1,0:T(8,128)(2,1)S(1)}, u32[]{:S(2)}, u32[]{:S(2)}) %collective-permute-start.6) | collective-permute-done | bytes 65568 | tf_op jit(solution)/shard_map/ppermute | solution.py:243
  20.0 0.5 %shard_map.85 = (bf16[2,2,32,256]{3,2,1,0:T(8,128)(2,1)S(1)}, bf16[2,2,32,256]{3,2,1,0:T(8,128)(2,1)S(1)}, bf16[4,1,2,32,256]{4,3,2,1,0:T(8,128)(2,1)S(1)}, bf16[4,1,2,32,256]{4,3,2,1,0:T(8,128)(2,1)S(1)}) custom-call(bf16[4,2,2,32,256]{4,3,2,1,0:T(8,128)(2,1)S(1)} %get-tuple-element.25.keep, bf16[4,2,2,32,256]{4,3,2,1,0:T(8,128)(2,1)S(1)} %collective-permute-done.got, ...), custom_call_target="tpu_custom_call" | custom-call | flops 2359296 | bytes 524288 | tf_op jit(solution)/shard_map/pallas_call | solution.py:24
  20.5 0.1 collective-permute-start.9
  20.5 1.4 %collective-permute-start.10 = (bf16[2,2,32,256]{3,2,1,0:T(8,128)(2,1)S(1)}, bf16[2,2,32,256]{3,2,1,0:T(8,128)(2,1)S(1)}, u32[]{:S(2)}, u32[]{:S(2)}) collective-permute-start(bf16[2,2,32,256]{3,2,1,0:T(8,128)(2,1)S(1)} %get-tuple-element.38), channel_id=1, source_target_pairs={{0,2},{1,17},{2,0},{3,19},{8,10},{9,25},{10,8},{11,27},{16,18},{17... | collective-permute-start | bytes 196616 | tf_op jit(solution)/shard_map/ppermute | solution.py:243
  21.9 1.7 %collective-permute-start.11 = (bf16[2,2,32,256]{3,2,1,0:T(8,128)(2,1)S(1)}, bf16[2,2,32,256]{3,2,1,0:T(8,128)(2,1)S(1)}, u32[]{:S(2)}, u32[]{:S(2)}) collective-permute-start(bf16[2,2,32,256]{3,2,1,0:T(8,128)(2,1)S(1)} %get-tuple-element.39), channel_id=1, source_target_pairs={{0,10},{1,3},{2,8},{3,1},{8,2},{9,11},{10,0},{11,9},{16,26},{17,19... | collective-permute-start | bytes 196616 | tf_op jit(solution)/shard_map/ppermute | solution.py:243
  23.6 2.1 %collective-permute-start.12 = (bf16[2,2,32,256]{3,2,1,0:T(8,128)(2,1)S(1)}, bf16[2,2,32,256]{3,2,1,0:T(8,128)(2,1)S(1)}, u32[]{:S(2)}, u32[]{:S(2)}) collective-permute-start(bf16[2,2,32,256]{3,2,1,0:T(8,128)(2,1)S(1)} %get-tuple-element.41), channel_id=1, source_target_pairs={{0,26},{1,25},{2,24},{3,27},{8,18},{9,17},{10,16},{11,19},{16,10},... | collective-permute-start | bytes 196616 | tf_op jit(solution)/shard_map/ppermute | solution.py:243
  25.8 1.5 %collective-permute-start.15 = (bf16[2,2,32,256]{3,2,1,0:T(8,128)(2,1)S(1)}, bf16[2,2,32,256]{3,2,1,0:T(8,128)(2,1)S(1)}, u32[]{:S(2)}, u32[]{:S(2)}) collective-permute-start(bf16[2,2,32,256]{3,2,1,0:T(8,128)(2,1)S(1)} %get-tuple-element.42), channel_id=1, source_target_pairs={{0,16},{1,9},{2,18},{3,11},{8,24},{9,1},{10,26},{11,3},{16,0},{17,... | collective-permute-start | bytes 196616 | tf_op jit(solution)/shard_map/ppermute | solution.py:243
  27.3 1.9 %collective-permute-start.16 = (bf16[2,2,32,256]{3,2,1,0:T(8,128)(2,1)S(1)}, bf16[2,2,32,256]{3,2,1,0:T(8,128)(2,1)S(1)}, u32[]{:S(2)}, u32[]{:S(2)}) collective-permute-start(bf16[2,2,32,256]{3,2,1,0:T(8,128)(2,1)S(1)} %get-tuple-element.43), channel_id=1, source_target_pairs={{0,18},{1,11},{2,16},{3,9},{8,26},{9,3},{10,24},{11,1},{16,2},{17,... | collective-permute-start | bytes 196616 | tf_op jit(solution)/shard_map/ppermute | solution.py:243
  29.2 1.3 %collective-permute-start.17 = (bf16[2,2,32,256]{3,2,1,0:T(8,128)(2,1)S(1)}, bf16[2,2,32,256]{3,2,1,0:T(8,128)(2,1)S(1)}, u32[]{:S(2)}, u32[]{:S(2)}) collective-permute-start(bf16[2,2,32,256]{3,2,1,0:T(8,128)(2,1)S(1)} %get-tuple-element.44), channel_id=1, source_target_pairs={{0,24},{1,27},{2,26},{3,25},{8,16},{9,19},{10,18},{11,17},{16,8},{... | collective-permute-start | bytes 196616 | tf_op jit(solution)/shard_map/ppermute | solution.py:243
  30.5 1.5 %collective-permute-start.14 = (bf16[2,2,32,256]{3,2,1,0:T(8,128)(2,1)S(1)}, bf16[2,2,32,256]{3,2,1,0:T(8,128)(2,1)S(1)}, u32[]{:S(2)}, u32[]{:S(2)}) collective-permute-start(bf16[2,2,32,256]{3,2,1,0:T(8,128)(2,1)S(1)} %get-tuple-element.40.refs_2_), channel_id=1, source_target_pairs={{0,8},{1,19},{2,10},{3,17},{8,0},{9,27},{10,2},{11,25},{16,24},{17... | collective-permute-start | bytes 196616 | tf_op jit(solution)/shard_map/ppermute | solution.py:243
  32.1 0.7 %shard_map.86 = (bf16[256,256]{1,0:T(8,128)(2,1)S(1)}, f32[2,8,128]{2,1,0:T(8,128)S(1)}) custom-call(s32[1,2]{1,0:T(1,128)S(1)} %copy-done.3, f32[3]{0:T(128)S(1)} %copy-done.4, f32[2]{0:T(128)S(1)} %copy-done.5, s32[3,3]{1,0:T(4,128)S(1)} %copy-done.2, bf16[256,256]{1,0:T(8,128)(2,1)S(1)} %copy-done.1, bf16[4,1,2,32,256]{4,3,2,1,0:T(8,128)(2,1)S(1)} %get-tuple-element.34._), custom_call_target="tpu_custom_call" | custom-call | bytes 524288 | tf_op jit(solution)/shard_map/pallas_call | solution.py:24
  32.8 0.2 collective-permute-done.15.refs_4_
  33.0 1.4 %collective-permute-done.16.refs_5_ = bf16[2,2,32,256]{3,2,1,0:T(8,128)(2,1)S(1)} collective-permute-done((bf16[2,2,32,256]{3,2,1,0:T(8,128)(2,1)S(1)}, bf16[2,2,32,256]{3,2,1,0:T(8,128)(2,1)S(1)}, u32[]{:S(2)}, u32[]{:S(2)}) %collective-permute-start.16) | collective-permute-done | bytes 65568 | tf_op jit(solution)/shard_map/ppermute | solution.py:243
  34.4 0.2 collective-permute-done.17.refs_6_
  34.6 0.2 collective-permute-done.14.refs_2_
  34.8 1.2 %shard_map.89 = bf16[2,1,256,256]{3,2,1,0:T(8,128)(2,1)} custom-call(bf16[256,256]{1,0:T(8,128)(2,1)S(1)} %copy-done, bf16[256,256]{1,0:T(8,128)(2,1)S(1)} %get-tuple-element.35.coupling, f32[2,8,128]{2,1,0:T(8,128)S(1)} %get-tuple-element.36.weights, bf16[4,1,2,32,256]{4,3,2,1,0:T(8,128)(2,1)S(1)} %get-tuple-element.37.keep, ...), custom_call_target="tpu_custom_call" | custom-call | flops 268435456 | bytes 524288 | tf_op jit(solution)/shard_map/pallas_call | solution.py:24
  (32 shorter events, 0.3 us)
Async XLA Ops:
  1.2 5.5 %collective-permute-start = (bf16[4,2,2,32,256]{4,3,2,1,0:T(8,128)(2,1)S(1)}, bf16[4,2,2,32,256]{4,3,2,1,0:T(8,128)(2,1)S(1)}, u32[]{:S(2)}, u32[]{:S(2)}) collective-permute-start(bf16[4,2,2,32,256]{4,3,2,1,0:T(8,128)(2,1)S(1)} %get-tuple-element.26), channel_id=1, source_target_pairs={{0,4},{4,0},{1,5},{5,1},{2,6},{6,2},{3,7},{7,3},{8,12},{12,8},{9,1... | collective-permute-start | bytes 786440 | tf_op jit(solution)/shard_map/ppermute | solution.py:226
  1.7 10.3 %collective-permute-start.1 = (bf16[2,2,32,256]{3,2,1,0:T(8,128)(2,1)S(1)}, bf16[2,2,32,256]{3,2,1,0:T(8,128)(2,1)S(1)}, u32[]{:S(2)}, u32[]{:S(2)}) collective-permute-start(bf16[2,2,32,256]{3,2,1,0:T(8,128)(2,1)S(1)} %get-tuple-element.27), channel_id=1, source_target_pairs={{0,2},{1,25},{2,0},{3,27},{8,10},{9,17},{10,8},{11,19},{16,18},{17... | collective-permute-start | bytes 196616 | tf_op jit(solution)/shard_map/ppermute | solution.py:243
  5.4 8.2 %collective-permute-start.2 = (bf16[2,2,32,256]{3,2,1,0:T(8,128)(2,1)S(1)}, bf16[2,2,32,256]{3,2,1,0:T(8,128)(2,1)S(1)}, u32[]{:S(2)}, u32[]{:S(2)}) collective-permute-start(bf16[2,2,32,256]{3,2,1,0:T(8,128)(2,1)S(1)} %get-tuple-element.28), channel_id=1, source_target_pairs={{0,18},{1,17},{2,16},{3,19},{8,26},{9,25},{10,24},{11,27},{16,2},{... | collective-permute-start | bytes 196616 | tf_op jit(solution)/shard_map/ppermute | solution.py:243
  6.7 8.2 %collective-permute-start.3 = (bf16[2,2,32,256]{3,2,1,0:T(8,128)(2,1)S(1)}, bf16[2,2,32,256]{3,2,1,0:T(8,128)(2,1)S(1)}, u32[]{:S(2)}, u32[]{:S(2)}) collective-permute-start(bf16[2,2,32,256]{3,2,1,0:T(8,128)(2,1)S(1)} %get-tuple-element.30), channel_id=1, source_target_pairs={{0,10},{1,3},{2,8},{3,1},{8,2},{9,11},{10,0},{11,9},{16,26},{17,19... | collective-permute-start | bytes 196616 | tf_op jit(solution)/shard_map/ppermute | solution.py:243
  10.3 9.7 %collective-permute-start.6 = (bf16[2,2,32,256]{3,2,1,0:T(8,128)(2,1)S(1)}, bf16[2,2,32,256]{3,2,1,0:T(8,128)(2,1)S(1)}, u32[]{:S(2)}, u32[]{:S(2)}) collective-permute-start(bf16[2,2,32,256]{3,2,1,0:T(8,128)(2,1)S(1)} %get-tuple-element.31), channel_id=1, source_target_pairs={{0,26},{1,9},{2,24},{3,11},{8,18},{9,1},{10,16},{11,3},{16,10},{17... | collective-permute-start | bytes 196616 | tf_op jit(solution)/shard_map/ppermute | solution.py:243
  10.3 9.7 %collective-permute-start.7 = (bf16[2,2,32,256]{3,2,1,0:T(8,128)(2,1)S(1)}, bf16[2,2,32,256]{3,2,1,0:T(8,128)(2,1)S(1)}, u32[]{:S(2)}, u32[]{:S(2)}) collective-permute-start(bf16[2,2,32,256]{3,2,1,0:T(8,128)(2,1)S(1)} %get-tuple-element.32), channel_id=1, source_target_pairs={{0,8},{1,19},{2,10},{3,17},{8,0},{9,27},{10,2},{11,25},{16,24},{17... | collective-permute-start | bytes 196616 | tf_op jit(solution)/shard_map/ppermute | solution.py:243
  12.0 8.0 %collective-permute-start.8 = (bf16[2,2,32,256]{3,2,1,0:T(8,128)(2,1)S(1)}, bf16[2,2,32,256]{3,2,1,0:T(8,128)(2,1)S(1)}, u32[]{:S(2)}, u32[]{:S(2)}) collective-permute-start(bf16[2,2,32,256]{3,2,1,0:T(8,128)(2,1)S(1)} %get-tuple-element.33), channel_id=1, source_target_pairs={{0,16},{1,11},{2,18},{3,9},{8,24},{9,3},{10,26},{11,1},{16,0},{17,... | collective-permute-start | bytes 196616 | tf_op jit(solution)/shard_map/ppermute | solution.py:243
  13.5 6.4 %collective-permute-start.5 = (bf16[2,2,32,256]{3,2,1,0:T(8,128)(2,1)S(1)}, bf16[2,2,32,256]{3,2,1,0:T(8,128)(2,1)S(1)}, u32[]{:S(2)}, u32[]{:S(2)}) collective-permute-start(bf16[2,2,32,256]{3,2,1,0:T(8,128)(2,1)S(1)} %get-tuple-element.29.refs_2_), channel_id=1, source_target_pairs={{0,24},{1,27},{2,26},{3,25},{8,16},{9,19},{10,18},{11,17},{16,8},{... | collective-permute-start | bytes 196616 | tf_op jit(solution)/shard_map/ppermute | solution.py:243
  14.9 5.1 %collective-permute-start.4 = (bf16[2,2,32,256]{3,2,1,0:T(8,128)(2,1)S(1)}, bf16[2,2,32,256]{3,2,1,0:T(8,128)(2,1)S(1)}, u32[]{:S(2)}, u32[]{:S(2)}) collective-permute-start(bf16[2,2,32,256]{3,2,1,0:T(8,128)(2,1)S(1)} %shard_map.84), channel_id=1, source_target_pairs={{0,4},{4,0},{1,5},{5,1},{2,6},{6,2},{3,7},{7,3},{8,12},{12,8},{9,1... | collective-permute-start | bytes 196616 | tf_op jit(solution)/shard_map/ppermute | solution.py:226
  20.5 3.1 %collective-permute-start.9 = (bf16[4,1,2,32,256]{4,3,2,1,0:T(8,128)(2,1)S(1)}, bf16[4,1,2,32,256]{4,3,2,1,0:T(8,128)(2,1)S(1)}, u32[]{:S(2)}, u32[]{:S(2)}) collective-permute-start(bf16[4,1,2,32,256]{4,3,2,1,0:T(8,128)(2,1)S(1)} %get-tuple-element.34._), channel_id=1, source_target_pairs={{0,4},{4,0},{1,5},{5,1},{2,6},{6,2},{3,7},{7,3},{8,12},{12,8},{9,1... | collective-permute-start | bytes 393224 | tf_op jit(solution)/shard_map/ppermute | solution.py:226
  20.5 8.6 %collective-permute-start.10 = (bf16[2,2,32,256]{3,2,1,0:T(8,128)(2,1)S(1)}, bf16[2,2,32,256]{3,2,1,0:T(8,128)(2,1)S(1)}, u32[]{:S(2)}, u32[]{:S(2)}) collective-permute-start(bf16[2,2,32,256]{3,2,1,0:T(8,128)(2,1)S(1)} %get-tuple-element.38), channel_id=1, source_target_pairs={{0,2},{1,17},{2,0},{3,19},{8,10},{9,25},{10,8},{11,27},{16,18},{17... | collective-permute-start | bytes 196616 | tf_op jit(solution)/shard_map/ppermute | solution.py:243
  21.9 8.6 %collective-permute-start.11 = (bf16[2,2,32,256]{3,2,1,0:T(8,128)(2,1)S(1)}, bf16[2,2,32,256]{3,2,1,0:T(8,128)(2,1)S(1)}, u32[]{:S(2)}, u32[]{:S(2)}) collective-permute-start(bf16[2,2,32,256]{3,2,1,0:T(8,128)(2,1)S(1)} %get-tuple-element.39), channel_id=1, source_target_pairs={{0,10},{1,3},{2,8},{3,1},{8,2},{9,11},{10,0},{11,9},{16,26},{17,19... | collective-permute-start | bytes 196616 | tf_op jit(solution)/shard_map/ppermute | solution.py:243
  23.6 8.3 %collective-permute-start.12 = (bf16[2,2,32,256]{3,2,1,0:T(8,128)(2,1)S(1)}, bf16[2,2,32,256]{3,2,1,0:T(8,128)(2,1)S(1)}, u32[]{:S(2)}, u32[]{:S(2)}) collective-permute-start(bf16[2,2,32,256]{3,2,1,0:T(8,128)(2,1)S(1)} %get-tuple-element.41), channel_id=1, source_target_pairs={{0,26},{1,25},{2,24},{3,27},{8,18},{9,17},{10,16},{11,19},{16,10},... | collective-permute-start | bytes 196616 | tf_op jit(solution)/shard_map/ppermute | solution.py:243
  25.8 7.2 %collective-permute-start.15 = (bf16[2,2,32,256]{3,2,1,0:T(8,128)(2,1)S(1)}, bf16[2,2,32,256]{3,2,1,0:T(8,128)(2,1)S(1)}, u32[]{:S(2)}, u32[]{:S(2)}) collective-permute-start(bf16[2,2,32,256]{3,2,1,0:T(8,128)(2,1)S(1)} %get-tuple-element.42), channel_id=1, source_target_pairs={{0,16},{1,9},{2,18},{3,11},{8,24},{9,1},{10,26},{11,3},{16,0},{17,... | collective-permute-start | bytes 196616 | tf_op jit(solution)/shard_map/ppermute | solution.py:243
  27.3 7.2 %collective-permute-start.16 = (bf16[2,2,32,256]{3,2,1,0:T(8,128)(2,1)S(1)}, bf16[2,2,32,256]{3,2,1,0:T(8,128)(2,1)S(1)}, u32[]{:S(2)}, u32[]{:S(2)}) collective-permute-start(bf16[2,2,32,256]{3,2,1,0:T(8,128)(2,1)S(1)} %get-tuple-element.43), channel_id=1, source_target_pairs={{0,18},{1,11},{2,16},{3,9},{8,26},{9,3},{10,24},{11,1},{16,2},{17,... | collective-permute-start | bytes 196616 | tf_op jit(solution)/shard_map/ppermute | solution.py:243
  29.2 5.4 %collective-permute-start.17 = (bf16[2,2,32,256]{3,2,1,0:T(8,128)(2,1)S(1)}, bf16[2,2,32,256]{3,2,1,0:T(8,128)(2,1)S(1)}, u32[]{:S(2)}, u32[]{:S(2)}) collective-permute-start(bf16[2,2,32,256]{3,2,1,0:T(8,128)(2,1)S(1)} %get-tuple-element.44), channel_id=1, source_target_pairs={{0,24},{1,27},{2,26},{3,25},{8,16},{9,19},{10,18},{11,17},{16,8},{... | collective-permute-start | bytes 196616 | tf_op jit(solution)/shard_map/ppermute | solution.py:243
  30.5 1.6 %copy-start.1 = (bf16[256,256]{1,0:T(8,128)(2,1)S(1)}, bf16[256,256]{1,0:T(8,128)(2,1)}, u32[]{:S(2)}) copy-start(bf16[256,256]{1,0:T(8,128)(2,1)} %link.1) | copy-start | bytes 393220
  30.5 1.6 %copy-start.2 = (s32[3,3]{1,0:T(4,128)S(1)}, s32[3,3]{1,0:T(4,128)}, u32[]{:S(2)}) copy-start(s32[3,3]{1,0:T(4,128)} %mask.1) | copy-start | bytes 112
  30.5 1.6 %copy-start.3 = (s32[1,2]{1,0:T(1,128)S(1)}, s32[1,2]{1,0:T(1,128)}, u32[]{:S(2)}) copy-start(s32[1,2]{1,0:T(1,128)} %blocks.1) | copy-start | bytes 28
  30.5 1.6 %copy-start.4 = (f32[3]{0:T(128)S(1)}, f32[3]{0:T(128)}, u32[]{:S(2)}) copy-start(f32[3]{0:T(128)} %onsite_scale.1) | copy-start | bytes 40
  30.5 1.6 %copy-start.5 = (f32[2]{0:T(128)S(1)}, f32[2]{0:T(128)}, u32[]{:S(2)}) copy-start(f32[2]{0:T(128)} %coupling_scale.1) | copy-start | bytes 28
  30.5 4.3 %collective-permute-start.14 = (bf16[2,2,32,256]{3,2,1,0:T(8,128)(2,1)S(1)}, bf16[2,2,32,256]{3,2,1,0:T(8,128)(2,1)S(1)}, u32[]{:S(2)}, u32[]{:S(2)}) collective-permute-start(bf16[2,2,32,256]{3,2,1,0:T(8,128)(2,1)S(1)} %get-tuple-element.40.refs_2_), channel_id=1, source_target_pairs={{0,8},{1,19},{2,10},{3,17},{8,0},{9,27},{10,2},{11,25},{16,24},{17... | collective-permute-start | bytes 196616 | tf_op jit(solution)/shard_map/ppermute | solution.py:243
  32.0 2.9 %copy-start = (bf16[256,256]{1,0:T(8,128)(2,1)S(1)}, bf16[256,256]{1,0:T(8,128)(2,1)}, u32[]{:S(2)}) copy-start(bf16[256,256]{1,0:T(8,128)(2,1)} %onsite.1) | copy-start | bytes 393220
  32.0 2.9 %collective-permute-start.13 = (bf16[2,2,32,256]{3,2,1,0:T(8,128)(2,1)S(1)}, bf16[2,2,32,256]{3,2,1,0:T(8,128)(2,1)S(1)}, u32[]{:S(2)}, u32[]{:S(2)}) collective-permute-start(bf16[2,2,32,256]{3,2,1,0:T(8,128)(2,1)S(1)} %shard_map.88), channel_id=1, source_target_pairs={{0,4},{4,0},{1,5},{5,1},{2,6},{6,2},{3,7},{7,3},{8,12},{12,8},{9,1... | collective-permute-start | bytes 196616 | tf_op jit(solution)/shard_map/ppermute | solution.py:226

commit v7 on v6

--- a/solution.py
+++ b/solution.py
@@ -15,8 +15,8 @@
 HBM = pl.BlockSpec(memory_space=pltpu.HBM)
 SOON = 2
 TURNS = (
-    ((0, 2, -3, 1, 3, -1, -2), (-3, -2, 3, 0, -1, 2, 1)),
-    ((0, 1, -1, 3, -2, 2, -3), (-2, 0, 2, -3, -1, 1, 3)),
+    ((0, 2, -3, 1, 3, -1, -2), (-3, -2, 3, 0, 2, -1, 1)),
+    ((0, 1, -1, 3, -2, 2, -3), (-2, 0, 2, -3, 1, -1, 3)),
 )
 
 

time: 36.4 us -> 36.5 us (level)
  no operation moved by 1% of the time
where the time goes in v7:
time: 36.5 us; the launch traced here: 36.4 us
  starting transfers between devices  25.2 us (69%)
  waiting for transfers between devices  7.35 us (20%)
  Pallas kernels  3.64 us (10%)
    ppermute x14, starting transfers between devices, spread(): came.append(lax.ppermute(block, ('chip', 'half', 'low'), pairs))  24.5 us
    ppermute x14, waiting for transfers between devices, spread(): came.append(lax.ppermute(block, ('chip', 'half', 'low'), pairs))  7.34 us
    pallas_call x8, Pallas kernels, run_kernel(): pl.pallas_call(body, out_shape=[jax.ShapeDtypeStruct(shape, dtype) for sh...  3.64 us
  transfers between devices with their start and end apart: 18, of which 5 were waited for; matrix products, arithmetic and copies ran while one was open for 0% of the time, Pallas kernels for 2%

profile of v7, /device:TPU:0, one launch (start us, length us, event | category | flops | bytes accessed | tf_op | source)
XLA Modules:
  0.0 36.4 jit_solution(11056576827146751666)
XLA Ops:
  0.0 1.2 %shard_map.82 = (bf16[2,2,32,256]{3,2,1,0:T(8,128)(2,1)S(1)}, bf16[2,2,32,256]{3,2,1,0:T(8,128)(2,1)S(1)}, bf16[4,2,2,32,256]{4,3,2,1,0:T(8,128)(2,1)S(1)}, bf16[4,2,2,32,256]{4,3,2,1,0:T(8,128)(2,1)S(1)}) custom-call(bf16[2,1,256,256]{3,2,1,0:T(8,128)(2,1)} %less.1, bf16[2,1,256,256]{3,2,1,0:T(8,128)(2,1)} %more.1), custom_call_target="tpu_custom_call" | custom-call | bytes 524288 | tf_op jit(solution)/shard_map/pallas_call | solution.py:24
  1.2 0.5 %collective-permute-start = (bf16[4,2,2,32,256]{4,3,2,1,0:T(8,128)(2,1)S(1)}, bf16[4,2,2,32,256]{4,3,2,1,0:T(8,128)(2,1)S(1)}, u32[]{:S(2)}, u32[]{:S(2)}) collective-permute-start(bf16[4,2,2,32,256]{4,3,2,1,0:T(8,128)(2,1)S(1)} %get-tuple-element.26), channel_id=1, source_target_pairs={{0,4},{4,0},{1,5},{5,1},{2,6},{6,2},{3,7},{7,3},{8,12},{12,8},{9,1... | collective-permute-start | bytes 786440 | tf_op jit(solution)/shard_map/ppermute | solution.py:226
  1.7 3.7 %collective-permute-start.1 = (bf16[2,2,32,256]{3,2,1,0:T(8,128)(2,1)S(1)}, bf16[2,2,32,256]{3,2,1,0:T(8,128)(2,1)S(1)}, u32[]{:S(2)}, u32[]{:S(2)}) collective-permute-start(bf16[2,2,32,256]{3,2,1,0:T(8,128)(2,1)S(1)} %get-tuple-element.27), channel_id=1, source_target_pairs={{0,2},{1,25},{2,0},{3,27},{8,10},{9,17},{10,8},{11,19},{16,18},{17... | collective-permute-start | bytes 196616 | tf_op jit(solution)/shard_map/ppermute | solution.py:243
  5.4 1.3 %collective-permute-start.2 = (bf16[2,2,32,256]{3,2,1,0:T(8,128)(2,1)S(1)}, bf16[2,2,32,256]{3,2,1,0:T(8,128)(2,1)S(1)}, u32[]{:S(2)}, u32[]{:S(2)}) collective-permute-start(bf16[2,2,32,256]{3,2,1,0:T(8,128)(2,1)S(1)} %get-tuple-element.28), channel_id=1, source_target_pairs={{0,18},{1,17},{2,16},{3,19},{8,26},{9,25},{10,24},{11,27},{16,2},{... | collective-permute-start | bytes 196616 | tf_op jit(solution)/shard_map/ppermute | solution.py:243
  6.7 3.6 %collective-permute-start.3 = (bf16[2,2,32,256]{3,2,1,0:T(8,128)(2,1)S(1)}, bf16[2,2,32,256]{3,2,1,0:T(8,128)(2,1)S(1)}, u32[]{:S(2)}, u32[]{:S(2)}) collective-permute-start(bf16[2,2,32,256]{3,2,1,0:T(8,128)(2,1)S(1)} %get-tuple-element.30), channel_id=1, source_target_pairs={{0,10},{1,3},{2,8},{3,1},{8,2},{9,11},{10,0},{11,9},{16,26},{17,19... | collective-permute-start | bytes 196616 | tf_op jit(solution)/shard_map/ppermute | solution.py:243
  10.3 1.7 %collective-permute-start.7 = (bf16[2,2,32,256]{3,2,1,0:T(8,128)(2,1)S(1)}, bf16[2,2,32,256]{3,2,1,0:T(8,128)(2,1)S(1)}, u32[]{:S(2)}, u32[]{:S(2)}) collective-permute-start(bf16[2,2,32,256]{3,2,1,0:T(8,128)(2,1)S(1)} %get-tuple-element.32), channel_id=1, source_target_pairs={{0,8},{1,9},{2,10},{3,11},{8,0},{9,1},{10,2},{11,3},{16,24},{17,25... | collective-permute-start | bytes 196616 | tf_op jit(solution)/shard_map/ppermute | solution.py:243
  12.0 1.5 %collective-permute-start.8 = (bf16[2,2,32,256]{3,2,1,0:T(8,128)(2,1)S(1)}, bf16[2,2,32,256]{3,2,1,0:T(8,128)(2,1)S(1)}, u32[]{:S(2)}, u32[]{:S(2)}) collective-permute-start(bf16[2,2,32,256]{3,2,1,0:T(8,128)(2,1)S(1)} %get-tuple-element.33), channel_id=1, source_target_pairs={{0,16},{1,11},{2,18},{3,9},{8,24},{9,3},{10,26},{11,1},{16,0},{17,... | collective-permute-start | bytes 196616 | tf_op jit(solution)/shard_map/ppermute | solution.py:243
  13.5 1.4 %collective-permute-start.5 = (bf16[2,2,32,256]{3,2,1,0:T(8,128)(2,1)S(1)}, bf16[2,2,32,256]{3,2,1,0:T(8,128)(2,1)S(1)}, u32[]{:S(2)}, u32[]{:S(2)}) collective-permute-start(bf16[2,2,32,256]{3,2,1,0:T(8,128)(2,1)S(1)} %get-tuple-element.29.refs_2_), channel_id=1, source_target_pairs={{0,24},{1,27},{2,26},{3,25},{8,16},{9,19},{10,18},{11,17},{16,8},{... | collective-permute-start | bytes 196616 | tf_op jit(solution)/shard_map/ppermute | solution.py:243
  14.9 2.8 %collective-permute-done.3.refs_3_ = bf16[2,2,32,256]{3,2,1,0:T(8,128)(2,1)S(1)} collective-permute-done((bf16[2,2,32,256]{3,2,1,0:T(8,128)(2,1)S(1)}, bf16[2,2,32,256]{3,2,1,0:T(8,128)(2,1)S(1)}, u32[]{:S(2)}, u32[]{:S(2)}) %collective-permute-start.3) | collective-permute-done | bytes 65568 | tf_op jit(solution)/shard_map/ppermute | solution.py:243
  17.7 2.3 %collective-permute-done.6.refs_4_ = bf16[2,2,32,256]{3,2,1,0:T(8,128)(2,1)S(1)} collective-permute-done((bf16[2,2,32,256]{3,2,1,0:T(8,128)(2,1)S(1)}, bf16[2,2,32,256]{3,2,1,0:T(8,128)(2,1)S(1)}, u32[]{:S(2)}, u32[]{:S(2)}) %collective-permute-start.6) | collective-permute-done | bytes 65568 | tf_op jit(solution)/shard_map/ppermute | solution.py:243
  20.0 0.5 %shard_map.85 = (bf16[2,2,32,256]{3,2,1,0:T(8,128)(2,1)S(1)}, bf16[2,2,32,256]{3,2,1,0:T(8,128)(2,1)S(1)}, bf16[4,1,2,32,256]{4,3,2,1,0:T(8,128)(2,1)S(1)}, bf16[4,1,2,32,256]{4,3,2,1,0:T(8,128)(2,1)S(1)}) custom-call(bf16[4,2,2,32,256]{4,3,2,1,0:T(8,128)(2,1)S(1)} %get-tuple-element.25.keep, bf16[4,2,2,32,256]{4,3,2,1,0:T(8,128)(2,1)S(1)} %collective-permute-done.got, ...), custom_call_target="tpu_custom_call" | custom-call | flops 2359296 | bytes 524288 | tf_op jit(solution)/shard_map/pallas_call | solution.py:24
  20.5 0.1 collective-permute-start.9
  20.5 1.4 %collective-permute-start.10 = (bf16[2,2,32,256]{3,2,1,0:T(8,128)(2,1)S(1)}, bf16[2,2,32,256]{3,2,1,0:T(8,128)(2,1)S(1)}, u32[]{:S(2)}, u32[]{:S(2)}) collective-permute-start(bf16[2,2,32,256]{3,2,1,0:T(8,128)(2,1)S(1)} %get-tuple-element.38), channel_id=1, source_target_pairs={{0,2},{1,17},{2,0},{3,19},{8,10},{9,25},{10,8},{11,27},{16,18},{17... | collective-permute-start | bytes 196616 | tf_op jit(solution)/shard_map/ppermute | solution.py:243
  21.9 2.0 %collective-permute-start.11 = (bf16[2,2,32,256]{3,2,1,0:T(8,128)(2,1)S(1)}, bf16[2,2,32,256]{3,2,1,0:T(8,128)(2,1)S(1)}, u32[]{:S(2)}, u32[]{:S(2)}) collective-permute-start(bf16[2,2,32,256]{3,2,1,0:T(8,128)(2,1)S(1)} %get-tuple-element.39), channel_id=1, source_target_pairs={{0,10},{1,3},{2,8},{3,1},{8,2},{9,11},{10,0},{11,9},{16,26},{17,19... | collective-permute-start | bytes 196616 | tf_op jit(solution)/shard_map/ppermute | solution.py:243
  23.9 1.9 %collective-permute-start.12 = (bf16[2,2,32,256]{3,2,1,0:T(8,128)(2,1)S(1)}, bf16[2,2,32,256]{3,2,1,0:T(8,128)(2,1)S(1)}, u32[]{:S(2)}, u32[]{:S(2)}) collective-permute-start(bf16[2,2,32,256]{3,2,1,0:T(8,128)(2,1)S(1)} %get-tuple-element.41), channel_id=1, source_target_pairs={{0,26},{1,25},{2,24},{3,27},{8,18},{9,17},{10,16},{11,19},{16,10},... | collective-permute-start | bytes 196616 | tf_op jit(solution)/shard_map/ppermute | solution.py:243
  25.8 1.5 %collective-permute-start.15 = (bf16[2,2,32,256]{3,2,1,0:T(8,128)(2,1)S(1)}, bf16[2,2,32,256]{3,2,1,0:T(8,128)(2,1)S(1)}, u32[]{:S(2)}, u32[]{:S(2)}) collective-permute-start(bf16[2,2,32,256]{3,2,1,0:T(8,128)(2,1)S(1)} %get-tuple-element.42), channel_id=1, source_target_pairs={{0,16},{1,11},{2,18},{3,9},{8,24},{9,3},{10,26},{11,1},{16,0},{17,... | collective-permute-start | bytes 196616 | tf_op jit(solution)/shard_map/ppermute | solution.py:243
  27.3 1.9 %collective-permute-start.16 = (bf16[2,2,32,256]{3,2,1,0:T(8,128)(2,1)S(1)}, bf16[2,2,32,256]{3,2,1,0:T(8,128)(2,1)S(1)}, u32[]{:S(2)}, u32[]{:S(2)}) collective-permute-start(bf16[2,2,32,256]{3,2,1,0:T(8,128)(2,1)S(1)} %get-tuple-element.43), channel_id=1, source_target_pairs={{0,18},{1,9},{2,16},{3,11},{8,26},{9,1},{10,24},{11,3},{16,2},{17,... | collective-permute-start | bytes 196616 | tf_op jit(solution)/shard_map/ppermute | solution.py:243
  29.2 1.5 %collective-permute-start.17 = (bf16[2,2,32,256]{3,2,1,0:T(8,128)(2,1)S(1)}, bf16[2,2,32,256]{3,2,1,0:T(8,128)(2,1)S(1)}, u32[]{:S(2)}, u32[]{:S(2)}) collective-permute-start(bf16[2,2,32,256]{3,2,1,0:T(8,128)(2,1)S(1)} %get-tuple-element.44), channel_id=1, source_target_pairs={{0,24},{1,27},{2,26},{3,25},{8,16},{9,19},{10,18},{11,17},{16,8},{... | collective-permute-start | bytes 196616 | tf_op jit(solution)/shard_map/ppermute | solution.py:243
  30.8 1.2 %collective-permute-start.14 = (bf16[2,2,32,256]{3,2,1,0:T(8,128)(2,1)S(1)}, bf16[2,2,32,256]{3,2,1,0:T(8,128)(2,1)S(1)}, u32[]{:S(2)}, u32[]{:S(2)}) collective-permute-start(bf16[2,2,32,256]{3,2,1,0:T(8,128)(2,1)S(1)} %get-tuple-element.40.refs_2_), channel_id=1, source_target_pairs={{0,8},{1,19},{2,10},{3,17},{8,0},{9,27},{10,2},{11,25},{16,24},{17... | collective-permute-start | bytes 196616 | tf_op jit(solution)/shard_map/ppermute | solution.py:243
  32.0 1.7 %collective-permute-done.12.refs_3_ = bf16[2,2,32,256]{3,2,1,0:T(8,128)(2,1)S(1)} collective-permute-done((bf16[2,2,32,256]{3,2,1,0:T(8,128)(2,1)S(1)}, bf16[2,2,32,256]{3,2,1,0:T(8,128)(2,1)S(1)}, u32[]{:S(2)}, u32[]{:S(2)}) %collective-permute-start.12) | collective-permute-done | bytes 65568 | tf_op jit(solution)/shard_map/ppermute | solution.py:243
  33.8 0.7 %shard_map.86 = (bf16[256,256]{1,0:T(8,128)(2,1)S(1)}, f32[2,8,128]{2,1,0:T(8,128)S(1)}) custom-call(s32[1,2]{1,0:T(1,128)S(1)} %copy-done.3, f32[3]{0:T(128)S(1)} %copy-done.4, f32[2]{0:T(128)S(1)} %copy-done.5, s32[3,3]{1,0:T(4,128)S(1)} %copy-done.2, bf16[256,256]{1,0:T(8,128)(2,1)S(1)} %copy-done.1, bf16[4,1,2,32,256]{4,3,2,1,0:T(8,128)(2,1)S(1)} %get-tuple-element.34._), custom_call_target="tpu_custom_call" | custom-call | bytes 524288 | tf_op jit(solution)/shard_map/pallas_call | solution.py:24
  34.5 0.2 collective-permute-done.17.refs_6_
  34.7 0.4 %collective-permute-done.14.refs_2_ = bf16[2,2,32,256]{3,2,1,0:T(8,128)(2,1)S(1)} collective-permute-done((bf16[2,2,32,256]{3,2,1,0:T(8,128)(2,1)S(1)}, bf16[2,2,32,256]{3,2,1,0:T(8,128)(2,1)S(1)}, u32[]{:S(2)}, u32[]{:S(2)}) %collective-permute-start.14) | collective-permute-done | bytes 65568 | tf_op jit(solution)/shard_map/ppermute | solution.py:243
  35.1 1.2 %shard_map.89 = bf16[2,1,256,256]{3,2,1,0:T(8,128)(2,1)} custom-call(bf16[256,256]{1,0:T(8,128)(2,1)S(1)} %copy-done, bf16[256,256]{1,0:T(8,128)(2,1)S(1)} %get-tuple-element.35.coupling, f32[2,8,128]{2,1,0:T(8,128)S(1)} %get-tuple-element.36.weights, bf16[4,1,2,32,256]{4,3,2,1,0:T(8,128)(2,1)S(1)} %get-tuple-element.37.keep, ...), custom_call_target="tpu_custom_call" | custom-call | flops 268435456 | bytes 524288 | tf_op jit(solution)/shard_map/pallas_call | solution.py:24
  (32 shorter events, 0.2 us)
Async XLA Ops:
  1.2 5.5 %collective-permute-start = (bf16[4,2,2,32,256]{4,3,2,1,0:T(8,128)(2,1)S(1)}, bf16[4,2,2,32,256]{4,3,2,1,0:T(8,128)(2,1)S(1)}, u32[]{:S(2)}, u32[]{:S(2)}) collective-permute-start(bf16[4,2,2,32,256]{4,3,2,1,0:T(8,128)(2,1)S(1)} %get-tuple-element.26), channel_id=1, source_target_pairs={{0,4},{4,0},{1,5},{5,1},{2,6},{6,2},{3,7},{7,3},{8,12},{12,8},{9,1... | collective-permute-start | bytes 786440 | tf_op jit(solution)/shard_map/ppermute | solution.py:226
  1.7 10.3 %collective-permute-start.1 = (bf16[2,2,32,256]{3,2,1,0:T(8,128)(2,1)S(1)}, bf16[2,2,32,256]{3,2,1,0:T(8,128)(2,1)S(1)}, u32[]{:S(2)}, u32[]{:S(2)}) collective-permute-start(bf16[2,2,32,256]{3,2,1,0:T(8,128)(2,1)S(1)} %get-tuple-element.27), channel_id=1, source_target_pairs={{0,2},{1,25},{2,0},{3,27},{8,10},{9,17},{10,8},{11,19},{16,18},{17... | collective-permute-start | bytes 196616 | tf_op jit(solution)/shard_map/ppermute | solution.py:243
  5.4 8.2 %collective-permute-start.2 = (bf16[2,2,32,256]{3,2,1,0:T(8,128)(2,1)S(1)}, bf16[2,2,32,256]{3,2,1,0:T(8,128)(2,1)S(1)}, u32[]{:S(2)}, u32[]{:S(2)}) collective-permute-start(bf16[2,2,32,256]{3,2,1,0:T(8,128)(2,1)S(1)} %get-tuple-element.28), channel_id=1, source_target_pairs={{0,18},{1,17},{2,16},{3,19},{8,26},{9,25},{10,24},{11,27},{16,2},{... | collective-permute-start | bytes 196616 | tf_op jit(solution)/shard_map/ppermute | solution.py:243
  6.7 11.0 %collective-permute-start.3 = (bf16[2,2,32,256]{3,2,1,0:T(8,128)(2,1)S(1)}, bf16[2,2,32,256]{3,2,1,0:T(8,128)(2,1)S(1)}, u32[]{:S(2)}, u32[]{:S(2)}) collective-permute-start(bf16[2,2,32,256]{3,2,1,0:T(8,128)(2,1)S(1)} %get-tuple-element.30), channel_id=1, source_target_pairs={{0,10},{1,3},{2,8},{3,1},{8,2},{9,11},{10,0},{11,9},{16,26},{17,19... | collective-permute-start | bytes 196616 | tf_op jit(solution)/shard_map/ppermute | solution.py:243
  10.3 9.7 %collective-permute-start.6 = (bf16[2,2,32,256]{3,2,1,0:T(8,128)(2,1)S(1)}, bf16[2,2,32,256]{3,2,1,0:T(8,128)(2,1)S(1)}, u32[]{:S(2)}, u32[]{:S(2)}) collective-permute-start(bf16[2,2,32,256]{3,2,1,0:T(8,128)(2,1)S(1)} %get-tuple-element.31), channel_id=1, source_target_pairs={{0,26},{1,19},{2,24},{3,17},{8,18},{9,27},{10,16},{11,25},{16,10},... | collective-permute-start | bytes 196616 | tf_op jit(solution)/shard_map/ppermute | solution.py:243
  10.3 9.7 %collective-permute-start.7 = (bf16[2,2,32,256]{3,2,1,0:T(8,128)(2,1)S(1)}, bf16[2,2,32,256]{3,2,1,0:T(8,128)(2,1)S(1)}, u32[]{:S(2)}, u32[]{:S(2)}) collective-permute-start(bf16[2,2,32,256]{3,2,1,0:T(8,128)(2,1)S(1)} %get-tuple-element.32), channel_id=1, source_target_pairs={{0,8},{1,9},{2,10},{3,11},{8,0},{9,1},{10,2},{11,3},{16,24},{17,25... | collective-permute-start | bytes 196616 | tf_op jit(solution)/shard_map/ppermute | solution.py:243
  12.0 8.0 %collective-permute-start.8 = (bf16[2,2,32,256]{3,2,1,0:T(8,128)(2,1)S(1)}, bf16[2,2,32,256]{3,2,1,0:T(8,128)(2,1)S(1)}, u32[]{:S(2)}, u32[]{:S(2)}) collective-permute-start(bf16[2,2,32,256]{3,2,1,0:T(8,128)(2,1)S(1)} %get-tuple-element.33), channel_id=1, source_target_pairs={{0,16},{1,11},{2,18},{3,9},{8,24},{9,3},{10,26},{11,1},{16,0},{17,... | collective-permute-start | bytes 196616 | tf_op jit(solution)/shard_map/ppermute | solution.py:243
  13.5 6.4 %collective-permute-start.5 = (bf16[2,2,32,256]{3,2,1,0:T(8,128)(2,1)S(1)}, bf16[2,2,32,256]{3,2,1,0:T(8,128)(2,1)S(1)}, u32[]{:S(2)}, u32[]{:S(2)}) collective-permute-start(bf16[2,2,32,256]{3,2,1,0:T(8,128)(2,1)S(1)} %get-tuple-element.29.refs_2_), channel_id=1, source_target_pairs={{0,24},{1,27},{2,26},{3,25},{8,16},{9,19},{10,18},{11,17},{16,8},{... | collective-permute-start | bytes 196616 | tf_op jit(solution)/shard_map/ppermute | solution.py:243
  17.7 2.3 %collective-permute-start.4 = (bf16[2,2,32,256]{3,2,1,0:T(8,128)(2,1)S(1)}, bf16[2,2,32,256]{3,2,1,0:T(8,128)(2,1)S(1)}, u32[]{:S(2)}, u32[]{:S(2)}) collective-permute-start(bf16[2,2,32,256]{3,2,1,0:T(8,128)(2,1)S(1)} %shard_map.84), channel_id=1, source_target_pairs={{0,4},{4,0},{1,5},{5,1},{2,6},{6,2},{3,7},{7,3},{8,12},{12,8},{9,1... | collective-permute-start | bytes 196616 | tf_op jit(solution)/shard_map/ppermute | solution.py:226
  20.5 3.4 %collective-permute-start.9 = (bf16[4,1,2,32,256]{4,3,2,1,0:T(8,128)(2,1)S(1)}, bf16[4,1,2,32,256]{4,3,2,1,0:T(8,128)(2,1)S(1)}, u32[]{:S(2)}, u32[]{:S(2)}) collective-permute-start(bf16[4,1,2,32,256]{4,3,2,1,0:T(8,128)(2,1)S(1)} %get-tuple-element.34._), channel_id=1, source_target_pairs={{0,4},{4,0},{1,5},{5,1},{2,6},{6,2},{3,7},{7,3},{8,12},{12,8},{9,1... | collective-permute-start | bytes 393224 | tf_op jit(solution)/shard_map/ppermute | solution.py:226
  20.5 8.6 %collective-permute-start.10 = (bf16[2,2,32,256]{3,2,1,0:T(8,128)(2,1)S(1)}, bf16[2,2,32,256]{3,2,1,0:T(8,128)(2,1)S(1)}, u32[]{:S(2)}, u32[]{:S(2)}) collective-permute-start(bf16[2,2,32,256]{3,2,1,0:T(8,128)(2,1)S(1)} %get-tuple-element.38), channel_id=1, source_target_pairs={{0,2},{1,17},{2,0},{3,19},{8,10},{9,25},{10,8},{11,27},{16,18},{17... | collective-permute-start | bytes 196616 | tf_op jit(solution)/shard_map/ppermute | solution.py:243
  21.9 8.8 %collective-permute-start.11 = (bf16[2,2,32,256]{3,2,1,0:T(8,128)(2,1)S(1)}, bf16[2,2,32,256]{3,2,1,0:T(8,128)(2,1)S(1)}, u32[]{:S(2)}, u32[]{:S(2)}) collective-permute-start(bf16[2,2,32,256]{3,2,1,0:T(8,128)(2,1)S(1)} %get-tuple-element.39), channel_id=1, source_target_pairs={{0,10},{1,3},{2,8},{3,1},{8,2},{9,11},{10,0},{11,9},{16,26},{17,19... | collective-permute-start | bytes 196616 | tf_op jit(solution)/shard_map/ppermute | solution.py:243
  23.9 9.8 %collective-permute-start.12 = (bf16[2,2,32,256]{3,2,1,0:T(8,128)(2,1)S(1)}, bf16[2,2,32,256]{3,2,1,0:T(8,128)(2,1)S(1)}, u32[]{:S(2)}, u32[]{:S(2)}) collective-permute-start(bf16[2,2,32,256]{3,2,1,0:T(8,128)(2,1)S(1)} %get-tuple-element.41), channel_id=1, source_target_pairs={{0,26},{1,25},{2,24},{3,27},{8,18},{9,17},{10,16},{11,19},{16,10},... | collective-permute-start | bytes 196616 | tf_op jit(solution)/shard_map/ppermute | solution.py:243
  25.8 8.8 %collective-permute-start.15 = (bf16[2,2,32,256]{3,2,1,0:T(8,128)(2,1)S(1)}, bf16[2,2,32,256]{3,2,1,0:T(8,128)(2,1)S(1)}, u32[]{:S(2)}, u32[]{:S(2)}) collective-permute-start(bf16[2,2,32,256]{3,2,1,0:T(8,128)(2,1)S(1)} %get-tuple-element.42), channel_id=1, source_target_pairs={{0,16},{1,11},{2,18},{3,9},{8,24},{9,3},{10,26},{11,1},{16,0},{17,... | collective-permute-start | bytes 196616 | tf_op jit(solution)/shard_map/ppermute | solution.py:243
  27.3 7.2 %collective-permute-start.16 = (bf16[2,2,32,256]{3,2,1,0:T(8,128)(2,1)S(1)}, bf16[2,2,32,256]{3,2,1,0:T(8,128)(2,1)S(1)}, u32[]{:S(2)}, u32[]{:S(2)}) collective-permute-start(bf16[2,2,32,256]{3,2,1,0:T(8,128)(2,1)S(1)} %get-tuple-element.43), channel_id=1, source_target_pairs={{0,18},{1,9},{2,16},{3,11},{8,26},{9,1},{10,24},{11,3},{16,2},{17,... | collective-permute-start | bytes 196616 | tf_op jit(solution)/shard_map/ppermute | solution.py:243
  29.2 5.5 %collective-permute-start.17 = (bf16[2,2,32,256]{3,2,1,0:T(8,128)(2,1)S(1)}, bf16[2,2,32,256]{3,2,1,0:T(8,128)(2,1)S(1)}, u32[]{:S(2)}, u32[]{:S(2)}) collective-permute-start(bf16[2,2,32,256]{3,2,1,0:T(8,128)(2,1)S(1)} %get-tuple-element.44), channel_id=1, source_target_pairs={{0,24},{1,27},{2,26},{3,25},{8,16},{9,19},{10,18},{11,17},{16,8},{... | collective-permute-start | bytes 196616 | tf_op jit(solution)/shard_map/ppermute | solution.py:243
  30.7 3.0 %copy-start.1 = (bf16[256,256]{1,0:T(8,128)(2,1)S(1)}, bf16[256,256]{1,0:T(8,128)(2,1)}, u32[]{:S(2)}) copy-start(bf16[256,256]{1,0:T(8,128)(2,1)} %link.1) | copy-start | bytes 393220
  30.7 3.0 %copy-start.2 = (s32[3,3]{1,0:T(4,128)S(1)}, s32[3,3]{1,0:T(4,128)}, u32[]{:S(2)}) copy-start(s32[3,3]{1,0:T(4,128)} %mask.1) | copy-start | bytes 112
  30.7 3.1 %copy-start.3 = (s32[1,2]{1,0:T(1,128)S(1)}, s32[1,2]{1,0:T(1,128)}, u32[]{:S(2)}) copy-start(s32[1,2]{1,0:T(1,128)} %blocks.1) | copy-start | bytes 28
  30.7 3.1 %copy-start.4 = (f32[3]{0:T(128)S(1)}, f32[3]{0:T(128)}, u32[]{:S(2)}) copy-start(f32[3]{0:T(128)} %onsite_scale.1) | copy-start | bytes 40
  30.8 3.1 %copy-start.5 = (f32[2]{0:T(128)S(1)}, f32[2]{0:T(128)}, u32[]{:S(2)}) copy-start(f32[2]{0:T(128)} %coupling_scale.1) | copy-start | bytes 28
  30.8 4.3 %collective-permute-start.14 = (bf16[2,2,32,256]{3,2,1,0:T(8,128)(2,1)S(1)}, bf16[2,2,32,256]{3,2,1,0:T(8,128)(2,1)S(1)}, u32[]{:S(2)}, u32[]{:S(2)}) collective-permute-start(bf16[2,2,32,256]{3,2,1,0:T(8,128)(2,1)S(1)} %get-tuple-element.40.refs_2_), channel_id=1, source_target_pairs={{0,8},{1,19},{2,10},{3,17},{8,0},{9,27},{10,2},{11,25},{16,24},{17... | collective-permute-start | bytes 196616 | tf_op jit(solution)/shard_map/ppermute | solution.py:243
  33.7 1.4 %copy-start = (bf16[256,256]{1,0:T(8,128)(2,1)S(1)}, bf16[256,256]{1,0:T(8,128)(2,1)}, u32[]{:S(2)}) copy-start(bf16[256,256]{1,0:T(8,128)(2,1)} %onsite.1) | copy-start | bytes 393220
  33.7 1.4 %collective-permute-start.13 = (bf16[2,2,32,256]{3,2,1,0:T(8,128)(2,1)S(1)}, bf16[2,2,32,256]{3,2,1,0:T(8,128)(2,1)S(1)}, u32[]{:S(2)}, u32[]{:S(2)}) collective-permute-start(bf16[2,2,32,256]{3,2,1,0:T(8,128)(2,1)S(1)} %shard_map.88), channel_id=1, source_target_pairs={{0,4},{4,0},{1,5},{5,1},{2,6},{6,2},{3,7},{7,3},{8,12},{12,8},{9,1... | collective-permute-start | bytes 196616 | tf_op jit(solution)/shard_map/ppermute | solution.py:226

commit v8 on v6

--- a/solution.py
+++ b/solution.py
@@ -110,7 +110,7 @@
             put(crosses, step, block[0], block[1])
 
 
-def lag_body(keep, got, late, *refs):
+def lag_body(_, keep, got, late, *refs):
     blocks, soon = refs[: -4 - SOON], refs[-4 - SOON : -4]
     away, kept, joined, polar = refs[-4:]
     chip, core = lax.axis_index("chip"), lax.axis_index("core")
@@ -255,10 +255,16 @@
             pltpu.SemaphoreType.DMA((2,)),
         ],
     )
+    coupling, weights = run_kernel(
+        weigh_body,
+        [((width, width), BF16), ((2, 8, 128), F32)],
+        (pair_blocks, onsite_scale, coupling_scale, coupling_mask, coupling_block, keep),
+        specs=[SMEM] * 4 + [VMEM] * 2,
+    )
     *soon, away, keep = run_kernel(
         lag_body,
         [block_shape] * SOON + [piles(1)] * 2,
-        spread(soon, away, keep, 0),
+        (weights, *spread(soon, away, keep, 0)),
         scratch=[
             pltpu.VMEM((energies, 2, 2, rows, width), BF16),
             pltpu.VMEM((energies, 2, rows, width), BF16),
@@ -266,12 +272,6 @@
         flops=energies * (energies + 1) * 4 * rows * width,
     )
     parts = spread(soon, away, keep, 1)
-    coupling, weights = run_kernel(
-        weigh_body,
-        [((width, width), BF16), ((2, 8, 128), F32)],
-        (pair_blocks, onsite_scale, coupling_scale, coupling_mask, coupling_block, away),
-        specs=[SMEM] * 4 + [VMEM] * 2,
-    )
     (screened,) = run_kernel(
         screen_body,
         [((2, 1, width, width), BF16)],

time: 36.4 us -> 36.3 us (level)
  no operation moved by 1% of the time
where the time goes in v8:
time: 36.3 us; the launch traced here: 36 us
  starting transfers between devices  25.2 us (69%)
  waiting for transfers between devices  7.01 us (19%)
  Pallas kernels  3.63 us (10%)
    ppermute x14, starting transfers between devices, spread(): came.append(lax.ppermute(block, ('chip', 'half', 'low'), pairs))  24.5 us
    ppermute x14, waiting for transfers between devices, spread(): came.append(lax.ppermute(block, ('chip', 'half', 'low'), pairs))  7 us
    pallas_call x8, Pallas kernels, run_kernel(): pl.pallas_call(body, out_shape=[jax.ShapeDtypeStruct(shape, dtype) for sh...  3.63 us
    ppermute x4, starting transfers between devices, swap_cores(): return lax.ppermute(value, 'core', [(0, 1), (1, 0)])  0.73 us
  transfers between devices with their start and end apart: 18, of which 5 were waited for; matrix products, arithmetic and copies ran while one was open for 0% of the time, Pallas kernels for 2%

profile of v8, /device:TPU:0, one launch (start us, length us, event | category | flops | bytes accessed | tf_op | source)
XLA Modules:
  0.0 36.0 jit_solution(3016061482249743686)
XLA Ops:
  0.0 1.2 %shard_map.82 = (bf16[2,2,32,256]{3,2,1,0:T(8,128)(2,1)S(1)}, bf16[2,2,32,256]{3,2,1,0:T(8,128)(2,1)S(1)}, bf16[4,2,2,32,256]{4,3,2,1,0:T(8,128)(2,1)S(1)}, bf16[4,2,2,32,256]{4,3,2,1,0:T(8,128)(2,1)S(1)}) custom-call(bf16[2,1,256,256]{3,2,1,0:T(8,128)(2,1)} %less.1, bf16[2,1,256,256]{3,2,1,0:T(8,128)(2,1)} %more.1), custom_call_target="tpu_custom_call" | custom-call | bytes 524288 | tf_op jit(solution)/shard_map/pallas_call | solution.py:24
  1.2 0.5 %collective-permute-start = (bf16[4,2,2,32,256]{4,3,2,1,0:T(8,128)(2,1)S(1)}, bf16[4,2,2,32,256]{4,3,2,1,0:T(8,128)(2,1)S(1)}, u32[]{:S(2)}, u32[]{:S(2)}) collective-permute-start(bf16[4,2,2,32,256]{4,3,2,1,0:T(8,128)(2,1)S(1)} %get-tuple-element.28), channel_id=1, source_target_pairs={{0,4},{4,0},{1,5},{5,1},{2,6},{6,2},{3,7},{7,3},{8,12},{12,8},{9,1... | collective-permute-start | bytes 786440 | tf_op jit(solution)/shard_map/ppermute | solution.py:226
  1.7 3.7 %collective-permute-start.1 = (bf16[2,2,32,256]{3,2,1,0:T(8,128)(2,1)S(1)}, bf16[2,2,32,256]{3,2,1,0:T(8,128)(2,1)S(1)}, u32[]{:S(2)}, u32[]{:S(2)}) collective-permute-start(bf16[2,2,32,256]{3,2,1,0:T(8,128)(2,1)S(1)} %get-tuple-element.29), channel_id=1, source_target_pairs={{0,2},{1,25},{2,0},{3,27},{8,10},{9,17},{10,8},{11,19},{16,18},{17... | collective-permute-start | bytes 196616 | tf_op jit(solution)/shard_map/ppermute | solution.py:243
  5.4 1.3 %collective-permute-start.2 = (bf16[2,2,32,256]{3,2,1,0:T(8,128)(2,1)S(1)}, bf16[2,2,32,256]{3,2,1,0:T(8,128)(2,1)S(1)}, u32[]{:S(2)}, u32[]{:S(2)}) collective-permute-start(bf16[2,2,32,256]{3,2,1,0:T(8,128)(2,1)S(1)} %get-tuple-element.30), channel_id=1, source_target_pairs={{0,18},{1,17},{2,16},{3,19},{8,26},{9,25},{10,24},{11,27},{16,2},{... | collective-permute-start | bytes 196616 | tf_op jit(solution)/shard_map/ppermute | solution.py:243
  6.7 3.6 %collective-permute-start.3 = (bf16[2,2,32,256]{3,2,1,0:T(8,128)(2,1)S(1)}, bf16[2,2,32,256]{3,2,1,0:T(8,128)(2,1)S(1)}, u32[]{:S(2)}, u32[]{:S(2)}) collective-permute-start(bf16[2,2,32,256]{3,2,1,0:T(8,128)(2,1)S(1)} %get-tuple-element.32), channel_id=1, source_target_pairs={{0,10},{1,3},{2,8},{3,1},{8,2},{9,11},{10,0},{11,9},{16,26},{17,19... | collective-permute-start | bytes 196616 | tf_op jit(solution)/shard_map/ppermute | solution.py:243
  10.3 1.7 %collective-permute-start.7 = (bf16[2,2,32,256]{3,2,1,0:T(8,128)(2,1)S(1)}, bf16[2,2,32,256]{3,2,1,0:T(8,128)(2,1)S(1)}, u32[]{:S(2)}, u32[]{:S(2)}) collective-permute-start(bf16[2,2,32,256]{3,2,1,0:T(8,128)(2,1)S(1)} %get-tuple-element.34), channel_id=1, source_target_pairs={{0,8},{1,19},{2,10},{3,17},{8,0},{9,27},{10,2},{11,25},{16,24},{17... | collective-permute-start | bytes 196616 | tf_op jit(solution)/shard_map/ppermute | solution.py:243
  12.0 1.5 %collective-permute-start.8 = (bf16[2,2,32,256]{3,2,1,0:T(8,128)(2,1)S(1)}, bf16[2,2,32,256]{3,2,1,0:T(8,128)(2,1)S(1)}, u32[]{:S(2)}, u32[]{:S(2)}) collective-permute-start(bf16[2,2,32,256]{3,2,1,0:T(8,128)(2,1)S(1)} %get-tuple-element.35), channel_id=1, source_target_pairs={{0,16},{1,11},{2,18},{3,9},{8,24},{9,3},{10,26},{11,1},{16,0},{17,... | collective-permute-start | bytes 196616 | tf_op jit(solution)/shard_map/ppermute | solution.py:243
  13.6 1.4 %collective-permute-start.5 = (bf16[2,2,32,256]{3,2,1,0:T(8,128)(2,1)S(1)}, bf16[2,2,32,256]{3,2,1,0:T(8,128)(2,1)S(1)}, u32[]{:S(2)}, u32[]{:S(2)}) collective-permute-start(bf16[2,2,32,256]{3,2,1,0:T(8,128)(2,1)S(1)} %get-tuple-element.31.refs_2_), channel_id=1, source_target_pairs={{0,24},{1,27},{2,26},{3,25},{8,16},{9,19},{10,18},{11,17},{16,8},{... | collective-permute-start | bytes 196616 | tf_op jit(solution)/shard_map/ppermute | solution.py:243
  15.1 0.7 %shard_map.83 = (bf16[256,256]{1,0:T(8,128)(2,1)S(1)}, f32[2,8,128]{2,1,0:T(8,128)S(1)}) custom-call(s32[1,2]{1,0:T(1,128)S(1)} %copy-done.3, f32[3]{0:T(128)S(1)} %copy-done.4, f32[2]{0:T(128)S(1)} %copy-done.5, s32[3,3]{1,0:T(4,128)S(1)} %copy-done.2, bf16[256,256]{1,0:T(8,128)(2,1)S(1)} %copy-done.1, bf16[4,2,2,32,256]{4,3,2,1,0:T(8,128)(2,1)S(1)} %get-tuple-element.25._.keep), custom_call_target="tpu_custom_call" | custom-call | bytes 524288 | tf_op jit(solution)/shard_map/pallas_call | solution.py:24
  15.8 4.1 %collective-permute-done.6.refs_4_ = bf16[2,2,32,256]{3,2,1,0:T(8,128)(2,1)S(1)} collective-permute-done((bf16[2,2,32,256]{3,2,1,0:T(8,128)(2,1)S(1)}, bf16[2,2,32,256]{3,2,1,0:T(8,128)(2,1)S(1)}, u32[]{:S(2)}, u32[]{:S(2)}) %collective-permute-start.6) | collective-permute-done | bytes 65568 | tf_op jit(solution)/shard_map/ppermute | solution.py:243
  20.0 0.5 %shard_map.86 = (bf16[2,2,32,256]{3,2,1,0:T(8,128)(2,1)S(1)}, bf16[2,2,32,256]{3,2,1,0:T(8,128)(2,1)S(1)}, bf16[4,1,2,32,256]{4,3,2,1,0:T(8,128)(2,1)S(1)}, bf16[4,1,2,32,256]{4,3,2,1,0:T(8,128)(2,1)S(1)}) custom-call(f32[2,8,128]{2,1,0:T(8,128)S(1)} %get-tuple-element.27._.weights, bf16[4,2,2,32,256]{4,3,2,1,0:T(8,128)(2,1)S(1)} %get-tuple-element.25._.keep, ...), custom_call_target="tpu_custom_call" | custom-call | flops 2359296 | bytes 524288 | tf_op jit(solution)/shard_map/pallas_call | solution.py:24
  20.5 0.1 collective-permute-start.9
  20.5 1.5 %collective-permute-start.10 = (bf16[2,2,32,256]{3,2,1,0:T(8,128)(2,1)S(1)}, bf16[2,2,32,256]{3,2,1,0:T(8,128)(2,1)S(1)}, u32[]{:S(2)}, u32[]{:S(2)}) collective-permute-start(bf16[2,2,32,256]{3,2,1,0:T(8,128)(2,1)S(1)} %get-tuple-element.38), channel_id=1, source_target_pairs={{0,2},{1,17},{2,0},{3,19},{8,10},{9,25},{10,8},{11,27},{16,18},{17... | collective-permute-start | bytes 196616 | tf_op jit(solution)/shard_map/ppermute | solution.py:243
  22.0 1.6 %collective-permute-start.11 = (bf16[2,2,32,256]{3,2,1,0:T(8,128)(2,1)S(1)}, bf16[2,2,32,256]{3,2,1,0:T(8,128)(2,1)S(1)}, u32[]{:S(2)}, u32[]{:S(2)}) collective-permute-start(bf16[2,2,32,256]{3,2,1,0:T(8,128)(2,1)S(1)} %get-tuple-element.39), channel_id=1, source_target_pairs={{0,10},{1,3},{2,8},{3,1},{8,2},{9,11},{10,0},{11,9},{16,26},{17,19... | collective-permute-start | bytes 196616 | tf_op jit(solution)/shard_map/ppermute | solution.py:243
  23.6 2.2 %collective-permute-start.12 = (bf16[2,2,32,256]{3,2,1,0:T(8,128)(2,1)S(1)}, bf16[2,2,32,256]{3,2,1,0:T(8,128)(2,1)S(1)}, u32[]{:S(2)}, u32[]{:S(2)}) collective-permute-start(bf16[2,2,32,256]{3,2,1,0:T(8,128)(2,1)S(1)} %get-tuple-element.41), channel_id=1, source_target_pairs={{0,26},{1,25},{2,24},{3,27},{8,18},{9,17},{10,16},{11,19},{16,10},... | collective-permute-start | bytes 196616 | tf_op jit(solution)/shard_map/ppermute | solution.py:243
  25.9 1.5 %collective-permute-start.15 = (bf16[2,2,32,256]{3,2,1,0:T(8,128)(2,1)S(1)}, bf16[2,2,32,256]{3,2,1,0:T(8,128)(2,1)S(1)}, u32[]{:S(2)}, u32[]{:S(2)}) collective-permute-start(bf16[2,2,32,256]{3,2,1,0:T(8,128)(2,1)S(1)} %get-tuple-element.42), channel_id=1, source_target_pairs={{0,16},{1,9},{2,18},{3,11},{8,24},{9,1},{10,26},{11,3},{16,0},{17,... | collective-permute-start | bytes 196616 | tf_op jit(solution)/shard_map/ppermute | solution.py:243
  27.4 1.8 %collective-permute-start.16 = (bf16[2,2,32,256]{3,2,1,0:T(8,128)(2,1)S(1)}, bf16[2,2,32,256]{3,2,1,0:T(8,128)(2,1)S(1)}, u32[]{:S(2)}, u32[]{:S(2)}) collective-permute-start(bf16[2,2,32,256]{3,2,1,0:T(8,128)(2,1)S(1)} %get-tuple-element.43), channel_id=1, source_target_pairs={{0,18},{1,11},{2,16},{3,9},{8,26},{9,3},{10,24},{11,1},{16,2},{17,... | collective-permute-start | bytes 196616 | tf_op jit(solution)/shard_map/ppermute | solution.py:243
  29.2 1.3 %collective-permute-start.17 = (bf16[2,2,32,256]{3,2,1,0:T(8,128)(2,1)S(1)}, bf16[2,2,32,256]{3,2,1,0:T(8,128)(2,1)S(1)}, u32[]{:S(2)}, u32[]{:S(2)}) collective-permute-start(bf16[2,2,32,256]{3,2,1,0:T(8,128)(2,1)S(1)} %get-tuple-element.44), channel_id=1, source_target_pairs={{0,24},{1,27},{2,26},{3,25},{8,16},{9,19},{10,18},{11,17},{16,8},{... | collective-permute-start | bytes 196616 | tf_op jit(solution)/shard_map/ppermute | solution.py:243
  30.5 1.4 %collective-permute-start.14 = (bf16[2,2,32,256]{3,2,1,0:T(8,128)(2,1)S(1)}, bf16[2,2,32,256]{3,2,1,0:T(8,128)(2,1)S(1)}, u32[]{:S(2)}, u32[]{:S(2)}) collective-permute-start(bf16[2,2,32,256]{3,2,1,0:T(8,128)(2,1)S(1)} %get-tuple-element.40.refs_2_), channel_id=1, source_target_pairs={{0,8},{1,19},{2,10},{3,17},{8,0},{9,27},{10,2},{11,25},{16,24},{17... | collective-permute-start | bytes 196616 | tf_op jit(solution)/shard_map/ppermute | solution.py:243
  31.9 1.6 %collective-permute-done.15.refs_4_ = bf16[2,2,32,256]{3,2,1,0:T(8,128)(2,1)S(1)} collective-permute-done((bf16[2,2,32,256]{3,2,1,0:T(8,128)(2,1)S(1)}, bf16[2,2,32,256]{3,2,1,0:T(8,128)(2,1)S(1)}, u32[]{:S(2)}, u32[]{:S(2)}) %collective-permute-start.15) | collective-permute-done | bytes 65568 | tf_op jit(solution)/shard_map/ppermute | solution.py:243
  33.5 0.7 %collective-permute-done.16.refs_5_ = bf16[2,2,32,256]{3,2,1,0:T(8,128)(2,1)S(1)} collective-permute-done((bf16[2,2,32,256]{3,2,1,0:T(8,128)(2,1)S(1)}, bf16[2,2,32,256]{3,2,1,0:T(8,128)(2,1)S(1)}, u32[]{:S(2)}, u32[]{:S(2)}) %collective-permute-start.16) | collective-permute-done | bytes 65568 | tf_op jit(solution)/shard_map/ppermute | solution.py:243
  34.2 0.2 collective-permute-done.17.refs_6_
  34.4 0.4 %collective-permute-done.14.refs_2_ = bf16[2,2,32,256]{3,2,1,0:T(8,128)(2,1)S(1)} collective-permute-done((bf16[2,2,32,256]{3,2,1,0:T(8,128)(2,1)S(1)}, bf16[2,2,32,256]{3,2,1,0:T(8,128)(2,1)S(1)}, u32[]{:S(2)}, u32[]{:S(2)}) %collective-permute-start.14) | collective-permute-done | bytes 65568 | tf_op jit(solution)/shard_map/ppermute | solution.py:243
  34.8 1.2 %shard_map.89 = bf16[2,1,256,256]{3,2,1,0:T(8,128)(2,1)} custom-call(bf16[256,256]{1,0:T(8,128)(2,1)S(1)} %copy-done, bf16[256,256]{1,0:T(8,128)(2,1)S(1)} %get-tuple-element.26.coupling, f32[2,8,128]{2,1,0:T(8,128)S(1)} %get-tuple-element.27._.weights, bf16[4,1,2,32,256]{4,3,2,1,0:T(8,128)(2,1)S(1)} %get-tuple-element.36.keep, ...), custom_call_target="tpu_custom_call" | custom-call | flops 268435456 | bytes 524288 | tf_op jit(solution)/shard_map/pallas_call | solution.py:24
  (32 shorter events, 0.3 us)
Async XLA Ops:
  1.2 5.5 %collective-permute-start = (bf16[4,2,2,32,256]{4,3,2,1,0:T(8,128)(2,1)S(1)}, bf16[4,2,2,32,256]{4,3,2,1,0:T(8,128)(2,1)S(1)}, u32[]{:S(2)}, u32[]{:S(2)}) collective-permute-start(bf16[4,2,2,32,256]{4,3,2,1,0:T(8,128)(2,1)S(1)} %get-tuple-element.28), channel_id=1, source_target_pairs={{0,4},{4,0},{1,5},{5,1},{2,6},{6,2},{3,7},{7,3},{8,12},{12,8},{9,1... | collective-permute-start | bytes 786440 | tf_op jit(solution)/shard_map/ppermute | solution.py:226
  1.7 10.3 %collective-permute-start.1 = (bf16[2,2,32,256]{3,2,1,0:T(8,128)(2,1)S(1)}, bf16[2,2,32,256]{3,2,1,0:T(8,128)(2,1)S(1)}, u32[]{:S(2)}, u32[]{:S(2)}) collective-permute-start(bf16[2,2,32,256]{3,2,1,0:T(8,128)(2,1)S(1)} %get-tuple-element.29), channel_id=1, source_target_pairs={{0,2},{1,25},{2,0},{3,27},{8,10},{9,17},{10,8},{11,19},{16,18},{17... | collective-permute-start | bytes 196616 | tf_op jit(solution)/shard_map/ppermute | solution.py:243
  5.4 8.2 %collective-permute-start.2 = (bf16[2,2,32,256]{3,2,1,0:T(8,128)(2,1)S(1)}, bf16[2,2,32,256]{3,2,1,0:T(8,128)(2,1)S(1)}, u32[]{:S(2)}, u32[]{:S(2)}) collective-permute-start(bf16[2,2,32,256]{3,2,1,0:T(8,128)(2,1)S(1)} %get-tuple-element.30), channel_id=1, source_target_pairs={{0,18},{1,17},{2,16},{3,19},{8,26},{9,25},{10,24},{11,27},{16,2},{... | collective-permute-start | bytes 196616 | tf_op jit(solution)/shard_map/ppermute | solution.py:243
  6.7 8.3 %collective-permute-start.3 = (bf16[2,2,32,256]{3,2,1,0:T(8,128)(2,1)S(1)}, bf16[2,2,32,256]{3,2,1,0:T(8,128)(2,1)S(1)}, u32[]{:S(2)}, u32[]{:S(2)}) collective-permute-start(bf16[2,2,32,256]{3,2,1,0:T(8,128)(2,1)S(1)} %get-tuple-element.32), channel_id=1, source_target_pairs={{0,10},{1,3},{2,8},{3,1},{8,2},{9,11},{10,0},{11,9},{16,26},{17,19... | collective-permute-start | bytes 196616 | tf_op jit(solution)/shard_map/ppermute | solution.py:243
  10.3 9.7 %collective-permute-start.6 = (bf16[2,2,32,256]{3,2,1,0:T(8,128)(2,1)S(1)}, bf16[2,2,32,256]{3,2,1,0:T(8,128)(2,1)S(1)}, u32[]{:S(2)}, u32[]{:S(2)}) collective-permute-start(bf16[2,2,32,256]{3,2,1,0:T(8,128)(2,1)S(1)} %get-tuple-element.33), channel_id=1, source_target_pairs={{0,26},{1,9},{2,24},{3,11},{8,18},{9,1},{10,16},{11,3},{16,10},{17... | collective-permute-start | bytes 196616 | tf_op jit(solution)/shard_map/ppermute | solution.py:243
  10.3 9.7 %collective-permute-start.7 = (bf16[2,2,32,256]{3,2,1,0:T(8,128)(2,1)S(1)}, bf16[2,2,32,256]{3,2,1,0:T(8,128)(2,1)S(1)}, u32[]{:S(2)}, u32[]{:S(2)}) collective-permute-start(bf16[2,2,32,256]{3,2,1,0:T(8,128)(2,1)S(1)} %get-tuple-element.34), channel_id=1, source_target_pairs={{0,8},{1,19},{2,10},{3,17},{8,0},{9,27},{10,2},{11,25},{16,24},{17... | collective-permute-start | bytes 196616 | tf_op jit(solution)/shard_map/ppermute | solution.py:243
  12.0 8.0 %collective-permute-start.8 = (bf16[2,2,32,256]{3,2,1,0:T(8,128)(2,1)S(1)}, bf16[2,2,32,256]{3,2,1,0:T(8,128)(2,1)S(1)}, u32[]{:S(2)}, u32[]{:S(2)}) collective-permute-start(bf16[2,2,32,256]{3,2,1,0:T(8,128)(2,1)S(1)} %get-tuple-element.35), channel_id=1, source_target_pairs={{0,16},{1,11},{2,18},{3,9},{8,24},{9,3},{10,26},{11,1},{16,0},{17,... | collective-permute-start | bytes 196616 | tf_op jit(solution)/shard_map/ppermute | solution.py:243
  13.5 1.6 %copy-start.1 = (bf16[256,256]{1,0:T(8,128)(2,1)S(1)}, bf16[256,256]{1,0:T(8,128)(2,1)}, u32[]{:S(2)}) copy-start(bf16[256,256]{1,0:T(8,128)(2,1)} %link.1) | copy-start | bytes 393220
  13.5 1.6 %copy-start.2 = (s32[3,3]{1,0:T(4,128)S(1)}, s32[3,3]{1,0:T(4,128)}, u32[]{:S(2)}) copy-start(s32[3,3]{1,0:T(4,128)} %mask.1) | copy-start | bytes 112
  13.5 1.6 %copy-start.3 = (s32[1,2]{1,0:T(1,128)S(1)}, s32[1,2]{1,0:T(1,128)}, u32[]{:S(2)}) copy-start(s32[1,2]{1,0:T(1,128)} %blocks.1) | copy-start | bytes 28
  13.5 1.6 %copy-start.4 = (f32[3]{0:T(128)S(1)}, f32[3]{0:T(128)}, u32[]{:S(2)}) copy-start(f32[3]{0:T(128)} %onsite_scale.1) | copy-start | bytes 40
  13.6 1.6 %copy-start.5 = (f32[2]{0:T(128)S(1)}, f32[2]{0:T(128)}, u32[]{:S(2)}) copy-start(f32[2]{0:T(128)} %coupling_scale.1) | copy-start | bytes 28
  13.6 6.4 %collective-permute-start.5 = (bf16[2,2,32,256]{3,2,1,0:T(8,128)(2,1)S(1)}, bf16[2,2,32,256]{3,2,1,0:T(8,128)(2,1)S(1)}, u32[]{:S(2)}, u32[]{:S(2)}) collective-permute-start(bf16[2,2,32,256]{3,2,1,0:T(8,128)(2,1)S(1)} %get-tuple-element.31.refs_2_), channel_id=1, source_target_pairs={{0,24},{1,27},{2,26},{3,25},{8,16},{9,19},{10,18},{11,17},{16,8},{... | collective-permute-start | bytes 196616 | tf_op jit(solution)/shard_map/ppermute | solution.py:243
  15.0 5.0 %collective-permute-start.4 = (bf16[2,2,32,256]{3,2,1,0:T(8,128)(2,1)S(1)}, bf16[2,2,32,256]{3,2,1,0:T(8,128)(2,1)S(1)}, u32[]{:S(2)}, u32[]{:S(2)}) collective-permute-start(bf16[2,2,32,256]{3,2,1,0:T(8,128)(2,1)S(1)} %shard_map.85), channel_id=1, source_target_pairs={{0,4},{4,0},{1,5},{5,1},{2,6},{6,2},{3,7},{7,3},{8,12},{12,8},{9,1... | collective-permute-start | bytes 196616 | tf_op jit(solution)/shard_map/ppermute | solution.py:226
  20.5 3.1 %collective-permute-start.9 = (bf16[4,1,2,32,256]{4,3,2,1,0:T(8,128)(2,1)S(1)}, bf16[4,1,2,32,256]{4,3,2,1,0:T(8,128)(2,1)S(1)}, u32[]{:S(2)}, u32[]{:S(2)}) collective-permute-start(bf16[4,1,2,32,256]{4,3,2,1,0:T(8,128)(2,1)S(1)} %get-tuple-element.37), channel_id=1, source_target_pairs={{0,4},{4,0},{1,5},{5,1},{2,6},{6,2},{3,7},{7,3},{8,12},{12,8},{9,1... | collective-permute-start | bytes 393224 | tf_op jit(solution)/shard_map/ppermute | solution.py:226
  20.5 8.6 %collective-permute-start.10 = (bf16[2,2,32,256]{3,2,1,0:T(8,128)(2,1)S(1)}, bf16[2,2,32,256]{3,2,1,0:T(8,128)(2,1)S(1)}, u32[]{:S(2)}, u32[]{:S(2)}) collective-permute-start(bf16[2,2,32,256]{3,2,1,0:T(8,128)(2,1)S(1)} %get-tuple-element.38), channel_id=1, source_target_pairs={{0,2},{1,17},{2,0},{3,19},{8,10},{9,25},{10,8},{11,27},{16,18},{17... | collective-permute-start | bytes 196616 | tf_op jit(solution)/shard_map/ppermute | solution.py:243
  22.0 8.5 %collective-permute-start.11 = (bf16[2,2,32,256]{3,2,1,0:T(8,128)(2,1)S(1)}, bf16[2,2,32,256]{3,2,1,0:T(8,128)(2,1)S(1)}, u32[]{:S(2)}, u32[]{:S(2)}) collective-permute-start(bf16[2,2,32,256]{3,2,1,0:T(8,128)(2,1)S(1)} %get-tuple-element.39), channel_id=1, source_target_pairs={{0,10},{1,3},{2,8},{3,1},{8,2},{9,11},{10,0},{11,9},{16,26},{17,19... | collective-permute-start | bytes 196616 | tf_op jit(solution)/shard_map/ppermute | solution.py:243
  23.6 8.2 %collective-permute-start.12 = (bf16[2,2,32,256]{3,2,1,0:T(8,128)(2,1)S(1)}, bf16[2,2,32,256]{3,2,1,0:T(8,128)(2,1)S(1)}, u32[]{:S(2)}, u32[]{:S(2)}) collective-permute-start(bf16[2,2,32,256]{3,2,1,0:T(8,128)(2,1)S(1)} %get-tuple-element.41), channel_id=1, source_target_pairs={{0,26},{1,25},{2,24},{3,27},{8,18},{9,17},{10,16},{11,19},{16,10},... | collective-permute-start | bytes 196616 | tf_op jit(solution)/shard_map/ppermute | solution.py:243
  25.9 7.6 %collective-permute-start.15 = (bf16[2,2,32,256]{3,2,1,0:T(8,128)(2,1)S(1)}, bf16[2,2,32,256]{3,2,1,0:T(8,128)(2,1)S(1)}, u32[]{:S(2)}, u32[]{:S(2)}) collective-permute-start(bf16[2,2,32,256]{3,2,1,0:T(8,128)(2,1)S(1)} %get-tuple-element.42), channel_id=1, source_target_pairs={{0,16},{1,9},{2,18},{3,11},{8,24},{9,1},{10,26},{11,3},{16,0},{17,... | collective-permute-start | bytes 196616 | tf_op jit(solution)/shard_map/ppermute | solution.py:243
  27.4 6.9 %collective-permute-start.16 = (bf16[2,2,32,256]{3,2,1,0:T(8,128)(2,1)S(1)}, bf16[2,2,32,256]{3,2,1,0:T(8,128)(2,1)S(1)}, u32[]{:S(2)}, u32[]{:S(2)}) collective-permute-start(bf16[2,2,32,256]{3,2,1,0:T(8,128)(2,1)S(1)} %get-tuple-element.43), channel_id=1, source_target_pairs={{0,18},{1,11},{2,16},{3,9},{8,26},{9,3},{10,24},{11,1},{16,2},{17,... | collective-permute-start | bytes 196616 | tf_op jit(solution)/shard_map/ppermute | solution.py:243
  29.2 5.2 %collective-permute-start.17 = (bf16[2,2,32,256]{3,2,1,0:T(8,128)(2,1)S(1)}, bf16[2,2,32,256]{3,2,1,0:T(8,128)(2,1)S(1)}, u32[]{:S(2)}, u32[]{:S(2)}) collective-permute-start(bf16[2,2,32,256]{3,2,1,0:T(8,128)(2,1)S(1)} %get-tuple-element.44), channel_id=1, source_target_pairs={{0,24},{1,27},{2,26},{3,25},{8,16},{9,19},{10,18},{11,17},{16,8},{... | collective-permute-start | bytes 196616 | tf_op jit(solution)/shard_map/ppermute | solution.py:243
  30.5 4.3 %copy-start = (bf16[256,256]{1,0:T(8,128)(2,1)S(1)}, bf16[256,256]{1,0:T(8,128)(2,1)}, u32[]{:S(2)}) copy-start(bf16[256,256]{1,0:T(8,128)(2,1)} %onsite.1) | copy-start | bytes 393220
  30.5 4.3 %collective-permute-start.14 = (bf16[2,2,32,256]{3,2,1,0:T(8,128)(2,1)S(1)}, bf16[2,2,32,256]{3,2,1,0:T(8,128)(2,1)S(1)}, u32[]{:S(2)}, u32[]{:S(2)}) collective-permute-start(bf16[2,2,32,256]{3,2,1,0:T(8,128)(2,1)S(1)} %get-tuple-element.40.refs_2_), channel_id=1, source_target_pairs={{0,8},{1,19},{2,10},{3,17},{8,0},{9,27},{10,2},{11,25},{16,24},{17... | collective-permute-start | bytes 196616 | tf_op jit(solution)/shard_map/ppermute | solution.py:243
  31.9 2.9 %collective-permute-start.13 = (bf16[2,2,32,256]{3,2,1,0:T(8,128)(2,1)S(1)}, bf16[2,2,32,256]{3,2,1,0:T(8,128)(2,1)S(1)}, u32[]{:S(2)}, u32[]{:S(2)}) collective-permute-start(bf16[2,2,32,256]{3,2,1,0:T(8,128)(2,1)S(1)} %shard_map.88), channel_id=1, source_target_pairs={{0,4},{4,0},{1,5},{5,1},{2,6},{6,2},{3,7},{7,3},{8,12},{12,8},{9,1... | collective-permute-start | bytes 196616 | tf_op jit(solution)/shard_map/ppermute | solution.py:226

commit v9 on v8

--- a/solution.py
+++ b/solution.py
@@ -118,8 +118,8 @@
     chips = energies // 2
 
     def put(crosses, step, mine, theirs):
-        joined[2 * (chip ^ step) + core, crosses] = mine
-        joined[2 * (chip ^ step) + 1 - core, crosses] = theirs
+        joined[2 * (chip ^ step) + core, crosses] = mine.astype(F32)
+        joined[2 * (chip ^ step) + 1 - core, crosses] = theirs.astype(F32)
 
     put(0, 0, keep[0, 0], got[0, 0])
     sort_blocks(chips, 0, blocks, late, put)
@@ -130,10 +130,10 @@
             for lag in range(energies):
                 real = imag = jnp.zeros((16, 128), F32)
                 for late in range(lag, energies):
-                    lr = joined[(late, 0, 0) + at].astype(F32)
-                    li = joined[(late, 0, 1) + at].astype(F32)
-                    mr = joined[(late - lag, 1, 0) + at].astype(F32)
-                    mi = joined[(late - lag, 1, 1) + at].astype(F32)
+                    lr = joined[(late, 0, 0) + at]
+                    li = joined[(late, 0, 1) + at]
+                    mr = joined[(late - lag, 1, 0) + at]
+                    mi = joined[(late - lag, 1, 1) + at]
                     real += lr * mr - li * mi
                     imag += lr * mi + li * mr
                 polar[(lag, 0) + at] = (factor * imag).astype(BF16)
@@ -266,7 +266,7 @@
         [block_shape] * SOON + [piles(1)] * 2,
         (weights, *spread(soon, away, keep, 0)),
         scratch=[
-            pltpu.VMEM((energies, 2, 2, rows, width), BF16),
+            pltpu.VMEM((energies, 2, 2, rows, width), F32),
             pltpu.VMEM((energies, 2, rows, width), BF16),
         ],
         flops=energies * (energies + 1) * 4 * rows * width,

time: 36.3 us -> 36.3 us (level)
  no operation moved by 1% of the time
where the time goes in v9:
time: 36.3 us; the launch traced here: 36 us
  starting transfers between devices  25.2 us (69%)
  waiting for transfers between devices  7.01 us (19%)
  Pallas kernels  3.64 us (10%)
    ppermute x14, starting transfers between devices, spread(): came.append(lax.ppermute(block, ('chip', 'half', 'low'), pairs))  24.5 us
    ppermute x14, waiting for transfers between devices, spread(): came.append(lax.ppermute(block, ('chip', 'half', 'low'), pairs))  7 us
    pallas_call x8, Pallas kernels, run_kernel(): pl.pallas_call(body, out_shape=[jax.ShapeDtypeStruct(shape, dtype) for sh...  3.64 us
    ppermute x4, starting transfers between devices, swap_cores(): return lax.ppermute(value, 'core', [(0, 1), (1, 0)])  0.73 us
  transfers between devices with their start and end apart: 18, of which 5 were waited for; matrix products, arithmetic and copies ran while one was open for 0% of the time, Pallas kernels for 2%

profile of v9, /device:TPU:0, one launch (start us, length us, event | category | flops | bytes accessed | tf_op | source)
XLA Modules:
  0.0 36.0 jit_solution(3668432708936562033)
XLA Ops:
  0.0 1.2 %shard_map.82 = (bf16[2,2,32,256]{3,2,1,0:T(8,128)(2,1)S(1)}, bf16[2,2,32,256]{3,2,1,0:T(8,128)(2,1)S(1)}, bf16[4,2,2,32,256]{4,3,2,1,0:T(8,128)(2,1)S(1)}, bf16[4,2,2,32,256]{4,3,2,1,0:T(8,128)(2,1)S(1)}) custom-call(bf16[2,1,256,256]{3,2,1,0:T(8,128)(2,1)} %less.1, bf16[2,1,256,256]{3,2,1,0:T(8,128)(2,1)} %more.1), custom_call_target="tpu_custom_call" | custom-call | bytes 524288 | tf_op jit(solution)/shard_map/pallas_call | solution.py:24
  1.2 0.5 %collective-permute-start = (bf16[4,2,2,32,256]{4,3,2,1,0:T(8,128)(2,1)S(1)}, bf16[4,2,2,32,256]{4,3,2,1,0:T(8,128)(2,1)S(1)}, u32[]{:S(2)}, u32[]{:S(2)}) collective-permute-start(bf16[4,2,2,32,256]{4,3,2,1,0:T(8,128)(2,1)S(1)} %get-tuple-element.28), channel_id=1, source_target_pairs={{0,4},{4,0},{1,5},{5,1},{2,6},{6,2},{3,7},{7,3},{8,12},{12,8},{9,1... | collective-permute-start | bytes 786440 | tf_op jit(solution)/shard_map/ppermute | solution.py:226
  1.7 3.7 %collective-permute-start.1 = (bf16[2,2,32,256]{3,2,1,0:T(8,128)(2,1)S(1)}, bf16[2,2,32,256]{3,2,1,0:T(8,128)(2,1)S(1)}, u32[]{:S(2)}, u32[]{:S(2)}) collective-permute-start(bf16[2,2,32,256]{3,2,1,0:T(8,128)(2,1)S(1)} %get-tuple-element.29), channel_id=1, source_target_pairs={{0,2},{1,25},{2,0},{3,27},{8,10},{9,17},{10,8},{11,19},{16,18},{17... | collective-permute-start | bytes 196616 | tf_op jit(solution)/shard_map/ppermute | solution.py:243
  5.4 1.3 %collective-permute-start.2 = (bf16[2,2,32,256]{3,2,1,0:T(8,128)(2,1)S(1)}, bf16[2,2,32,256]{3,2,1,0:T(8,128)(2,1)S(1)}, u32[]{:S(2)}, u32[]{:S(2)}) collective-permute-start(bf16[2,2,32,256]{3,2,1,0:T(8,128)(2,1)S(1)} %get-tuple-element.30), channel_id=1, source_target_pairs={{0,18},{1,17},{2,16},{3,19},{8,26},{9,25},{10,24},{11,27},{16,2},{... | collective-permute-start | bytes 196616 | tf_op jit(solution)/shard_map/ppermute | solution.py:243
  6.7 3.6 %collective-permute-start.3 = (bf16[2,2,32,256]{3,2,1,0:T(8,128)(2,1)S(1)}, bf16[2,2,32,256]{3,2,1,0:T(8,128)(2,1)S(1)}, u32[]{:S(2)}, u32[]{:S(2)}) collective-permute-start(bf16[2,2,32,256]{3,2,1,0:T(8,128)(2,1)S(1)} %get-tuple-element.32), channel_id=1, source_target_pairs={{0,10},{1,3},{2,8},{3,1},{8,2},{9,11},{10,0},{11,9},{16,26},{17,19... | collective-permute-start | bytes 196616 | tf_op jit(solution)/shard_map/ppermute | solution.py:243
  10.3 1.7 %collective-permute-start.7 = (bf16[2,2,32,256]{3,2,1,0:T(8,128)(2,1)S(1)}, bf16[2,2,32,256]{3,2,1,0:T(8,128)(2,1)S(1)}, u32[]{:S(2)}, u32[]{:S(2)}) collective-permute-start(bf16[2,2,32,256]{3,2,1,0:T(8,128)(2,1)S(1)} %get-tuple-element.34), channel_id=1, source_target_pairs={{0,8},{1,19},{2,10},{3,17},{8,0},{9,27},{10,2},{11,25},{16,24},{17... | collective-permute-start | bytes 196616 | tf_op jit(solution)/shard_map/ppermute | solution.py:243
  12.0 1.5 %collective-permute-start.8 = (bf16[2,2,32,256]{3,2,1,0:T(8,128)(2,1)S(1)}, bf16[2,2,32,256]{3,2,1,0:T(8,128)(2,1)S(1)}, u32[]{:S(2)}, u32[]{:S(2)}) collective-permute-start(bf16[2,2,32,256]{3,2,1,0:T(8,128)(2,1)S(1)} %get-tuple-element.35), channel_id=1, source_target_pairs={{0,16},{1,11},{2,18},{3,9},{8,24},{9,3},{10,26},{11,1},{16,0},{17,... | collective-permute-start | bytes 196616 | tf_op jit(solution)/shard_map/ppermute | solution.py:243
  13.6 1.4 %collective-permute-start.5 = (bf16[2,2,32,256]{3,2,1,0:T(8,128)(2,1)S(1)}, bf16[2,2,32,256]{3,2,1,0:T(8,128)(2,1)S(1)}, u32[]{:S(2)}, u32[]{:S(2)}) collective-permute-start(bf16[2,2,32,256]{3,2,1,0:T(8,128)(2,1)S(1)} %get-tuple-element.31.refs_2_), channel_id=1, source_target_pairs={{0,24},{1,27},{2,26},{3,25},{8,16},{9,19},{10,18},{11,17},{16,8},{... | collective-permute-start | bytes 196616 | tf_op jit(solution)/shard_map/ppermute | solution.py:243
  15.0 0.1 collective-permute-start.4
  15.1 0.7 %shard_map.83 = (bf16[256,256]{1,0:T(8,128)(2,1)S(1)}, f32[2,8,128]{2,1,0:T(8,128)S(1)}) custom-call(s32[1,2]{1,0:T(1,128)S(1)} %copy-done.3, f32[3]{0:T(128)S(1)} %copy-done.4, f32[2]{0:T(128)S(1)} %copy-done.5, s32[3,3]{1,0:T(4,128)S(1)} %copy-done.2, bf16[256,256]{1,0:T(8,128)(2,1)S(1)} %copy-done.1, bf16[4,2,2,32,256]{4,3,2,1,0:T(8,128)(2,1)S(1)} %get-tuple-element.25._.keep), custom_call_target="tpu_custom_call" | custom-call | bytes 524288 | tf_op jit(solution)/shard_map/pallas_call | solution.py:24
  15.8 4.1 %collective-permute-done.6.refs_4_ = bf16[2,2,32,256]{3,2,1,0:T(8,128)(2,1)S(1)} collective-permute-done((bf16[2,2,32,256]{3,2,1,0:T(8,128)(2,1)S(1)}, bf16[2,2,32,256]{3,2,1,0:T(8,128)(2,1)S(1)}, u32[]{:S(2)}, u32[]{:S(2)}) %collective-permute-start.6) | collective-permute-done | bytes 65568 | tf_op jit(solution)/shard_map/ppermute | solution.py:243
  20.0 0.5 %shard_map.86 = (bf16[2,2,32,256]{3,2,1,0:T(8,128)(2,1)S(1)}, bf16[2,2,32,256]{3,2,1,0:T(8,128)(2,1)S(1)}, bf16[4,1,2,32,256]{4,3,2,1,0:T(8,128)(2,1)S(1)}, bf16[4,1,2,32,256]{4,3,2,1,0:T(8,128)(2,1)S(1)}) custom-call(f32[2,8,128]{2,1,0:T(8,128)S(1)} %get-tuple-element.27._.weights, bf16[4,2,2,32,256]{4,3,2,1,0:T(8,128)(2,1)S(1)} %get-tuple-element.25._.keep, ...), custom_call_target="tpu_custom_call" | custom-call | flops 2359296 | bytes 524288 | tf_op jit(solution)/shard_map/pallas_call | solution.py:24
  20.5 1.5 %collective-permute-start.10 = (bf16[2,2,32,256]{3,2,1,0:T(8,128)(2,1)S(1)}, bf16[2,2,32,256]{3,2,1,0:T(8,128)(2,1)S(1)}, u32[]{:S(2)}, u32[]{:S(2)}) collective-permute-start(bf16[2,2,32,256]{3,2,1,0:T(8,128)(2,1)S(1)} %get-tuple-element.38), channel_id=1, source_target_pairs={{0,2},{1,17},{2,0},{3,19},{8,10},{9,25},{10,8},{11,27},{16,18},{17... | collective-permute-start | bytes 196616 | tf_op jit(solution)/shard_map/ppermute | solution.py:243
  22.0 1.6 %collective-permute-start.11 = (bf16[2,2,32,256]{3,2,1,0:T(8,128)(2,1)S(1)}, bf16[2,2,32,256]{3,2,1,0:T(8,128)(2,1)S(1)}, u32[]{:S(2)}, u32[]{:S(2)}) collective-permute-start(bf16[2,2,32,256]{3,2,1,0:T(8,128)(2,1)S(1)} %get-tuple-element.39), channel_id=1, source_target_pairs={{0,10},{1,3},{2,8},{3,1},{8,2},{9,11},{10,0},{11,9},{16,26},{17,19... | collective-permute-start | bytes 196616 | tf_op jit(solution)/shard_map/ppermute | solution.py:243
  23.6 2.2 %collective-permute-start.12 = (bf16[2,2,32,256]{3,2,1,0:T(8,128)(2,1)S(1)}, bf16[2,2,32,256]{3,2,1,0:T(8,128)(2,1)S(1)}, u32[]{:S(2)}, u32[]{:S(2)}) collective-permute-start(bf16[2,2,32,256]{3,2,1,0:T(8,128)(2,1)S(1)} %get-tuple-element.41), channel_id=1, source_target_pairs={{0,26},{1,25},{2,24},{3,27},{8,18},{9,17},{10,16},{11,19},{16,10},... | collective-permute-start | bytes 196616 | tf_op jit(solution)/shard_map/ppermute | solution.py:243
  25.9 1.5 %collective-permute-start.15 = (bf16[2,2,32,256]{3,2,1,0:T(8,128)(2,1)S(1)}, bf16[2,2,32,256]{3,2,1,0:T(8,128)(2,1)S(1)}, u32[]{:S(2)}, u32[]{:S(2)}) collective-permute-start(bf16[2,2,32,256]{3,2,1,0:T(8,128)(2,1)S(1)} %get-tuple-element.42), channel_id=1, source_target_pairs={{0,16},{1,9},{2,18},{3,11},{8,24},{9,1},{10,26},{11,3},{16,0},{17,... | collective-permute-start | bytes 196616 | tf_op jit(solution)/shard_map/ppermute | solution.py:243
  27.4 1.8 %collective-permute-start.16 = (bf16[2,2,32,256]{3,2,1,0:T(8,128)(2,1)S(1)}, bf16[2,2,32,256]{3,2,1,0:T(8,128)(2,1)S(1)}, u32[]{:S(2)}, u32[]{:S(2)}) collective-permute-start(bf16[2,2,32,256]{3,2,1,0:T(8,128)(2,1)S(1)} %get-tuple-element.43), channel_id=1, source_target_pairs={{0,18},{1,11},{2,16},{3,9},{8,26},{9,3},{10,24},{11,1},{16,2},{17,... | collective-permute-start | bytes 196616 | tf_op jit(solution)/shard_map/ppermute | solution.py:243
  29.2 1.3 %collective-permute-start.17 = (bf16[2,2,32,256]{3,2,1,0:T(8,128)(2,1)S(1)}, bf16[2,2,32,256]{3,2,1,0:T(8,128)(2,1)S(1)}, u32[]{:S(2)}, u32[]{:S(2)}) collective-permute-start(bf16[2,2,32,256]{3,2,1,0:T(8,128)(2,1)S(1)} %get-tuple-element.44), channel_id=1, source_target_pairs={{0,24},{1,27},{2,26},{3,25},{8,16},{9,19},{10,18},{11,17},{16,8},{... | collective-permute-start | bytes 196616 | tf_op jit(solution)/shard_map/ppermute | solution.py:243
  30.5 1.4 %collective-permute-start.14 = (bf16[2,2,32,256]{3,2,1,0:T(8,128)(2,1)S(1)}, bf16[2,2,32,256]{3,2,1,0:T(8,128)(2,1)S(1)}, u32[]{:S(2)}, u32[]{:S(2)}) collective-permute-start(bf16[2,2,32,256]{3,2,1,0:T(8,128)(2,1)S(1)} %get-tuple-element.40.refs_2_), channel_id=1, source_target_pairs={{0,8},{1,19},{2,10},{3,17},{8,0},{9,27},{10,2},{11,25},{16,24},{17... | collective-permute-start | bytes 196616 | tf_op jit(solution)/shard_map/ppermute | solution.py:243
  31.9 1.6 %collective-permute-done.15.refs_4_ = bf16[2,2,32,256]{3,2,1,0:T(8,128)(2,1)S(1)} collective-permute-done((bf16[2,2,32,256]{3,2,1,0:T(8,128)(2,1)S(1)}, bf16[2,2,32,256]{3,2,1,0:T(8,128)(2,1)S(1)}, u32[]{:S(2)}, u32[]{:S(2)}) %collective-permute-start.15) | collective-permute-done | bytes 65568 | tf_op jit(solution)/shard_map/ppermute | solution.py:243
  33.5 0.7 %collective-permute-done.16.refs_5_ = bf16[2,2,32,256]{3,2,1,0:T(8,128)(2,1)S(1)} collective-permute-done((bf16[2,2,32,256]{3,2,1,0:T(8,128)(2,1)S(1)}, bf16[2,2,32,256]{3,2,1,0:T(8,128)(2,1)S(1)}, u32[]{:S(2)}, u32[]{:S(2)}) %collective-permute-start.16) | collective-permute-done | bytes 65568 | tf_op jit(solution)/shard_map/ppermute | solution.py:243
  34.2 0.2 collective-permute-done.17.refs_6_
  34.4 0.4 %collective-permute-done.14.refs_2_ = bf16[2,2,32,256]{3,2,1,0:T(8,128)(2,1)S(1)} collective-permute-done((bf16[2,2,32,256]{3,2,1,0:T(8,128)(2,1)S(1)}, bf16[2,2,32,256]{3,2,1,0:T(8,128)(2,1)S(1)}, u32[]{:S(2)}, u32[]{:S(2)}) %collective-permute-start.14) | collective-permute-done | bytes 65568 | tf_op jit(solution)/shard_map/ppermute | solution.py:243
  34.8 1.2 %shard_map.89 = bf16[2,1,256,256]{3,2,1,0:T(8,128)(2,1)} custom-call(bf16[256,256]{1,0:T(8,128)(2,1)S(1)} %copy-done, bf16[256,256]{1,0:T(8,128)(2,1)S(1)} %get-tuple-element.26.coupling, f32[2,8,128]{2,1,0:T(8,128)S(1)} %get-tuple-element.27._.weights, bf16[4,1,2,32,256]{4,3,2,1,0:T(8,128)(2,1)S(1)} %get-tuple-element.36.keep, ...), custom_call_target="tpu_custom_call" | custom-call | flops 268435456 | bytes 524288 | tf_op jit(solution)/shard_map/pallas_call | solution.py:24
  (32 shorter events, 0.3 us)
Async XLA Ops:
  1.2 5.5 %collective-permute-start = (bf16[4,2,2,32,256]{4,3,2,1,0:T(8,128)(2,1)S(1)}, bf16[4,2,2,32,256]{4,3,2,1,0:T(8,128)(2,1)S(1)}, u32[]{:S(2)}, u32[]{:S(2)}) collective-permute-start(bf16[4,2,2,32,256]{4,3,2,1,0:T(8,128)(2,1)S(1)} %get-tuple-element.28), channel_id=1, source_target_pairs={{0,4},{4,0},{1,5},{5,1},{2,6},{6,2},{3,7},{7,3},{8,12},{12,8},{9,1... | collective-permute-start | bytes 786440 | tf_op jit(solution)/shard_map/ppermute | solution.py:226
  1.7 10.3 %collective-permute-start.1 = (bf16[2,2,32,256]{3,2,1,0:T(8,128)(2,1)S(1)}, bf16[2,2,32,256]{3,2,1,0:T(8,128)(2,1)S(1)}, u32[]{:S(2)}, u32[]{:S(2)}) collective-permute-start(bf16[2,2,32,256]{3,2,1,0:T(8,128)(2,1)S(1)} %get-tuple-element.29), channel_id=1, source_target_pairs={{0,2},{1,25},{2,0},{3,27},{8,10},{9,17},{10,8},{11,19},{16,18},{17... | collective-permute-start | bytes 196616 | tf_op jit(solution)/shard_map/ppermute | solution.py:243
  5.4 8.2 %collective-permute-start.2 = (bf16[2,2,32,256]{3,2,1,0:T(8,128)(2,1)S(1)}, bf16[2,2,32,256]{3,2,1,0:T(8,128)(2,1)S(1)}, u32[]{:S(2)}, u32[]{:S(2)}) collective-permute-start(bf16[2,2,32,256]{3,2,1,0:T(8,128)(2,1)S(1)} %get-tuple-element.30), channel_id=1, source_target_pairs={{0,18},{1,17},{2,16},{3,19},{8,26},{9,25},{10,24},{11,27},{16,2},{... | collective-permute-start | bytes 196616 | tf_op jit(solution)/shard_map/ppermute | solution.py:243
  6.7 8.3 %collective-permute-start.3 = (bf16[2,2,32,256]{3,2,1,0:T(8,128)(2,1)S(1)}, bf16[2,2,32,256]{3,2,1,0:T(8,128)(2,1)S(1)}, u32[]{:S(2)}, u32[]{:S(2)}) collective-permute-start(bf16[2,2,32,256]{3,2,1,0:T(8,128)(2,1)S(1)} %get-tuple-element.32), channel_id=1, source_target_pairs={{0,10},{1,3},{2,8},{3,1},{8,2},{9,11},{10,0},{11,9},{16,26},{17,19... | collective-permute-start | bytes 196616 | tf_op jit(solution)/shard_map/ppermute | solution.py:243
  10.3 9.7 %collective-permute-start.6 = (bf16[2,2,32,256]{3,2,1,0:T(8,128)(2,1)S(1)}, bf16[2,2,32,256]{3,2,1,0:T(8,128)(2,1)S(1)}, u32[]{:S(2)}, u32[]{:S(2)}) collective-permute-start(bf16[2,2,32,256]{3,2,1,0:T(8,128)(2,1)S(1)} %get-tuple-element.33), channel_id=1, source_target_pairs={{0,26},{1,9},{2,24},{3,11},{8,18},{9,1},{10,16},{11,3},{16,10},{17... | collective-permute-start | bytes 196616 | tf_op jit(solution)/shard_map/ppermute | solution.py:243
  10.3 9.7 %collective-permute-start.7 = (bf16[2,2,32,256]{3,2,1,0:T(8,128)(2,1)S(1)}, bf16[2,2,32,256]{3,2,1,0:T(8,128)(2,1)S(1)}, u32[]{:S(2)}, u32[]{:S(2)}) collective-permute-start(bf16[2,2,32,256]{3,2,1,0:T(8,128)(2,1)S(1)} %get-tuple-element.34), channel_id=1, source_target_pairs={{0,8},{1,19},{2,10},{3,17},{8,0},{9,27},{10,2},{11,25},{16,24},{17... | collective-permute-start | bytes 196616 | tf_op jit(solution)/shard_map/ppermute | solution.py:243
  12.0 8.0 %collective-permute-start.8 = (bf16[2,2,32,256]{3,2,1,0:T(8,128)(2,1)S(1)}, bf16[2,2,32,256]{3,2,1,0:T(8,128)(2,1)S(1)}, u32[]{:S(2)}, u32[]{:S(2)}) collective-permute-start(bf16[2,2,32,256]{3,2,1,0:T(8,128)(2,1)S(1)} %get-tuple-element.35), channel_id=1, source_target_pairs={{0,16},{1,11},{2,18},{3,9},{8,24},{9,3},{10,26},{11,1},{16,0},{17,... | collective-permute-start | bytes 196616 | tf_op jit(solution)/shard_map/ppermute | solution.py:243
  13.5 1.6 %copy-start.1 = (bf16[256,256]{1,0:T(8,128)(2,1)S(1)}, bf16[256,256]{1,0:T(8,128)(2,1)}, u32[]{:S(2)}) copy-start(bf16[256,256]{1,0:T(8,128)(2,1)} %link.1) | copy-start | bytes 393220
  13.5 1.6 %copy-start.2 = (s32[3,3]{1,0:T(4,128)S(1)}, s32[3,3]{1,0:T(4,128)}, u32[]{:S(2)}) copy-start(s32[3,3]{1,0:T(4,128)} %mask.1) | copy-start | bytes 112
  13.5 1.6 %copy-start.3 = (s32[1,2]{1,0:T(1,128)S(1)}, s32[1,2]{1,0:T(1,128)}, u32[]{:S(2)}) copy-start(s32[1,2]{1,0:T(1,128)} %blocks.1) | copy-start | bytes 28
  13.5 1.6 %copy-start.4 = (f32[3]{0:T(128)S(1)}, f32[3]{0:T(128)}, u32[]{:S(2)}) copy-start(f32[3]{0:T(128)} %onsite_scale.1) | copy-start | bytes 40
  13.6 1.6 %copy-start.5 = (f32[2]{0:T(128)S(1)}, f32[2]{0:T(128)}, u32[]{:S(2)}) copy-start(f32[2]{0:T(128)} %coupling_scale.1) | copy-start | bytes 28
  13.6 6.4 %collective-permute-start.5 = (bf16[2,2,32,256]{3,2,1,0:T(8,128)(2,1)S(1)}, bf16[2,2,32,256]{3,2,1,0:T(8,128)(2,1)S(1)}, u32[]{:S(2)}, u32[]{:S(2)}) collective-permute-start(bf16[2,2,32,256]{3,2,1,0:T(8,128)(2,1)S(1)} %get-tuple-element.31.refs_2_), channel_id=1, source_target_pairs={{0,24},{1,27},{2,26},{3,25},{8,16},{9,19},{10,18},{11,17},{16,8},{... | collective-permute-start | bytes 196616 | tf_op jit(solution)/shard_map/ppermute | solution.py:243
  15.0 5.0 %collective-permute-start.4 = (bf16[2,2,32,256]{3,2,1,0:T(8,128)(2,1)S(1)}, bf16[2,2,32,256]{3,2,1,0:T(8,128)(2,1)S(1)}, u32[]{:S(2)}, u32[]{:S(2)}) collective-permute-start(bf16[2,2,32,256]{3,2,1,0:T(8,128)(2,1)S(1)} %shard_map.85), channel_id=1, source_target_pairs={{0,4},{4,0},{1,5},{5,1},{2,6},{6,2},{3,7},{7,3},{8,12},{12,8},{9,1... | collective-permute-start | bytes 196616 | tf_op jit(solution)/shard_map/ppermute | solution.py:226
  20.5 3.1 %collective-permute-start.9 = (bf16[4,1,2,32,256]{4,3,2,1,0:T(8,128)(2,1)S(1)}, bf16[4,1,2,32,256]{4,3,2,1,0:T(8,128)(2,1)S(1)}, u32[]{:S(2)}, u32[]{:S(2)}) collective-permute-start(bf16[4,1,2,32,256]{4,3,2,1,0:T(8,128)(2,1)S(1)} %get-tuple-element.37), channel_id=1, source_target_pairs={{0,4},{4,0},{1,5},{5,1},{2,6},{6,2},{3,7},{7,3},{8,12},{12,8},{9,1... | collective-permute-start | bytes 393224 | tf_op jit(solution)/shard_map/ppermute | solution.py:226
  20.5 8.6 %collective-permute-start.10 = (bf16[2,2,32,256]{3,2,1,0:T(8,128)(2,1)S(1)}, bf16[2,2,32,256]{3,2,1,0:T(8,128)(2,1)S(1)}, u32[]{:S(2)}, u32[]{:S(2)}) collective-permute-start(bf16[2,2,32,256]{3,2,1,0:T(8,128)(2,1)S(1)} %get-tuple-element.38), channel_id=1, source_target_pairs={{0,2},{1,17},{2,0},{3,19},{8,10},{9,25},{10,8},{11,27},{16,18},{17... | collective-permute-start | bytes 196616 | tf_op jit(solution)/shard_map/ppermute | solution.py:243
  22.0 8.5 %collective-permute-start.11 = (bf16[2,2,32,256]{3,2,1,0:T(8,128)(2,1)S(1)}, bf16[2,2,32,256]{3,2,1,0:T(8,128)(2,1)S(1)}, u32[]{:S(2)}, u32[]{:S(2)}) collective-permute-start(bf16[2,2,32,256]{3,2,1,0:T(8,128)(2,1)S(1)} %get-tuple-element.39), channel_id=1, source_target_pairs={{0,10},{1,3},{2,8},{3,1},{8,2},{9,11},{10,0},{11,9},{16,26},{17,19... | collective-permute-start | bytes 196616 | tf_op jit(solution)/shard_map/ppermute | solution.py:243
  23.6 8.2 %collective-permute-start.12 = (bf16[2,2,32,256]{3,2,1,0:T(8,128)(2,1)S(1)}, bf16[2,2,32,256]{3,2,1,0:T(8,128)(2,1)S(1)}, u32[]{:S(2)}, u32[]{:S(2)}) collective-permute-start(bf16[2,2,32,256]{3,2,1,0:T(8,128)(2,1)S(1)} %get-tuple-element.41), channel_id=1, source_target_pairs={{0,26},{1,25},{2,24},{3,27},{8,18},{9,17},{10,16},{11,19},{16,10},... | collective-permute-start | bytes 196616 | tf_op jit(solution)/shard_map/ppermute | solution.py:243
  25.9 7.6 %collective-permute-start.15 = (bf16[2,2,32,256]{3,2,1,0:T(8,128)(2,1)S(1)}, bf16[2,2,32,256]{3,2,1,0:T(8,128)(2,1)S(1)}, u32[]{:S(2)}, u32[]{:S(2)}) collective-permute-start(bf16[2,2,32,256]{3,2,1,0:T(8,128)(2,1)S(1)} %get-tuple-element.42), channel_id=1, source_target_pairs={{0,16},{1,9},{2,18},{3,11},{8,24},{9,1},{10,26},{11,3},{16,0},{17,... | collective-permute-start | bytes 196616 | tf_op jit(solution)/shard_map/ppermute | solution.py:243
  27.4 6.9 %collective-permute-start.16 = (bf16[2,2,32,256]{3,2,1,0:T(8,128)(2,1)S(1)}, bf16[2,2,32,256]{3,2,1,0:T(8,128)(2,1)S(1)}, u32[]{:S(2)}, u32[]{:S(2)}) collective-permute-start(bf16[2,2,32,256]{3,2,1,0:T(8,128)(2,1)S(1)} %get-tuple-element.43), channel_id=1, source_target_pairs={{0,18},{1,11},{2,16},{3,9},{8,26},{9,3},{10,24},{11,1},{16,2},{17,... | collective-permute-start | bytes 196616 | tf_op jit(solution)/shard_map/ppermute | solution.py:243
  29.2 5.2 %collective-permute-start.17 = (bf16[2,2,32,256]{3,2,1,0:T(8,128)(2,1)S(1)}, bf16[2,2,32,256]{3,2,1,0:T(8,128)(2,1)S(1)}, u32[]{:S(2)}, u32[]{:S(2)}) collective-permute-start(bf16[2,2,32,256]{3,2,1,0:T(8,128)(2,1)S(1)} %get-tuple-element.44), channel_id=1, source_target_pairs={{0,24},{1,27},{2,26},{3,25},{8,16},{9,19},{10,18},{11,17},{16,8},{... | collective-permute-start | bytes 196616 | tf_op jit(solution)/shard_map/ppermute | solution.py:243
  30.5 4.3 %copy-start = (bf16[256,256]{1,0:T(8,128)(2,1)S(1)}, bf16[256,256]{1,0:T(8,128)(2,1)}, u32[]{:S(2)}) copy-start(bf16[256,256]{1,0:T(8,128)(2,1)} %onsite.1) | copy-start | bytes 393220
  30.5 4.3 %collective-permute-start.14 = (bf16[2,2,32,256]{3,2,1,0:T(8,128)(2,1)S(1)}, bf16[2,2,32,256]{3,2,1,0:T(8,128)(2,1)S(1)}, u32[]{:S(2)}, u32[]{:S(2)}) collective-permute-start(bf16[2,2,32,256]{3,2,1,0:T(8,128)(2,1)S(1)} %get-tuple-element.40.refs_2_), channel_id=1, source_target_pairs={{0,8},{1,19},{2,10},{3,17},{8,0},{9,27},{10,2},{11,25},{16,24},{17... | collective-permute-start | bytes 196616 | tf_op jit(solution)/shard_map/ppermute | solution.py:243
  31.9 2.9 %collective-permute-start.13 = (bf16[2,2,32,256]{3,2,1,0:T(8,128)(2,1)S(1)}, bf16[2,2,32,256]{3,2,1,0:T(8,128)(2,1)S(1)}, u32[]{:S(2)}, u32[]{:S(2)}) collective-permute-start(bf16[2,2,32,256]{3,2,1,0:T(8,128)(2,1)S(1)} %shard_map.88), channel_id=1, source_target_pairs={{0,4},{4,0},{1,5},{5,1},{2,6},{6,2},{3,7},{7,3},{8,12},{12,8},{9,1... | collective-permute-start | bytes 196616 | tf_op jit(solution)/shard_map/ppermute | solution.py:226
